TPU v7x, 512 devices: a whole 4x4x16 slice. The times are simulated.
512 devices in a mesh: wide: 64 (over z, y), narrow: 8 (over x, core).
Axes of the slice: x: 4, y: 4, z: 16, core: 2. Of those that a mesh axis runs over, the one named last changes fastest.
Arguments:
- activations: bfloat16 [192, 2, 8192], P('wide', None, 'narrow'), may hold values from -24 to 24
- norm_gain: float32 [8192], P('narrow'), may hold values from 0.1 to 1.9
- w_query: bfloat16 [8192, 8192], P('narrow', 'wide'), may hold values from -0.0625 to 0.0625
- w_keyval: bfloat16 [8192, 512], P('narrow', 'wide'), may hold values from -0.1875 to 0.1875
- w_out: bfloat16 [8192, 8192], P('wide', 'narrow'), may hold values from -0.0625 to 0.0625
- w_gate: bfloat16 [8192, 32768], P('narrow', 'wide'), may hold values from -0.0625 to 0.0625
- w_up: bfloat16 [8192, 32768], P('narrow', 'wide'), may hold values from -0.0625 to 0.0625
- w_down: bfloat16 [32768, 8192], P('wide', 'narrow'), may hold values from -0.03125 to 0.03125
- key_cache: bfloat16 [192, 2048, 256], P('wide', 'narrow'), may hold values from -240 to 240
- value_cache: bfloat16 [192, 2048, 256], P('wide', 'narrow'), may hold values from -6 to 6
- lengths: int32 [192], P('wide'), may hold values from 1 to 2048, as said below
Outputs:
- mixed: bfloat16 [192, 2, 8192], P('wide', None, 'narrow')
Inputs may be any that keep to these rules, and one draw needn't show every extreme that they name: Row r's cache is filled at positions below lengths[r]; in every draw some row is full and some row holds one position.
All inputs are finite; a program needn't handle non-finite values.
Results may differ from a plain program's by a relative error of at most 0.01.
Values may be sent and summed in bfloat16 or wider, within the bound.
No kernel may reach another device: no remote copies, remote signals or barrier semaphores. Data moves between devices by JAX's collectives and lax.ppermute only.
A program may use at most 64 MiB of HBM per device.

v0:
```python
import jax
import jax.numpy as jnp
from jax import lax
from jax.sharding import PartitionSpec as P

D = 8192


eps_norm = 1e-05
masked_score = -1e30


def merged(shard, axis, combine):
    everything = jax.tree.map(lambda part: lax.all_gather(part, axis), shard)
    leading = jax.tree.map(lambda part: part[0], everything)

    def hop(k, so_far):
        return combine(so_far, jax.tree.map(lambda part: part[k], everything))

    return lax.fori_loop(1, lax.axis_size(axis), hop, leading)


def join_parts(earlier, later):
    max_early, sum_early, acc_early = earlier
    max_late, sum_late, acc_late = later
    highest = jnp.maximum(max_early, max_late)
    early_factor = jnp.exp(max_early - highest)
    late_factor = jnp.exp(max_late - highest)
    return (
        highest,
        sum_early * early_factor + sum_late * late_factor,
        acc_early * early_factor[..., None] + acc_late * late_factor[..., None],
    )


def local(
    activations,
    norm_gain,
    w_query,
    w_keyval,
    w_out,
    w_gate,
    w_up,
    w_down,
    key_cache,
    value_cache,
    lengths,
):
    values_f = activations.astype(jnp.float32)
    row_sums, square_sums = lax.psum((values_f.sum(-1), (values_f * values_f).sum(-1)), "narrow")
    centre = row_sums / D
    spread = square_sums / D - centre * centre
    normed = (
        (values_f - centre[..., None]) * lax.rsqrt(spread[..., None] + eps_norm) * norm_gain
    ).astype(jnp.bfloat16)
    width_local = activations.shape[2]
    query_cols = w_query.shape[1]
    pair_cols = w_keyval.shape[1]
    hidden_cols = w_gate.shape[1]
    boundary = query_cols + pair_cols
    shard_rows = lax.all_gather(normed, "wide", axis=0, tiled=True)
    flat_rows = shard_rows.reshape(-1, width_local)
    products = [
        jnp.dot(flat_rows, weight, preferred_element_type=jnp.float32)
        for weight in (w_query, w_keyval, w_gate, w_up)
    ]
    partial_sums = jnp.concatenate(products, axis=1).reshape(
        shard_rows.shape[0], shard_rows.shape[1], -1
    )
    summed = lax.psum(partial_sums, "narrow")
    gate_sum = summed[..., boundary : boundary + hidden_cols]
    up_sum = summed[..., boundary + hidden_cols :]
    query_loc, pair_loc = (
        lax.all_to_all(
            summed[..., :query_cols].astype(jnp.bfloat16),
            "wide",
            split_axis=0,
            concat_axis=2,
            tiled=True,
        ),
        lax.all_to_all(
            summed[..., query_cols:boundary].astype(jnp.bfloat16),
            "wide",
            split_axis=0,
            concat_axis=2,
            tiled=True,
        ),
    )
    hidden = (jax.nn.silu(gate_sum) * up_sum).astype(jnp.bfloat16)
    row_count = key_cache.shape[0]
    new_count = activations.shape[1]
    head_dim = key_cache.shape[2]
    cache_part = key_cache.shape[1]
    queries = query_loc.reshape(row_count, new_count, query_loc.shape[2] // head_dim, head_dim)
    new_keys = pair_loc[..., :head_dim]
    new_values = pair_loc[..., head_dim:]
    factor = head_dim ** (-0.5)
    narrow_index = lax.axis_index("narrow")
    positions = narrow_index * cache_part + jnp.arange(cache_part, dtype=jnp.int32)
    usable = (positions[None, :] < lengths[:, None])[:, None, None, :]
    cache_scores = (
        jnp.einsum("rthd,rpd->rthp", queries, key_cache, preferred_element_type=jnp.float32)
        * factor
    )
    cache_scores = jnp.where(usable, cache_scores, masked_score)
    own_scores = (
        jnp.einsum("rthd,rud->rthu", queries, new_keys, preferred_element_type=jnp.float32) * factor
    )
    causal = (jnp.arange(new_count)[:, None] >= jnp.arange(new_count)[None, :])[None, :, None, :]
    causal = jnp.logical_and(causal, narrow_index == 0)
    own_scores = jnp.where(causal, own_scores, masked_score)
    local_max = jnp.maximum(cache_scores.max(-1), own_scores.max(-1))
    cache_weights = jnp.where(usable, jnp.exp(cache_scores - local_max[..., None]), 0.0)
    own_weights = jnp.where(causal, jnp.exp(own_scores - local_max[..., None]), 0.0)
    weight_sum = cache_weights.sum(-1) + own_weights.sum(-1)
    weighted = jnp.einsum("rthp,rpd->rthd", cache_weights, value_cache.astype(jnp.float32))
    weighted = weighted + jnp.einsum("rthu,rud->rthd", own_weights, new_values.astype(jnp.float32))
    highest, weight_sum, weighted = merged((local_max, weight_sum, weighted), "narrow", join_parts)
    attended = (
        (weighted / weight_sum[..., None]).reshape(row_count, new_count, -1).astype(jnp.bfloat16)
    )
    returned = lax.all_to_all(attended, "wide", split_axis=2, concat_axis=0, tiled=True)
    flat_heads = returned.reshape(-1, returned.shape[2])
    flat_hidden = hidden.reshape(-1, hidden.shape[2])
    summed_out = lax.psum_scatter(
        jnp.dot(flat_heads, w_out, preferred_element_type=jnp.float32)
        + jnp.dot(flat_hidden, w_down, preferred_element_type=jnp.float32),
        "wide",
        scatter_dimension=0,
        tiled=True,
    )
    summed_out = summed_out.reshape(activations.shape)
    return (values_f + summed_out).astype(jnp.bfloat16)


def solution(mesh):
    return jax.shard_map(
        local,
        mesh=mesh,
        in_specs=(
            P("wide", None, "narrow"),
            P("narrow"),
            P("narrow", "wide"),
            P("narrow", "wide"),
            P("wide", "narrow"),
            P("narrow", "wide"),
            P("narrow", "wide"),
            P("wide", "narrow"),
            P("wide", "narrow", None),
            P("wide", "narrow", None),
            P("wide"),
        ),
        out_specs=P("wide", None, "narrow"),
        check_vma=False,
    )
```

profile of v0, /device:TPU:32, one launch (start us, length us, event | category | flops | bytes accessed | tf_op | source)
XLA Modules:
  0.0 582.3 jit_solution(12853958979748908973)
XLA Ops:
  7.5 14.6 %all-reduce.2 = (f32[3,2]{1,0:T(4,128)S(1)}, f32[3,2]{1,0:T(4,128)S(1)}) all-reduce(f32[3,2]{1,0:T(4,128)S(1)} %get-tuple-element.185, f32[3,2]{1,0:T(4,128)S(1)} %get-tuple-element.184), channel_id=1, replica_groups=mesh['wide'=64,'narrow'=8] {'narrow'}, use_global_device_ids=true, to_apply=%region_3.0 | all-reduce | flops 12 | bytes 96 | tf_op jit(solution)/shard_map/psum | solution.py:50
  22.9 106.2 %all_gather.17 = bf16[192,2,1024]{2,1,0:T(2,128)(2,1)S(1)} all-gather(bf16[3,2,1024]{2,1,0:T(2,128)(2,1)S(1)} %fusion.16), channel_id=1, replica_groups=mesh['wide'=64,'narrow'=8] {'wide'}, dimensions={0}, use_global_device_ids=true | all-gather | bytes 798720 | tf_op jit(solution)/shard_map/all_gather | solution.py:61
  141.1 74.4 %all-reduce.5.cloned.1.call-done = f32[192,2,1160]{2,0,1:T(8,128)} async-done(((f32[192,2,1160]{2,0,1:T(8,128)}), f32[192,2,1160]{2,0,1:T(8,128)}) %all-reduce.5.cloned.1.call-update) | async-done | bytes 1781776 | tf_op jit(solution)/shard_map/psum | solution.py:70
  217.9 15.7 %all-to-all-start.1 = ((bf16[192,2,8]{2,1,0:T(2,128)(2,1)}), bf16[192,2,8]{2,1,0:T(2,128)(2,1)S(1)}, u32[]{:S(2)}, u32[]{:S(2)}) async-start(bf16[192,2,8]{2,1,0:T(2,128)(2,1)} %copy.63), calls=%async_computation.1 | async-start | bytes 196608 | tf_op jit(solution)/shard_map/all_to_all | solution.py:81
  234.3 14.2 %all-to-all-done.1 = bf16[192,2,8]{2,1,0:T(2,128)(2,1)S(1)} async-done(((bf16[192,2,8]{2,1,0:T(2,128)(2,1)}), bf16[192,2,8]{2,1,0:T(2,128)(2,1)S(1)}, u32[]{:S(2)}, u32[]{:S(2)}) %all-to-all-start.1) | async-done | bytes 6176 | tf_op jit(solution)/shard_map/all_to_all | solution.py:81
  248.5 5.4 all-to-all-start
  254.2 14.8 %all-to-all-done = bf16[192,2,128]{2,1,0:T(2,128)(2,1)S(1)} async-done(((bf16[192,2,128]{2,1,0:T(2,128)(2,1)}), bf16[192,2,128]{2,1,0:T(2,128)(2,1)S(1)}, u32[]{:S(2)}, u32[]{:S(2)}) %all-to-all-start) | async-done | bytes 98336 | tf_op jit(solution)/shard_map/all_to_all | solution.py:74
  270.9 12.7 %all-gather = f32[24,2,32]{2,1,0:T(2,128)S(1)} all-gather(f32[3,2,32]{2,1,0:T(2,128)S(1)} %max.27), channel_id=2, replica_groups=mesh['wide'=64,'narrow'=8] {'narrow'}, dimensions={0}, use_global_device_ids=true | all-gather | bytes 6912 | tf_op jit(solution)/shard_map/all_gather | solution.py:14
  283.9 12.7 %all-gather.1 = f32[24,2,32]{2,1,0:T(2,128)S(1)} all-gather(f32[3,2,32]{2,1,0:T(2,128)S(1)} %add.106), channel_id=3, replica_groups=mesh['wide'=64,'narrow'=8] {'narrow'}, dimensions={0}, use_global_device_ids=true | all-gather | bytes 6912 | tf_op jit(solution)/shard_map/all_gather | solution.py:14
  297.5 7.8 %while.19 = (s32[]{:T(128)}, f32[3,2,32]{2,1,0:T(2,128)S(1)}, f32[3,2,32]{2,1,0:T(2,128)S(1)}, f32[3,2,32,256]{3,2,1,0:T(8,128)S(1)}, f32[8,3,2,32]{3,2,1,0:T(2,...) while((s32[]{:T(128)}, f32[3,2,32]{2,1,0:T(2,128)S(1)}, ...), condition=%wide.region_10.11_spmd, body=%wide.region_9.10_spmd.sunk | while | flops 148613 | bytes 597647 | solution.py:20
  305.4 4.9 copy.65
  310.4 7.6 %reshape.120 = bf16[64,2,384]{2,1,0:T(2,128)(2,1)} reshape(bf16[8192,2,3]{2,1,0:T(2,128)(2,1)} %bitcast.79) | data formatting | bytes 196608
  318.0 12.8 %all-to-all-start.2 = ((bf16[64,2,384]{2,1,0:T(2,128)(2,1)}), bf16[64,2,384]{2,1,0:T(2,128)(2,1)S(1)}, u32[]{:S(2)}, u32[]{:S(2)}) async-start(bf16[64,2,384]{2,1,0:T(2,128)(2,1)} %reshape.120), calls=%async_computation.2 | async-start | bytes 196608 | tf_op jit(solution)/shard_map/all_to_all | solution.py:122
  331.8 14.8 %all-to-all-done.2 = bf16[64,2,384]{2,1,0:T(2,128)(2,1)S(1)} async-done(((bf16[64,2,384]{2,1,0:T(2,128)(2,1)}), bf16[64,2,384]{2,1,0:T(2,128)(2,1)S(1)}, u32[]{:S(2)}, u32[]{:S(2)}) %all-to-all-start.2) | async-done | bytes 98336 | tf_op jit(solution)/shard_map/all_to_all | solution.py:122
  346.6 9.8 %reshape.121 = bf16[8192,2,3]{2,1,0:T(2,128)(2,1)} reshape(bf16[64,2,384]{2,1,0:T(2,128)(2,1)S(1)} %all-to-all-done.2) | data formatting | bytes 196608
  356.4 6.1 %copy.75 = bf16[3,2,64,128]{3,2,1,0:T(8,128)(2,1)S(1)} copy(bf16[3,2,64,128]{0,1,3,2:T(2,128)(2,1)} %bitcast.80) | data formatting | bytes 196608 | tf_op jit(solution)/shard_map/all_to_all | solution.py:122
  363.6 147.3 %fusion = f32[8,1024]{1,0:T(8,128)S(1)} fusion(f32[384,1024]{1,0:T(8,128)S(1)} %convolution_add_fusion), kind=kCustom, calls=%all-reduce-scatter | all-reduce-scatter fusion | flops 524289 | bytes 1607680
  510.9 4.3 collective-permute-start.15
  518.8 11.6 %collective-permute-start.13 = (f32[8,1024]{1,0:T(8,128)S(1)}, f32[8,1024]{1,0:T(8,128)S(1)}, u32[]{:S(2)}, u32[]{:S(2)}) collective-permute-start(f32[8,1024]{1,0:T(8,128)S(1)} %fusion), channel_id=1, source_target_pairs={{0,112},{8,120},{16,128},{24,136},{32,144},{40,152},{48,160},{56,1... | collective-permute-start | bytes 98312
  536.8 6.4 %collective-permute-start.8 = (f32[8,1024]{1,0:T(8,128)S(1)}, f32[8,1024]{1,0:T(8,128)S(1)}, u32[]{:S(2)}, u32[]{:S(2)}) collective-permute-start(f32[8,1024]{1,0:T(8,128)S(1)} %fusion), channel_id=1, source_target_pairs={{0,72},{8,80},{16,88},{24,96},{32,104},{40,112},{48,120},{56,128},... | collective-permute-start | bytes 98312
  550.9 4.1 collective-permute-start.4
  556.9 4.3 collective-permute-start.2
  561.3 3.8 collective-permute-start.1
  569.5 3.5 collective-permute-done
  (113 shorter events, 55.4 us)
Async XLA Ops:
  6.5 356.4 %copy-start = (bf16[512,1024]{1,0:T(8,128)(2,1)S(1)}, bf16[512,1024]{1,0:T(8,128)(2,1)}, u32[]{:S(2)}) copy-start(bf16[512,1024]{1,0:T(8,128)(2,1)} %param.20) | copy-start | bytes 3145732
  6.5 208.9 %all-reduce.5.cloned.1.call-start = ((), (), s32[]{:S(2)}) async-start(), calls=%async_computation.3 | async-start | bytes 3932160 | tf_op jit(solution)/shard_map/psum | solution.py:70
  141.1 128.1 %copy-start.5 = (bf16[3,256,256]{2,1,0:T(8,128)(2,1)S(1)}, bf16[3,256,256]{2,1,0:T(8,128)(2,1)}, u32[]{:S(2)}) copy-start(bf16[3,256,256]{2,1,0:T(8,128)(2,1)} %param.21) | copy-start | bytes 1179652
  217.9 30.6 %all-to-all-start.1 = ((bf16[192,2,8]{2,1,0:T(2,128)(2,1)}), bf16[192,2,8]{2,1,0:T(2,128)(2,1)S(1)}, u32[]{:S(2)}, u32[]{:S(2)}) async-start(bf16[192,2,8]{2,1,0:T(2,128)(2,1)} %copy.63), calls=%async_computation.1 | async-start | bytes 196608 | tf_op jit(solution)/shard_map/all_to_all | solution.py:81
  248.5 20.5 %all-to-all-start = ((bf16[192,2,128]{2,1,0:T(2,128)(2,1)}), bf16[192,2,128]{2,1,0:T(2,128)(2,1)S(1)}, u32[]{:S(2)}, u32[]{:S(2)}) async-start(bf16[192,2,128]{2,1,0:T(2,128)(2,1)} %copy.61), calls=%async_computation | async-start | bytes 196608 | tf_op jit(solution)/shard_map/all_to_all | solution.py:74
  253.9 42.7 %all-gather.5.cloned.1.call-start = ((), (), s32[]{:S(2)}) async-start(), calls=%async_computation.4 | async-start | bytes 1769472 | tf_op jit(solution)/shard_map/all_gather | solution.py:14
  318.0 28.6 %all-to-all-start.2 = ((bf16[64,2,384]{2,1,0:T(2,128)(2,1)}), bf16[64,2,384]{2,1,0:T(2,128)(2,1)S(1)}, u32[]{:S(2)}, u32[]{:S(2)}) async-start(bf16[64,2,384]{2,1,0:T(2,128)(2,1)} %reshape.120), calls=%async_computation.2 | async-start | bytes 196608 | tf_op jit(solution)/shard_map/all_to_all | solution.py:122
  363.6 211.2 %copy-start.8 = (bf16[3,2,1024]{2,1,0:T(2,128)(2,1)S(1)}, bf16[3,2,1024]{2,1,0:T(2,128)(2,1)}, u32[]{:S(2)}) copy-start(bf16[3,2,1024]{2,1,0:T(2,128)(2,1)} %param.13) | copy-start | bytes 36868
  510.9 22.4 %collective-permute-start.15 = (f32[6,1024]{1,0:T(8,128)S(1)}, f32[6,1024]{1,0:T(8,128)S(1)}, u32[]{:S(2)}, u32[]{:S(2)}) collective-permute-start(f32[6,1024]{1,0:T(8,128)S(1)} %slice.50), channel_id=1, source_target_pairs={{0,128},{8,136},{16,144},{24,152},{32,160},{40,168},{48,176},{56,1... | collective-permute-start | bytes 73736
  515.3 20.2 %collective-permute-start.14 = (f32[8,1024]{1,0:T(8,128)S(1)}, f32[8,1024]{1,0:T(8,128)S(1)}, u32[]{:S(2)}, u32[]{:S(2)}) collective-permute-start(f32[8,1024]{1,0:T(8,128)S(1)} %fusion), channel_id=1, source_target_pairs={{0,120},{8,128},{16,136},{24,144},{32,152},{40,160},{48,168},{56,1... | collective-permute-start | bytes 98312
  518.8 18.0 %collective-permute-start.13 = (f32[8,1024]{1,0:T(8,128)S(1)}, f32[8,1024]{1,0:T(8,128)S(1)}, u32[]{:S(2)}, u32[]{:S(2)}) collective-permute-start(f32[8,1024]{1,0:T(8,128)S(1)} %fusion), channel_id=1, source_target_pairs={{0,112},{8,120},{16,128},{24,136},{32,144},{40,152},{48,160},{56,1... | collective-permute-start | bytes 98312
  530.4 12.9 %collective-permute-start.12 = (f32[8,1024]{1,0:T(8,128)S(1)}, f32[8,1024]{1,0:T(8,128)S(1)}, u32[]{:S(2)}, u32[]{:S(2)}) collective-permute-start(f32[8,1024]{1,0:T(8,128)S(1)} %fusion), channel_id=1, source_target_pairs={{0,104},{8,112},{16,120},{24,128},{32,136},{40,144},{48,152},{56,1... | collective-permute-start | bytes 98312
  532.1 12.9 %collective-permute-start.11 = (f32[8,1024]{1,0:T(8,128)S(1)}, f32[8,1024]{1,0:T(8,128)S(1)}, u32[]{:S(2)}, u32[]{:S(2)}) collective-permute-start(f32[8,1024]{1,0:T(8,128)S(1)} %fusion), channel_id=1, source_target_pairs={{0,96},{8,104},{16,112},{24,120},{32,128},{40,136},{48,144},{56,15... | collective-permute-start | bytes 98312
  533.4 15.0 %collective-permute-start.10 = (f32[8,1024]{1,0:T(8,128)S(1)}, f32[8,1024]{1,0:T(8,128)S(1)}, u32[]{:S(2)}, u32[]{:S(2)}) collective-permute-start(f32[8,1024]{1,0:T(8,128)S(1)} %fusion), channel_id=1, source_target_pairs={{0,88},{8,96},{16,104},{24,112},{32,120},{40,128},{48,136},{56,144... | collective-permute-start | bytes 98312
  535.5 15.3 %collective-permute-start.9 = (f32[8,1024]{1,0:T(8,128)S(1)}, f32[8,1024]{1,0:T(8,128)S(1)}, u32[]{:S(2)}, u32[]{:S(2)}) collective-permute-start(f32[8,1024]{1,0:T(8,128)S(1)} %fusion), channel_id=1, source_target_pairs={{0,80},{8,88},{16,96},{24,104},{32,112},{40,120},{48,128},{56,136}... | collective-permute-start | bytes 98312
  536.8 18.2 %collective-permute-start.8 = (f32[8,1024]{1,0:T(8,128)S(1)}, f32[8,1024]{1,0:T(8,128)S(1)}, u32[]{:S(2)}, u32[]{:S(2)}) collective-permute-start(f32[8,1024]{1,0:T(8,128)S(1)} %fusion), channel_id=1, source_target_pairs={{0,72},{8,80},{16,88},{24,96},{32,104},{40,112},{48,120},{56,128},... | collective-permute-start | bytes 98312
  543.3 13.7 %collective-permute-start.7 = (f32[8,1024]{1,0:T(8,128)S(1)}, f32[8,1024]{1,0:T(8,128)S(1)}, u32[]{:S(2)}, u32[]{:S(2)}) collective-permute-start(f32[8,1024]{1,0:T(8,128)S(1)} %fusion), channel_id=1, source_target_pairs={{0,64},{8,72},{16,80},{24,88},{32,96},{40,104},{48,112},{56,120},{... | collective-permute-start | bytes 98312
  544.9 16.3 %collective-permute-start.6 = (f32[8,1024]{1,0:T(8,128)S(1)}, f32[8,1024]{1,0:T(8,128)S(1)}, u32[]{:S(2)}, u32[]{:S(2)}) collective-permute-start(f32[8,1024]{1,0:T(8,128)S(1)} %fusion), channel_id=1, source_target_pairs={{0,56},{8,64},{16,72},{24,80},{32,88},{40,96},{48,104},{56,112},{6... | collective-permute-start | bytes 98312
  548.4 16.7 %collective-permute-start.5 = (f32[8,1024]{1,0:T(8,128)S(1)}, f32[8,1024]{1,0:T(8,128)S(1)}, u32[]{:S(2)}, u32[]{:S(2)}) collective-permute-start(f32[8,1024]{1,0:T(8,128)S(1)} %fusion), channel_id=1, source_target_pairs={{0,48},{8,56},{16,64},{24,72},{32,80},{40,88},{48,96},{56,104},{64... | collective-permute-start | bytes 98312
  550.9 18.1 %collective-permute-start.4 = (f32[8,1024]{1,0:T(8,128)S(1)}, f32[8,1024]{1,0:T(8,128)S(1)}, u32[]{:S(2)}, u32[]{:S(2)}) collective-permute-start(f32[8,1024]{1,0:T(8,128)S(1)} %fusion), channel_id=1, source_target_pairs={{0,40},{8,48},{16,56},{24,64},{32,72},{40,80},{48,88},{56,96},{64,... | collective-permute-start | bytes 98312
  555.0 14.0 %collective-permute-start.3 = (f32[8,1024]{1,0:T(8,128)S(1)}, f32[8,1024]{1,0:T(8,128)S(1)}, u32[]{:S(2)}, u32[]{:S(2)}) collective-permute-start(f32[8,1024]{1,0:T(8,128)S(1)} %fusion), channel_id=1, source_target_pairs={{0,32},{8,40},{16,48},{24,56},{32,64},{40,72},{48,80},{56,88},{64,... | collective-permute-start | bytes 98312
  556.9 12.0 %collective-permute-start.2 = (f32[8,1024]{1,0:T(8,128)S(1)}, f32[8,1024]{1,0:T(8,128)S(1)}, u32[]{:S(2)}, u32[]{:S(2)}) collective-permute-start(f32[8,1024]{1,0:T(8,128)S(1)} %fusion), channel_id=1, source_target_pairs={{0,24},{8,32},{16,40},{24,48},{32,56},{40,64},{48,72},{56,80},{64,... | collective-permute-start | bytes 98312
  561.3 8.2 %collective-permute-start.1 = (f32[8,1024]{1,0:T(8,128)S(1)}, f32[8,1024]{1,0:T(8,128)S(1)}, u32[]{:S(2)}, u32[]{:S(2)}) collective-permute-start(f32[8,1024]{1,0:T(8,128)S(1)} %fusion), channel_id=1, source_target_pairs={{0,16},{8,24},{16,32},{24,40},{32,48},{40,56},{48,64},{56,72},{64,... | collective-permute-start | bytes 98312
  565.1 7.9 %collective-permute-start = (f32[8,1024]{1,0:T(8,128)S(1)}, f32[8,1024]{1,0:T(8,128)S(1)}, u32[]{:S(2)}, u32[]{:S(2)}) collective-permute-start(f32[8,1024]{1,0:T(8,128)S(1)} %fusion), channel_id=1, source_target_pairs={{0,8},{8,16},{16,24},{24,32},{32,40},{40,48},{48,56},{56,64},{64,7... | collective-permute-start | bytes 98312
  (8 other events, 441.7 us)
Sparse Core Ops, SparseCore 0:
  141.2 74.2 all-reduce.4
  271.0 22.8 all-gather.4
where the time goes:
time: 584 us; the launch traced here: 582 us
  blocking collectives  294 us (50%)
  waiting for transfers between devices  122 us (21%)
  starting transfers between devices  89.7 us (15%)
  local copies, waits for them, and re-layouts  43 us (7%)
  between operations  14.7 us (3%)
  other arithmetic  12.5 us (2%)
  matrix products  6.38 us (1%)
    unnamed x1, blocking collectives  147 us
    all_gather x1, blocking collectives, local(): shard_rows = lax.all_gather(normed, 'wide', axis=0, tiled=True)  106 us
    psum x1, waiting for transfers between devices, local(): summed = lax.psum(partial_sums, 'narrow')  74.4 us
    unnamed x16, starting transfers between devices  55.8 us
    all_gather x2, blocking collectives, merged(): everything = jax.tree.map(lambda part: lax.all_gather(part, axis), shard)  25.4 us
    unnamed x28, local copies, waits for them, and re-layouts  20.9 us
    all_to_all x1, starting transfers between devices, local(): lax.all_to_all(summed[..., query_cols:boundary].astype(jnp.bfloat16), 'wi...  15.7 us
    all_to_all x1, waiting for transfers between devices, local(): lax.all_to_all(attended, 'wide', split_axis=2, concat_axis=0, tiled=True)  14.8 us
  transfers between devices with their start and end apart: 21, of which 6 were waited for; matrix products, arithmetic and copies ran while one was open for 1% of the time, Pallas kernels for 0%

commit v1 on v0

v1 whole, which is shorter than its diff:
```python
import jax
import jax.numpy as jnp
import numpy as np
from jax import lax
from jax.sharding import Mesh
from jax.sharding import PartitionSpec as P

D = 8192
eps_norm = 1e-05
masked_score = -1e30
bf16 = jnp.bfloat16
f32 = jnp.float32
WIDE = ("z", "y")
NARROW = ("x", "core")


def three_parts(value):
    first = lax.reduce_precision(value, 8, 7)
    rest = value - first
    second = lax.reduce_precision(rest, 8, 7)
    return first, second, lax.reduce_precision(rest - second, 8, 7)


def local(
    activations,
    norm_gain,
    w_query,
    w_keyval,
    w_out,
    w_gate,
    w_up,
    w_down,
    key_cache,
    value_cache,
    lengths,
):
    zs, ys, ns = lax.axis_size("z"), lax.axis_size("y"), lax.axis_size(NARROW)
    ws = zs * ys
    rows, new, width = activations.shape
    toks = rows * new
    every = ws * toks
    head_dim = key_cache.shape[2]
    kv_cols = w_keyval.shape[1]
    lanes = w_query.shape[1]
    heads = ws * lanes // head_dim
    halves = head_dim // lanes
    ffn = w_gate.shape[1]

    values = activations.reshape(toks, width).astype(f32)
    sums = jnp.concatenate([values.sum(-1), (values * values).sum(-1)])
    sums = jnp.pad(sums, (0, 128 - 2 * toks))[None]
    sums = lax.all_gather(sums, NARROW, axis=0, tiled=True).sum(0)
    centre = sums[:toks, None] / D
    spread = sums[toks : 2 * toks, None] / D - centre * centre
    normed = ((values - centre) * lax.rsqrt(spread + eps_norm) * norm_gain).astype(bf16)

    copies = jnp.broadcast_to(jnp.pad(normed, ((0, 8 - toks), (0, 0)))[None], (zs, 8, width))
    column = lax.all_to_all(copies, "z", 0, 0, tiled=True)
    column = column[:, :toks].reshape(zs * toks, width)
    flat = lax.all_gather(column, "y", axis=0, tiled=True)

    gate_up = jnp.dot(flat, jnp.concatenate([w_gate, w_up], axis=1), preferred_element_type=f32)

    query_part = jnp.dot(flat, w_query, preferred_element_type=f32).astype(bf16)
    lane = np.arange(lanes)
    spreader = jnp.asarray((lane[None, :] % kv_cols) == np.arange(kv_cols)[:, None], bf16)
    w_pair = jnp.dot(w_keyval, spreader, preferred_element_type=f32).astype(bf16)
    pair_part = jnp.dot(flat, w_pair, preferred_element_type=f32).astype(bf16)
    keep = (lane[None, :] // kv_cols) == (np.arange(every)[:, None] % toks)
    pair_part = jnp.where(keep, pair_part, jnp.zeros_like(pair_part))
    collect = jnp.asarray(np.arange(ws)[:, None] == (np.arange(every)[None, :] // toks), bf16)
    pair_rows = jnp.dot(collect, pair_part, preferred_element_type=f32).astype(bf16)
    parts = jnp.concatenate([query_part, pair_rows], axis=0)
    parts = lax.all_gather(parts, NARROW, axis=0, tiled=False)
    summed = parts.astype(f32).sum(0).astype(bf16)

    gate_up = lax.psum_scatter(gate_up, NARROW, scatter_dimension=0, tiled=True)

    block = jnp.concatenate(
        [
            summed[:every].reshape(ws, toks, lanes),
            summed[every:][:, None, :],
            jnp.zeros((ws, 8 - toks - 1, lanes), bf16),
        ],
        axis=1,
    )
    block = lax.all_to_all(block.reshape(ys, zs * 8, lanes), "y", 0, 0, tiled=True)
    block = block.reshape(ys, zs, 8, lanes).transpose(1, 0, 2, 3).reshape(zs, ys * 8, lanes)
    block = lax.all_to_all(block, "z", 0, 0, tiled=True)
    block = block.reshape(ws, 8, lanes)

    queries = (
        block[:, :toks]
        .reshape(heads, halves, rows, new, lanes)
        .transpose(2, 3, 0, 1, 4)
        .reshape(rows, new * heads, head_dim)
    )
    pairs = (
        block[:, toks, : toks * kv_cols]
        .reshape(ws, toks, kv_cols)
        .transpose(1, 0, 2)
        .reshape(rows, new, 2 * head_dim)
    )
    new_keys, new_values = pairs[..., :head_dim], pairs[..., head_dim:]
    narrow_index = lax.axis_index(NARROW)
    cache_part = key_cache.shape[1]
    factor = head_dim ** (-0.5)
    positions = narrow_index * cache_part + jnp.arange(cache_part, dtype=jnp.int32)
    usable = (positions[None, :] < lengths[:, None])[:, None, :]
    scores = jnp.einsum("rqd,rpd->rqp", queries, key_cache, preferred_element_type=f32) * factor
    scores = jnp.where(usable, scores, masked_score)
    own = jnp.einsum("rqd,rud->rqu", queries, new_keys, preferred_element_type=f32) * factor
    token_of = np.arange(new * heads) // heads
    causal = (token_of[:, None] >= np.arange(new)[None, :])[None]
    causal = jnp.logical_and(causal, narrow_index == 0)
    own = jnp.where(causal, own, masked_score)
    top = jnp.maximum(scores.max(-1), own.max(-1))
    weights = jnp.where(usable, jnp.exp(scores - top[..., None]), 0.0)
    own_weights = jnp.where(causal, jnp.exp(own - top[..., None]), 0.0)
    total = weights.sum(-1) + own_weights.sum(-1)
    weighted = jnp.einsum("rqp,rpd->rqd", weights.astype(bf16), value_cache, preferred_element_type=f32)
    weighted = weighted + jnp.einsum("rqu,rud->rqd", own_weights, new_values.astype(f32))

    sent = (
        weighted.astype(bf16)
        .reshape(rows, new, heads, halves, lanes)
        .transpose(2, 3, 0, 1, 4)
        .reshape(ws, toks, lanes)
    )
    marks = jnp.stack(three_parts(top) + three_parts(total))
    marks = marks.reshape(6, toks, heads).transpose(2, 0, 1)
    marks = jnp.pad(marks, ((0, 0), (0, 0), (0, 8 - toks))).reshape(heads, 48)
    marks = jnp.pad(marks, ((0, 0), (0, lanes - 48))).astype(bf16)
    marks = jnp.broadcast_to(marks[:, None], (heads, halves, lanes)).reshape(ws, 1, lanes)
    block = jnp.concatenate([sent, marks, jnp.zeros((ws, 8 - toks - 1, lanes), bf16)], axis=1)
    block = lax.all_to_all(block.reshape(zs, ys * 8, lanes), "z", 0, 0, tiled=True)
    block = block.reshape(zs, ys, 8, lanes).transpose(1, 0, 2, 3).reshape(ys, zs * 8, lanes)
    block = lax.all_to_all(block, "y", 0, 0, tiled=True).reshape(ws, 8, lanes)
    parts = jnp.concatenate([block[:, :toks].reshape(every, lanes), block[:, toks]], axis=0)
    parts = lax.all_gather(parts, NARROW, axis=0, tiled=False)
    weighted = parts[:, :every].astype(f32).reshape(ns, ws, toks, lanes)
    marks = parts[:, every:, :48].astype(f32).reshape(ns, ws, 6, 8)[..., :toks]
    top = marks[:, :, 0] + marks[:, :, 1] + marks[:, :, 2]
    total = marks[:, :, 3] + marks[:, :, 4] + marks[:, :, 5]
    scale = jnp.exp(top - top.max(0))
    scale = scale / (total * scale).sum(0)
    attended = (weighted * scale[..., None]).sum(0).reshape(every, lanes).astype(bf16)

    hidden = (jax.nn.silu(gate_up[:, :ffn]) * gate_up[:, ffn:]).astype(bf16)
    hidden = lax.all_gather(hidden, NARROW, axis=0, tiled=True)

    mixed = jnp.dot(attended, w_out, preferred_element_type=f32) + jnp.dot(
        hidden, w_down, preferred_element_type=f32
    )
    mixed = lax.all_to_all(mixed.astype(bf16).reshape(ys, zs * toks, width), "y", 0, 0, tiled=True)
    mixed = mixed.astype(f32).sum(0).astype(bf16).reshape(zs, toks, width)
    mixed = jnp.pad(mixed, ((0, 0), (0, 8 - toks), (0, 0)))
    mixed = lax.all_to_all(mixed, "z", 0, 0, tiled=True)[:, :toks]
    return (values + mixed.astype(f32).sum(0)).astype(bf16).reshape(activations.shape)


def solution(mesh):
    names = ("z", "y", "x", "core")
    split = Mesh(mesh.devices.reshape(16, 4, 4, 2), names)
    return jax.shard_map(
        local,
        mesh=split,
        in_specs=(
            P(WIDE, None, NARROW),
            P(NARROW),
            P(NARROW, WIDE),
            P(NARROW, WIDE),
            P(WIDE, NARROW),
            P(NARROW, WIDE),
            P(NARROW, WIDE),
            P(WIDE, NARROW),
            P(WIDE, NARROW, None),
            P(WIDE, NARROW, None),
            P(WIDE),
        ),
        out_specs=P(WIDE, None, NARROW),
        check_vma=False,
    )
```

time: 584 us -> 220 us (0.38)
  the two profiles are of different devices: /device:TPU:32 before, /device:TPU:64 now
where the time goes in v1:
time: 220 us; the launch traced here: 219 us
  blocking collectives  131 us (60%)
  waiting for transfers between devices  32.4 us (15%)
  starting transfers between devices  25.3 us (12%)
  between operations  13.8 us (6%)
  matrix products  6.69 us (3%)
  other arithmetic  5.52 us (3%)
  local copies, waits for them, and re-layouts  4.6 us (2%)
    all_gather x2, blocking collectives, local(): parts = lax.all_gather(parts, NARROW, axis=0, tiled=False)  27.2 us
    all_to_all x1, blocking collectives, local(): mixed = lax.all_to_all(mixed, 'z', 0, 0, tiled=True)[:, :toks]  24.1 us
    all_to_all x1, waiting for transfers between devices, local(): column = lax.all_to_all(copies, 'z', 0, 0, tiled=True)  17.7 us
    all_to_all x1, blocking collectives, local(): lax.all_to_all(block.reshape(zs, ys * 8, lanes), 'z', 0, 0, tiled=True)  16.9 us
    all_to_all x1, blocking collectives, local(): lax.all_to_all(mixed.astype(bf16).reshape(ys, zs * toks, width), 'y', 0,...  15.5 us
    all_gather x1, blocking collectives, local(): flat = lax.all_gather(column, 'y', axis=0, tiled=True)  15 us
    all_to_all x1, starting transfers between devices, local(): column = lax.all_to_all(copies, 'z', 0, 0, tiled=True)  14.9 us
    all_gather x1, blocking collectives, local(): hidden = lax.all_gather(hidden, NARROW, axis=0, tiled=True)  13 us
  transfers between devices with their start and end apart: 4, of which 3 were waited for; matrix products, arithmetic and copies ran while one was open for 4% of the time, Pallas kernels for 0%

profile of v1, /device:TPU:64, one launch (start us, length us, event | category | flops | bytes accessed | tf_op | source)
XLA Modules:
  0.0 218.9 jit_solution(5820226802048403011)
XLA Ops:
  6.5 0.9 convert_reduce_fusion.1
  7.5 0.7 reshape.289
  8.4 10.5 %all-gather.3 = f32[8,1,128]{2,1,0:T(1,128)S(1)} all-gather(f32[1,1,128]{2,1,0:T(1,128)S(1)} %fusion.34), channel_id=2, replica_groups=mesh['z'=16,'y'=4,'x'=4,'core'=2] {'x','core'}, dimensions={0}, use_global_device_ids=true | all-gather | bytes 4608 | tf_op jit(solution)/shard_map/all_gather | solution.py:52
  19.0 0.8 multiply_convert_fusion
  19.8 0.7 broadcast_in_dim.72
  20.5 14.9 %all-to-all-start = ((bf16[16,8,1024]{2,1,0:T(8,128)(2,1)}), bf16[16,8,1024]{2,1,0:T(8,128)(2,1)S(1)}, u32[]{:S(2)}, u32[]{:S(2)}) async-start(bf16[16,8,1024]{2,1,0:T(8,128)(2,1)} %broadcast_in_dim.72), calls=%async_computation | async-start | bytes 524288 | tf_op jit(solution)/shard_map/all_to_all | solution.py:58
  35.5 17.7 %all-to-all-done = bf16[16,8,1024]{2,1,0:T(8,128)(2,1)S(1)} async-done(((bf16[16,8,1024]{2,1,0:T(8,128)(2,1)}), bf16[16,8,1024]{2,1,0:T(8,128)(2,1)S(1)}, u32[]{:S(2)}, u32[]{:S(2)}) %all-to-all-start) | async-done | bytes 262176 | tf_op jit(solution)/shard_map/all_to_all | solution.py:58
  53.3 15.0 %all_gather.22 = bf16[384,1024]{1,0:T(8,128)(2,1)S(1)} all-gather(bf16[96,1024]{1,0:T(8,128)(2,1)S(1)} %reshape.267), channel_id=1, replica_groups=mesh['z'=16,'y'=4,'x'=4,'core'=2] {'y'}, dimensions={0}, use_global_device_ids=true | all-gather | bytes 983040 | tf_op jit(solution)/shard_map/all_gather | solution.py:60
  69.5 13.6 %all-gather.1 = bf16[3584,128]{1,0:T(8,128)(2,1)S(1)} all-gather(bf16[448,128]{1,0:T(8,128)(2,1)S(1)} %pad_maximum_fusion), channel_id=3, replica_groups=mesh['z'=16,'y'=4,'x'=4,'core'=2] {'x','core'}, dimensions={0}, use_global_device_ids=true | all-gather | bytes 1032192 | tf_op jit(solution)/shard_map/all_gather | solution.py:74
  83.3 0.7 maximum_maximum_fusion
  84.1 3.3 %all-to-all-start.1 = ((bf16[4,128,128]{2,1,0:T(8,128)(2,1)}), bf16[4,128,128]{2,1,0:T(8,128)(2,1)S(1)}, u32[]{:S(2)}, u32[]{:S(2)}) async-start(bf16[4,128,128]{2,1,0:T(8,128)(2,1)} %bitcast.4), calls=%async_computation.1 | async-start | bytes 262144 | tf_op jit(solution)/shard_map/all_to_all | solution.py:87
  87.5 5.9 %all-to-all-done.1 = bf16[4,128,128]{2,1,0:T(8,128)(2,1)S(1)} async-done(((bf16[4,128,128]{2,1,0:T(8,128)(2,1)}), bf16[4,128,128]{2,1,0:T(8,128)(2,1)S(1)}, u32[]{:S(2)}, u32[]{:S(2)}) %all-to-all-start.1) | async-done | bytes 131104 | tf_op jit(solution)/shard_map/all_to_all | solution.py:87
  93.4 0.7 copy_bitcast_fusion.1
  94.1 7.0 %all-to-all-start.2 = ((bf16[16,32,128]{2,1,0:T(8,128)(2,1)}), bf16[16,32,128]{2,1,0:T(8,128)(2,1)S(1)}, u32[]{:S(2)}, u32[]{:S(2)}) async-start(bf16[16,32,128]{2,1,0:T(8,128)(2,1)} %copy_bitcast_fusion.1), calls=%async_computation.2 | async-start | bytes 262144 | tf_op jit(solution)/shard_map/all_to_all | solution.py:89
  101.2 3.7 %fusion = f32[384,1024]{1,0:T(8,128)} fusion(bf16[384,1024]{1,0:T(8,128)(2,1)S(1)} %all_gather.22, bf16[1024,512]{1,0:T(8,128)(2,1)} %param.21, bf16[1024,512]{1,0:T(8,128)(2,1)} %param.20), kind=kOutput, calls=%fused_computation | convolution fusion | flops 809500672 | bytes 4456448 | tf_op jit(solution)/shard_map/dot_general | solution.py:62
  104.9 8.7 %all-to-all-done.2 = bf16[16,32,128]{2,1,0:T(8,128)(2,1)S(1)} async-done(((bf16[16,32,128]{2,1,0:T(8,128)(2,1)}), bf16[16,32,128]{2,1,0:T(8,128)(2,1)S(1)}, u32[]{:S(2)}, u32[]{:S(2)}) %all-to-all-start.2) | async-done | bytes 131104 | tf_op jit(solution)/shard_map/all_to_all | solution.py:89
  115.9 16.9 %all_to_all.35 = bf16[16,32,128]{2,1,0:T(8,128)(2,1)S(1)} all-to-all(bf16[16,32,128]{2,1,0:T(8,128)(2,1)S(1)} %bitcast.111), channel_id=1, replica_groups=mesh['z'=16,'y'=4,'x'=4,'core'=2] {'z'}, dimensions={0} | all-to-all | bytes 262144 | tf_op jit(solution)/shard_map/all_to_all | solution.py:136
  132.8 8.5 %all_to_all.36 = bf16[4,128,128]{2,1,0:T(8,128)(2,1)S(1)} all-to-all(bf16[4,128,128]{2,1,0:T(8,128)(2,1)S(1)} %copy_bitcast_fusion), channel_id=1, replica_groups=mesh['z'=16,'y'=4,'x'=4,'core'=2] {'y'}, dimensions={0} | all-to-all | bytes 262144 | tf_op jit(solution)/shard_map/all_to_all | solution.py:138
  141.4 13.6 %all-gather.2 = bf16[3584,128]{1,0:T(8,128)(2,1)S(1)} all-gather(bf16[448,128]{1,0:T(8,128)(2,1)S(1)} %pad_maximum_fusion.1), channel_id=4, replica_groups=mesh['z'=16,'y'=4,'x'=4,'core'=2] {'x','core'}, dimensions={0}, use_global_device_ids=true | all-gather | bytes 1032192 | tf_op jit(solution)/shard_map/all_gather | solution.py:140
  157.0 1.0 fusion.14
  157.9 13.0 %all_gather.27 = bf16[384,512]{1,0:T(8,128)(2,1)S(1)} all-gather(bf16[48,512]{1,0:T(8,128)(2,1)S(1)} %fusion.14), channel_id=1, replica_groups=mesh['z'=16,'y'=4,'x'=4,'core'=2] {'x','core'}, dimensions={0}, use_global_device_ids=true | all-gather | bytes 442368 | tf_op jit(solution)/shard_map/all_gather | solution.py:150
  171.5 15.5 %all_to_all.37 = bf16[4,96,1024]{2,1,0:T(8,128)(2,1)S(1)} all-to-all(bf16[4,96,1024]{2,1,0:T(8,128)(2,1)S(1)} %bitcast.105), channel_id=1, replica_groups=mesh['z'=16,'y'=4,'x'=4,'core'=2] {'y'}, dimensions={0} | all-to-all | bytes 1572864 | tf_op jit(solution)/shard_map/all_to_all | solution.py:155
  187.3 24.1 %all_to_all.38 = bf16[16,8,1024]{2,1,0:T(8,128)(2,1)S(1)} all-to-all(bf16[16,8,1024]{2,1,0:T(8,128)(2,1)S(1)} %pad.26), channel_id=1, replica_groups=mesh['z'=16,'y'=4,'x'=4,'core'=2] {'z'}, dimensions={0} | all-to-all | bytes 524288 | tf_op jit(solution)/shard_map/all_to_all | solution.py:158
  211.4 0.6 add_convert_fusion.1
  (101 shorter events, 7.1 us)
Async XLA Ops:
  6.5 164.4 %copy-start = (bf16[512,1024]{1,0:T(8,128)(2,1)S(1)}, bf16[512,1024]{1,0:T(8,128)(2,1)}, u32[]{:S(2)}) copy-start(bf16[512,1024]{1,0:T(8,128)(2,1)} %param.22) | copy-start | bytes 3145732
  6.5 61.7 %copy-start.3 = (bf16[1024,128]{1,0:T(8,128)(2,1)S(1)}, bf16[1024,128]{1,0:T(8,128)(2,1)}, u32[]{:S(2)}) copy-start(bf16[1024,128]{1,0:T(8,128)(2,1)} %param.17) | copy-start | bytes 786436
  20.5 48.2 %copy-start.8 = (bf16[1024,8]{0,1:T(8,128)(2,1)S(1)}, bf16[1024,8]{0,1:T(8,128)(2,1)}, u32[]{:S(2)}) copy-start(bf16[1024,8]{0,1:T(8,128)(2,1)} %param.18) | copy-start | bytes 49156
  20.5 48.2 %copy-start.9 = (pred[384,128]{1,0:T(32,128)(4,1)S(1)}, pred[384,128]{1,0:T(32,128)(4,1)}, u32[]{:S(2)}) copy-start(pred[384,128]{1,0:T(32,128)(4,1)} %constant.49.clone) | copy-start | bytes 147460
  20.5 48.2 %copy-start.11 = (bf16[8,128]{1,0:T(8,128)(2,1)S(1)}, bf16[8,128]{1,0:T(8,128)(2,1)}, u32[]{:S(2)}) copy-start(bf16[8,128]{1,0:T(8,128)(2,1)} %constant.48.clone) | copy-start | bytes 6148
  20.5 32.7 %all-to-all-start = ((bf16[16,8,1024]{2,1,0:T(8,128)(2,1)}), bf16[16,8,1024]{2,1,0:T(8,128)(2,1)S(1)}, u32[]{:S(2)}, u32[]{:S(2)}) async-start(bf16[16,8,1024]{2,1,0:T(8,128)(2,1)} %broadcast_in_dim.72), calls=%async_computation | async-start | bytes 524288 | tf_op jit(solution)/shard_map/all_to_all | solution.py:58
  53.3 16.0 %copy-start.6 = (bf16[64,384]{1,0:T(8,128)(2,1)S(1)}, bf16[64,384]{1,0:T(8,128)(2,1)}, u32[]{:S(2)}) copy-start(bf16[64,384]{1,0:T(8,128)(2,1)} %constant.50.clone) | copy-start | bytes 147460
  69.5 17.9 %copy-start.7 = (s32[3]{0:T(128)S(1)}, s32[3]{0:T(128)}, u32[]{:S(2)}) copy-start(s32[3]{0:T(128)} %param.25) | copy-start | bytes 40
  83.1 18.1 %copy-start.10 = (pred[1,64,2]{1,2,0:T(4,128)(4,1)S(1)}, pred[1,64,2]{1,2,0:T(4,128)(4,1)}, u32[]{:S(2)}) copy-start(pred[1,64,2]{1,2,0:T(4,128)(4,1)} %constant.51.clone) | copy-start | bytes 388
  84.1 9.4 %all-to-all-start.1 = ((bf16[4,128,128]{2,1,0:T(8,128)(2,1)}), bf16[4,128,128]{2,1,0:T(8,128)(2,1)S(1)}, u32[]{:S(2)}, u32[]{:S(2)}) async-start(bf16[4,128,128]{2,1,0:T(8,128)(2,1)} %bitcast.4), calls=%async_computation.1 | async-start | bytes 262144 | tf_op jit(solution)/shard_map/all_to_all | solution.py:87
  94.1 19.5 %all-to-all-start.2 = ((bf16[16,32,128]{2,1,0:T(8,128)(2,1)}), bf16[16,32,128]{2,1,0:T(8,128)(2,1)S(1)}, u32[]{:S(2)}, u32[]{:S(2)}) async-start(bf16[16,32,128]{2,1,0:T(8,128)(2,1)} %copy_bitcast_fusion.1), calls=%async_computation.2 | async-start | bytes 262144 | tf_op jit(solution)/shard_map/all_to_all | solution.py:89
  101.1 55.8 %reduce-scatter.2.cloned.1.call-start = ((), (), s32[]{:S(2)}) async-start(), calls=%async_computation.8 | async-start | bytes 1769472 | tf_op jit(solution)/shard_map/reduce_scatter | solution.py:77
  104.9 9.4 %copy-start.2 = (bf16[3,256,256]{2,1,0:T(8,128)(2,1)S(1)}, bf16[3,256,256]{2,1,0:T(8,128)(2,1)}, u32[]{:S(2)}) copy-start(bf16[3,256,256]{2,1,0:T(8,128)(2,1)} %param.23) | copy-start | bytes 1179652
  104.9 10.6 %copy-start.1 = (bf16[3,256,256]{2,1,0:T(8,128)(2,1)S(1)}, bf16[3,256,256]{2,1,0:T(8,128)(2,1)}, u32[]{:S(2)}) copy-start(bf16[3,256,256]{2,1,0:T(8,128)(2,1)} %param.24) | copy-start | bytes 1179652
  155.1 1.5 copy-start.4
  187.0 24.4 %copy-start.5 = (bf16[3,2,1024]{2,1,0:T(2,128)(2,1)S(1)}, bf16[3,2,1024]{2,1,0:T(2,128)(2,1)}, u32[]{:S(2)}) copy-start(bf16[3,2,1024]{2,1,0:T(2,128)(2,1)} %param.15) | copy-start | bytes 36868
Sparse Core Ops, SparseCore 0:
  105.0 38.1 reduce-scatter.1

commit v2 on v1

v2 whole, which is shorter than its diff:
```python
import jax
import jax.numpy as jnp
import numpy as np
from jax import lax
from jax.sharding import Mesh
from jax.sharding import PartitionSpec as P

D = 8192
eps_norm = 1e-05
masked_score = -1e30
bf16 = jnp.bfloat16
f32 = jnp.float32
WIDE = ("z", "y")
NARROW = ("x", "core")


def three_parts(value):
    first = lax.reduce_precision(value, 8, 7)
    rest = value - first
    second = lax.reduce_precision(rest, 8, 7)
    return first, second, lax.reduce_precision(rest - second, 8, 7)


def local(
    activations,
    norm_gain,
    w_query,
    w_keyval,
    w_out,
    w_gate,
    w_up,
    w_down,
    key_cache,
    value_cache,
    lengths,
):
    zs, ys, ns = lax.axis_size("z"), lax.axis_size("y"), lax.axis_size(NARROW)
    ws = zs * ys
    rows, new, width = activations.shape
    toks = rows * new
    mine = zs * toks
    head_dim = key_cache.shape[2]
    kv_cols = w_keyval.shape[1]
    lanes = w_query.shape[1]
    heads = ws * lanes // head_dim
    cols = ys * lanes
    pair_cols = ys * kv_cols
    per_z = cols // head_dim
    ffn = w_gate.shape[1]

    values = activations.reshape(toks, width).astype(f32)
    sums = jnp.concatenate([values.sum(-1), (values * values).sum(-1)])
    sums = jnp.pad(sums, (0, 128 - 2 * toks))[None]
    sums = lax.all_gather(sums, NARROW, axis=0, tiled=True).sum(0)
    centre = sums[:toks, None] / D
    spread = sums[toks : 2 * toks, None] / D - centre * centre
    normed = ((values - centre) * lax.rsqrt(spread + eps_norm) * norm_gain).astype(bf16)

    w_first = lax.all_gather(jnp.concatenate([w_query, w_keyval], axis=1), "y", axis=0, tiled=False)
    w_last = lax.all_gather(w_out, "y", axis=0, tiled=True)

    packed = normed.reshape(toks * width // 128, 128)
    copies = jnp.broadcast_to(packed[None], (zs,) + packed.shape)
    column = lax.all_to_all(copies, "z", 0, 0, tiled=True).reshape(mine, width)

    flat = lax.all_gather(column, "y", axis=0, tiled=True)
    gate_up = jnp.dot(flat, jnp.concatenate([w_gate, w_up], axis=1), preferred_element_type=f32)
    column, gate_up = lax.optimization_barrier((column, gate_up))
    gate_up = lax.psum_scatter(gate_up, NARROW, scatter_dimension=0, tiled=True)

    query_part = jnp.concatenate(
        [jnp.dot(column, w_first[k, :, :lanes], preferred_element_type=f32) for k in range(ys)], axis=1
    ).astype(bf16)
    lane = np.arange(cols)
    spreader = jnp.asarray(
        (lane[None, :] % pair_cols == np.arange(pair_cols)[:, None]) & (lane[None, :] < toks * pair_cols), bf16
    )
    w_pair = jnp.concatenate([w_first[k, :, lanes:] for k in range(ys)], axis=1)
    w_pair = jnp.dot(w_pair, spreader, preferred_element_type=f32).astype(bf16)
    pair_part = jnp.dot(column, w_pair, preferred_element_type=f32).astype(bf16)
    keep = (lane[None, :] // pair_cols) == (np.arange(mine)[:, None] % toks)
    pair_part = jnp.where(keep, pair_part, jnp.zeros_like(pair_part))
    collect = jnp.asarray(np.arange(zs)[:, None] == (np.arange(mine)[None, :] // toks), bf16)
    pair_rows = jnp.dot(collect, pair_part, preferred_element_type=f32).astype(bf16)
    parts = jnp.concatenate([query_part, pair_rows], axis=0)
    parts = lax.all_gather(parts, NARROW, axis=0, tiled=False)
    summed = parts.astype(f32).sum(0).astype(bf16)
    block = jnp.concatenate(
        [
            summed[:mine].reshape(zs, toks, cols),
            summed[mine:][:, None, :],
            jnp.zeros((zs, 8 - toks - 1, cols), bf16),
        ],
        axis=1,
    )
    block = lax.all_to_all(block, "z", 0, 0, tiled=True)

    queries = (
        block[:, :toks]
        .reshape(zs, rows, new, per_z, head_dim)
        .transpose(1, 2, 0, 3, 4)
        .reshape(rows, new * heads, head_dim)
    )
    pairs = (
        block[:, toks, : toks * pair_cols]
        .reshape(zs, toks, pair_cols)
        .transpose(1, 0, 2)
        .reshape(rows, new, 2 * head_dim)
    )
    new_keys, new_values = pairs[..., :head_dim], pairs[..., head_dim:]
    narrow_index = lax.axis_index(NARROW)
    cache_part = key_cache.shape[1]
    factor = head_dim ** (-0.5)
    positions = narrow_index * cache_part + jnp.arange(cache_part, dtype=jnp.int32)
    usable = (positions[None, :] < lengths[:, None])[:, None, :]
    scores = jnp.einsum("rqd,rpd->rqp", queries, key_cache, preferred_element_type=f32) * factor
    scores = jnp.where(usable, scores, masked_score)
    own = jnp.einsum("rqd,rud->rqu", queries, new_keys, preferred_element_type=f32) * factor
    token_of = np.arange(new * heads) // heads
    causal = (token_of[:, None] >= np.arange(new)[None, :])[None]
    causal = jnp.logical_and(causal, narrow_index == 0)
    own = jnp.where(causal, own, masked_score)
    top = jnp.maximum(scores.max(-1), own.max(-1))
    weights = jnp.where(usable, jnp.exp(scores - top[..., None]), 0.0)
    own_weights = jnp.where(causal, jnp.exp(own - top[..., None]), 0.0)
    total = weights.sum(-1) + own_weights.sum(-1)
    weighted = jnp.einsum("rqp,rpd->rqd", weights.astype(bf16), value_cache, preferred_element_type=f32)
    weighted = weighted + jnp.einsum("rqu,rud->rqd", own_weights, new_values.astype(f32))

    sent = (
        weighted.astype(bf16)
        .reshape(rows, new, zs, per_z, head_dim)
        .transpose(2, 0, 1, 3, 4)
        .reshape(zs, toks, cols)
    )
    marks = jnp.stack(three_parts(top) + three_parts(total)).astype(bf16)
    marks = marks.reshape(6, toks, zs, per_z).transpose(2, 3, 0, 1)
    marks = jnp.pad(marks, ((0, 0), (0, 0), (0, 0), (0, 8 - toks))).reshape(zs, per_z, 48)
    marks = jnp.pad(marks, ((0, 0), (0, 0), (0, head_dim - 48))).reshape(zs, 1, cols)
    block = jnp.concatenate([sent, marks, jnp.zeros((zs, 8 - toks - 1, cols), bf16)], axis=1)
    block = lax.all_to_all(block, "z", 0, 0, tiled=True)
    parts = jnp.concatenate([block[:, :toks].reshape(mine, cols), block[:, toks]], axis=0)
    parts = lax.all_gather(parts, NARROW, axis=0, tiled=False)
    weighted = parts[:, :mine].astype(f32).reshape(ns, zs, toks, per_z, head_dim)
    marks = parts[:, mine:].astype(f32).reshape(ns, zs, per_z, head_dim)[..., :48]
    marks = marks.reshape(ns, zs, per_z, 6, 8)[..., :toks].transpose(3, 0, 1, 4, 2)
    top = marks[0] + marks[1] + marks[2]
    total = marks[3] + marks[4] + marks[5]
    scale = jnp.exp(top - top.max(0))
    scale = scale / (total * scale).sum(0)
    attended = (weighted * scale[..., None]).sum(0).reshape(mine, cols).astype(bf16)
    mixed = jnp.dot(attended, w_last, preferred_element_type=f32)

    hidden = (jax.nn.silu(gate_up[:, :ffn]) * gate_up[:, ffn:]).astype(bf16)
    hidden = lax.all_gather(hidden, NARROW, axis=0, tiled=True)
    down = jnp.dot(hidden, w_down, preferred_element_type=f32).astype(bf16)
    down = lax.all_to_all(down.reshape(ys, mine, width), "y", 0, 0, tiled=True)
    mixed = mixed + down.astype(f32).sum(0)

    mixed = mixed.astype(bf16).reshape(zs, toks * width // 128, 128)
    mixed = lax.all_to_all(mixed, "z", 0, 0, tiled=True)
    mixed = mixed.astype(f32).sum(0).reshape(toks, width)
    return (values + mixed).astype(bf16).reshape(activations.shape)


def solution(mesh):
    names = ("z", "y", "x", "core")
    split = Mesh(mesh.devices.reshape(16, 4, 4, 2), names)
    return jax.shard_map(
        local,
        mesh=split,
        in_specs=(
            P(WIDE, None, NARROW),
            P(NARROW),
            P(NARROW, WIDE),
            P(NARROW, WIDE),
            P(WIDE, NARROW),
            P(NARROW, WIDE),
            P(NARROW, WIDE),
            P(WIDE, NARROW),
            P(WIDE, NARROW, None),
            P(WIDE, NARROW, None),
            P(WIDE),
        ),
        out_specs=P(WIDE, None, NARROW),
        check_vma=False,
    )
```

time: 220 us -> 226 us (1.027)
  the two profiles are of different devices: /device:TPU:64 before, /device:TPU:32 now
where the time goes in v2:
time: 226 us; the launch traced here: 225 us
  blocking collectives  85.4 us (38%)
  waiting for transfers between devices  52.3 us (23%)
  starting transfers between devices  30.5 us (13%)
  matrix products  21.8 us (10%)
  between operations  15.3 us (7%)
  local copies, waits for them, and re-layouts  10.6 us (5%)
  other arithmetic  8.86 us (4%)
    all_to_all x2, waiting for transfers between devices, local(): block = lax.all_to_all(block, 'z', 0, 0, tiled=True)  27.5 us
    all_gather x2, blocking collectives, local(): parts = lax.all_gather(parts, NARROW, axis=0, tiled=False)  27.2 us
    all_to_all x1, blocking collectives, local(): mixed = lax.all_to_all(mixed, 'z', 0, 0, tiled=True)  20.8 us
    all_to_all x1, waiting for transfers between devices, local(): column = lax.all_to_all(copies, 'z', 0, 0, tiled=True).reshape(mine, width)  16.3 us
    all_to_all x1, starting transfers between devices, local(): column = lax.all_to_all(copies, 'z', 0, 0, tiled=True).reshape(mine, width)  15.2 us
    all_gather x1, blocking collectives, local(): flat = lax.all_gather(column, 'y', axis=0, tiled=True)  13.9 us
    all_gather x1, blocking collectives, local(): hidden = lax.all_gather(hidden, NARROW, axis=0, tiled=True)  13 us
    all_to_all x2, starting transfers between devices, local(): block = lax.all_to_all(block, 'z', 0, 0, tiled=True)  11 us
  transfers between devices with their start and end apart: 7, of which 4 were waited for; matrix products, arithmetic and copies ran while one was open for 9% of the time, Pallas kernels for 0%

profile of v2, /device:TPU:32, one launch (start us, length us, event | category | flops | bytes accessed | tf_op | source)
XLA Modules:
  0.0 224.7 jit_solution(7418844767456469345)
XLA Ops:
  8.4 1.8 pad_maximum_fusion
  12.1 10.5 %all-gather.4 = f32[8,1,128]{2,1,0:T(1,128)S(1)} all-gather(f32[1,1,128]{2,1,0:T(1,128)S(1)} %fusion.39), channel_id=2, replica_groups=mesh['z'=16,'y'=4,'x'=4,'core'=2] {'x','core'}, dimensions={0}, use_global_device_ids=true | all-gather | bytes 4608 | tf_op jit(solution)/shard_map/all_gather | solution.py:54
  24.4 15.2 %all-to-all-start = ((bf16[16,48,128]{2,1,0:T(8,128)(2,1)}), bf16[16,48,128]{2,1,0:T(8,128)(2,1)S(1)}, u32[]{:S(2)}, u32[]{:S(2)}) async-start(bf16[16,48,128]{2,1,0:T(8,128)(2,1)} %broadcast_in_dim.65), calls=%async_computation | async-start | bytes 393216 | tf_op jit(solution)/shard_map/all_to_all | solution.py:64
  39.7 16.3 %all-to-all-done = bf16[16,48,128]{2,1,0:T(8,128)(2,1)S(1)} async-done(((bf16[16,48,128]{2,1,0:T(8,128)(2,1)}), bf16[16,48,128]{2,1,0:T(8,128)(2,1)S(1)}, u32[]{:S(2)}, u32[]{:S(2)}) %all-to-all-start) | async-done | bytes 196640 | tf_op jit(solution)/shard_map/all_to_all | solution.py:64
  56.1 13.9 %all_gather.31 = bf16[384,1024]{1,0:T(8,128)(2,1)S(1)} all-gather(bf16[96,1024]{1,0:T(8,128)(2,1)S(1)} %reshape.277), channel_id=1, replica_groups=mesh['z'=16,'y'=4,'x'=4,'core'=2] {'y'}, dimensions={0}, use_global_device_ids=true | all-gather | bytes 983040 | tf_op jit(solution)/shard_map/all_gather | solution.py:66
  70.0 3.4 %fusion = f32[384,1024]{1,0:T(8,128)} fusion(bf16[384,1024]{1,0:T(8,128)(2,1)S(1)} %all_gather.31, bf16[1024,512]{1,0:T(8,128)(2,1)S(1)} %copy-done.10, bf16[1024,512]{1,0:T(8,128)(2,1)} %param.20), kind=kOutput, calls=%fused_computation | convolution fusion | flops 809500672 | bytes 4456448 | tf_op jit(solution)/shard_map/dot_general | solution.py:67
  78.0 1.4 fusion.12
  79.4 2.7 %fusion.14 = f32[1024,512]{1,0:T(8,128)} fusion(bf16[8,512]{1,0:T(8,128)(2,1)S(1)} %copy-done.6, bf16[4,1024,136]{2,1,0:T(8,128)(2,1)} %bitcast.122), kind=kOutput, calls=%fused_computation.34 | convolution fusion | flops 8388608 | bytes 2367488 | tf_op jit(solution)/shard_map/dot_general | solution.py:79
  82.1 2.7 %fusion.13 = f32[1024,512]{1,0:T(8,128)} fusion(bf16[8,512]{1,0:T(8,128)(2,1)S(1)} %copy-done.5, bf16[4,1024,136]{2,1,0:T(8,128)(2,1)} %bitcast.123), kind=kOutput, calls=%fused_computation.32 | convolution fusion | flops 8388608 | bytes 2367488 | tf_op jit(solution)/shard_map/dot_general | solution.py:79
  84.8 3.0 %fusion.9 = bf16[96,512]{1,0:T(8,128)(2,1)S(1)} fusion(pred[96,512]{1,0:T(32,128)(4,1)} %constant.47.clone, bf16[96,1024]{1,0:T(8,128)(2,1)S(1)} %reshape.277, f32[1024,512]{1,0:T(8,128)S(1)} %fusion.12, f32[1024,512]{1,0:T(8,128)} %fusion.14, f32[1024,512]{1,0:T(8,128)} %fusion.13, bf16[8,512]{1,0:T(8,128)(2,1)S(1)} %copy-done.4, ...), kind=kOutput, calls=%fused_computation.16 | convolution fusion | flops 111247360 | bytes 6905856 | tf_op jit(solution)/shard_map/dot_general | solution.py:80
  87.9 13.6 %all-gather.2 = bf16[896,512]{1,0:T(8,128)(2,1)S(1)} all-gather(bf16[112,512]{1,0:T(8,128)(2,1)S(1)} %pad_maximum_fusion.1), channel_id=4, replica_groups=mesh['z'=16,'y'=4,'x'=4,'core'=2] {'x','core'}, dimensions={0}, use_global_device_ids=true | all-gather | bytes 1032192 | tf_op jit(solution)/shard_map/all_gather | solution.py:86
  102.5 6.3 %all-to-all-start.1 = ((bf16[16,8,512]{2,1,0:T(8,128)(2,1)}), bf16[16,8,512]{2,1,0:T(8,128)(2,1)S(1)}, u32[]{:S(2)}, u32[]{:S(2)}) async-start(bf16[16,8,512]{2,1,0:T(8,128)(2,1)} %maximum_maximum_fusion), calls=%async_computation.1 | async-start | bytes 262144 | tf_op jit(solution)/shard_map/all_to_all | solution.py:96
  109.4 13.8 %all-to-all-done.1 = bf16[16,8,512]{2,1,0:T(8,128)(2,1)S(1)} async-done(((bf16[16,8,512]{2,1,0:T(8,128)(2,1)}), bf16[16,8,512]{2,1,0:T(8,128)(2,1)S(1)}, u32[]{:S(2)}, u32[]{:S(2)}) %all-to-all-start.1) | async-done | bytes 131104 | tf_op jit(solution)/shard_map/all_to_all | solution.py:96
  126.5 4.7 %all-to-all-start.2 = ((bf16[16,8,512]{2,1,0:T(8,128)(2,1)}), bf16[16,8,512]{2,1,0:T(8,128)(2,1)S(1)}, u32[]{:S(2)}, u32[]{:S(2)}) async-start(bf16[16,8,512]{2,1,0:T(8,128)(2,1)} %copy.93), calls=%async_computation.2 | async-start | bytes 262144 | tf_op jit(solution)/shard_map/all_to_all | solution.py:141
  132.0 13.7 %all-to-all-done.2 = bf16[16,8,512]{2,1,0:T(8,128)(2,1)S(1)} async-done(((bf16[16,8,512]{2,1,0:T(8,128)(2,1)}), bf16[16,8,512]{2,1,0:T(8,128)(2,1)S(1)}, u32[]{:S(2)}, u32[]{:S(2)}) %all-to-all-start.2) | async-done | bytes 131104 | tf_op jit(solution)/shard_map/all_to_all | solution.py:141
  145.8 13.6 %all-gather.3 = bf16[896,512]{1,0:T(8,128)(2,1)S(1)} all-gather(bf16[112,512]{1,0:T(8,128)(2,1)S(1)} %pad_maximum_fusion.2), channel_id=5, replica_groups=mesh['z'=16,'y'=4,'x'=4,'core'=2] {'x','core'}, dimensions={0}, use_global_device_ids=true | all-gather | bytes 1032192 | tf_op jit(solution)/shard_map/all_gather | solution.py:143
  161.0 13.0 %all_gather.39 = bf16[384,512]{1,0:T(8,128)(2,1)S(1)} all-gather(bf16[48,512]{1,0:T(8,128)(2,1)S(1)} %fusion.18), channel_id=1, replica_groups=mesh['z'=16,'y'=4,'x'=4,'core'=2] {'x','core'}, dimensions={0}, use_global_device_ids=true | all-gather | bytes 442368 | tf_op jit(solution)/shard_map/all_gather | solution.py:155
  173.9 1.5 convolution_convert_fusion
  175.4 4.2 %all-to-all-start.3 = ((bf16[4,96,1024]{2,1,0:T(8,128)(2,1)}), bf16[4,96,1024]{2,1,0:T(8,128)(2,1)}, u32[]{:S(2)}, u32[]{:S(2)}) async-start(bf16[4,96,1024]{2,1,0:T(8,128)(2,1)} %bitcast.28), calls=%async_computation.4 | async-start | bytes 1572864 | tf_op jit(solution)/shard_map/all_to_all | solution.py:157
  180.2 1.9 mul.96
  182.0 2.5 %mul.97 = f32[8,96,512]{2,1,0:T(8,128)S(1)} reshape(f32[8,16,6,2,256]{4,3,2,1,0:T(2,128)} %mul.96) | data formatting | bytes 3145728 | tf_op jit(solution)/shard_map/mul | solution.py:151
  185.5 7.3 %all-to-all-done.3 = bf16[4,96,1024]{2,1,0:T(8,128)(2,1)} async-done(((bf16[4,96,1024]{2,1,0:T(8,128)(2,1)}), bf16[4,96,1024]{2,1,0:T(8,128)(2,1)}, u32[]{:S(2)}, u32[]{:S(2)}) %all-to-all-start.3) | async-done | bytes 786464 | tf_op jit(solution)/shard_map/all_to_all | solution.py:157
  194.1 1.6 fusion.5
  195.8 20.8 %all_to_all.25 = bf16[16,48,128]{2,1,0:T(8,128)(2,1)S(1)} all-to-all(bf16[16,48,128]{2,1,0:T(8,128)(2,1)S(1)} %reshape.290), channel_id=1, replica_groups=mesh['z'=16,'y'=4,'x'=4,'core'=2] {'z'}, dimensions={0} | all-to-all | bytes 393216 | tf_op jit(solution)/shard_map/all_to_all | solution.py:161
  (116 shorter events, 20.2 us)
Async XLA Ops:
  7.4 166.6 %copy-start = (bf16[512,1024]{1,0:T(8,128)(2,1)S(1)}, bf16[512,1024]{1,0:T(8,128)(2,1)}, u32[]{:S(2)}) copy-start(bf16[512,1024]{1,0:T(8,128)(2,1)} %param.22) | copy-start | bytes 3145732
  7.4 62.6 %copy-start.10 = (bf16[1024,512]{1,0:T(8,128)(2,1)S(1)}, bf16[1024,512]{1,0:T(8,128)(2,1)}, u32[]{:S(2)}) copy-start(bf16[1024,512]{1,0:T(8,128)(2,1)} %param.21) | copy-start | bytes 3145732
  7.4 66.0 %all-gather.10.cloned.1.call-start = ((), (), s32[]{:S(2)}) async-start(), calls=%async_computation.8 | async-start | bytes 2621440 | tf_op jit(solution)/shard_map/all_gather | solution.py:59
  24.4 31.6 %all-to-all-start = ((bf16[16,48,128]{2,1,0:T(8,128)(2,1)}), bf16[16,48,128]{2,1,0:T(8,128)(2,1)S(1)}, u32[]{:S(2)}, u32[]{:S(2)}) async-start(bf16[16,48,128]{2,1,0:T(8,128)(2,1)} %broadcast_in_dim.65), calls=%async_computation | async-start | bytes 393216 | tf_op jit(solution)/shard_map/all_to_all | solution.py:64
  70.0 8.0 %copy-start.7 = (bf16[8,512]{1,0:T(8,128)(2,1)S(1)}, bf16[8,512]{1,0:T(8,128)(2,1)}, u32[]{:S(2)}) copy-start(bf16[8,512]{1,0:T(8,128)(2,1)} %constant.63) | copy-start | bytes 24580
  73.4 6.0 %copy-start.6 = (bf16[8,512]{1,0:T(8,128)(2,1)S(1)}, bf16[8,512]{1,0:T(8,128)(2,1)}, u32[]{:S(2)}) copy-start(bf16[8,512]{1,0:T(8,128)(2,1)} %constant.61) | copy-start | bytes 24580
  78.0 4.0 %copy-start.5 = (bf16[8,512]{1,0:T(8,128)(2,1)S(1)}, bf16[8,512]{1,0:T(8,128)(2,1)}, u32[]{:S(2)}) copy-start(bf16[8,512]{1,0:T(8,128)(2,1)} %constant.62) | copy-start | bytes 24580
  79.4 5.3 %copy-start.4 = (bf16[8,512]{1,0:T(8,128)(2,1)S(1)}, bf16[8,512]{1,0:T(8,128)(2,1)}, u32[]{:S(2)}) copy-start(bf16[8,512]{1,0:T(8,128)(2,1)} %constant.64) | copy-start | bytes 24580
  84.8 3.0 %copy-start.8 = (bf16[16,96]{1,0:T(8,128)(2,1)S(1)}, bf16[16,96]{1,0:T(8,128)(2,1)}, u32[]{:S(2)}) copy-start(bf16[16,96]{1,0:T(8,128)(2,1)} %constant.48.clone) | copy-start | bytes 9220
  87.7 21.2 %copy-start.11 = (pred[1,64,2]{1,2,0:T(4,128)(4,1)S(1)}, pred[1,64,2]{1,2,0:T(4,128)(4,1)}, u32[]{:S(2)}) copy-start(pred[1,64,2]{1,2,0:T(4,128)(4,1)} %constant.49.clone) | copy-start | bytes 388
  87.8 21.2 %copy-start.9 = (s32[3]{0:T(128)S(1)}, s32[3]{0:T(128)}, u32[]{:S(2)}) copy-start(s32[3]{0:T(128)} %param.25) | copy-start | bytes 40
  101.5 22.3 %copy-start.2 = (bf16[3,256,256]{2,1,0:T(8,128)(2,1)S(1)}, bf16[3,256,256]{2,1,0:T(8,128)(2,1)}, u32[]{:S(2)}) copy-start(bf16[3,256,256]{2,1,0:T(8,128)(2,1)} %param.23) | copy-start | bytes 1179652
  102.5 22.8 %copy-start.1 = (bf16[3,256,256]{2,1,0:T(8,128)(2,1)S(1)}, bf16[3,256,256]{2,1,0:T(8,128)(2,1)}, u32[]{:S(2)}) copy-start(bf16[3,256,256]{2,1,0:T(8,128)(2,1)} %param.24) | copy-start | bytes 1179652
  102.5 20.7 %all-to-all-start.1 = ((bf16[16,8,512]{2,1,0:T(8,128)(2,1)}), bf16[16,8,512]{2,1,0:T(8,128)(2,1)S(1)}, u32[]{:S(2)}, u32[]{:S(2)}) async-start(bf16[16,8,512]{2,1,0:T(8,128)(2,1)} %maximum_maximum_fusion), calls=%async_computation.1 | async-start | bytes 262144 | tf_op jit(solution)/shard_map/all_to_all | solution.py:96
  108.8 51.1 %reduce-scatter.2.cloned.1.call-start = ((), (), s32[]{:S(2)}) async-start(), calls=%async_computation.7 | async-start | bytes 1769472 | tf_op jit(solution)/shard_map/reduce_scatter | solution.py:69
  126.5 19.1 %all-to-all-start.2 = ((bf16[16,8,512]{2,1,0:T(8,128)(2,1)}), bf16[16,8,512]{2,1,0:T(8,128)(2,1)S(1)}, u32[]{:S(2)}, u32[]{:S(2)}) async-start(bf16[16,8,512]{2,1,0:T(8,128)(2,1)} %copy.93), calls=%async_computation.2 | async-start | bytes 262144 | tf_op jit(solution)/shard_map/all_to_all | solution.py:141
  131.2 62.9 %all-gather.8.cloned.1.call-start = ((), (), s32[]{:S(2)}) async-start(), calls=%async_computation.6 | async-start | bytes 1310720 | tf_op jit(solution)/shard_map/all_gather | solution.py:60
  175.4 17.3 %all-to-all-start.3 = ((bf16[4,96,1024]{2,1,0:T(8,128)(2,1)}), bf16[4,96,1024]{2,1,0:T(8,128)(2,1)}, u32[]{:S(2)}, u32[]{:S(2)}) async-start(bf16[4,96,1024]{2,1,0:T(8,128)(2,1)} %bitcast.28), calls=%async_computation.4 | async-start | bytes 1572864 | tf_op jit(solution)/shard_map/all_to_all | solution.py:157
  185.5 31.2 %copy-start.3 = (bf16[3,2,1024]{2,1,0:T(2,128)(2,1)S(1)}, bf16[3,2,1024]{2,1,0:T(2,128)(2,1)}, u32[]{:S(2)}) copy-start(bf16[3,2,1024]{2,1,0:T(2,128)(2,1)} %param.15) | copy-start | bytes 36868
Sparse Core Ops, SparseCore 0:
  10.4 42.6 all-gather.9
  134.2 30.3 all-gather.7
Sparse Core Ops, SparseCore 1:
  112.1 39.5 reduce-scatter.1

commit v3 on v2

--- a/solution.py
+++ b/solution.py
@@ -1,7 +1,11 @@
+import functools
+
 import jax
 import jax.numpy as jnp
 import numpy as np
 from jax import lax
+from jax.experimental import pallas as pl
+from jax.experimental.pallas import tpu as pltpu
 from jax.sharding import Mesh
 from jax.sharding import PartitionSpec as P
 
@@ -10,6 +14,8 @@
 masked_score = -1e30
 bf16 = jnp.bfloat16
 f32 = jnp.float32
+vmem = pl.BlockSpec(memory_space=pltpu.VMEM)
+anywhere = pl.BlockSpec(memory_space=pl.ANY)
 WIDE = ("z", "y")
 NARROW = ("x", "core")
 
@@ -19,6 +25,108 @@
     rest = value - first
     second = lax.reduce_precision(rest, 8, 7)
     return first, second, lax.reduce_precision(rest - second, 8, 7)
+
+
+def iota(shape, axis):
+    return lax.broadcasted_iota(jnp.int32, shape, axis)
+
+
+def first_kernel(toks, column_ref, source_ref, parts_ref, weights_ref, sems):
+    mine, width = column_ref.shape
+    ys, _, lanes = weights_ref.shape
+    cols = ys * lanes
+    chunks = width // lanes
+    copies = [pltpu.make_async_copy(source_ref.at[k], weights_ref.at[k], sems.at[k]) for k in range(ys)]
+    for copy in copies:
+        copy.start()
+    column = column_ref[...]
+    pairs = []
+    for k in range(ys):
+        copies[k].wait()
+        query = jnp.dot(column, weights_ref[k, :width], preferred_element_type=f32)
+        parts_ref[:mine, k * lanes : (k + 1) * lanes] = query.astype(bf16)
+        rows = weights_ref[k, width:].astype(f32)
+        count = rows.shape[0] // chunks
+        pairs.append(jnp.concatenate([rows[j * count : (j + 1) * count] for j in range(chunks)], axis=1))
+    pairs = jnp.concatenate(pairs, axis=0).astype(bf16)
+    count = pairs.shape[0]
+    pairs = lax.dot_general(column, pairs, (((1,), (1,)), ((), ())), preferred_element_type=f32).astype(bf16)
+    at = iota((count, cols), 1)
+    spread = jnp.where((lax.rem(at, count) == iota((count, cols), 0)) & (at < toks * count), 1.0, 0.0)
+    pairs = jnp.dot(pairs, spread.astype(bf16), preferred_element_type=f32)
+    start = lax.rem(iota((mine, cols), 0), toks) * count
+    at = iota((mine, cols), 1)
+    pairs = jnp.where((at >= start) & (at < start + count), pairs, 0.0).astype(bf16)
+    start = iota((mine // toks, mine), 0) * toks
+    at = iota((mine // toks, mine), 1)
+    collect = jnp.where((at >= start) & (at < start + toks), 1.0, 0.0).astype(bf16)
+    parts_ref[mine:] = jnp.dot(collect, pairs, preferred_element_type=f32).astype(bf16)
+
+
+def second_kernel(toks, gate_up_ref, parts_ref, hidden_ref, block_ref):
+    ns, rows, cols = parts_ref.shape
+    ffn = hidden_ref.shape[1]
+    gate = gate_up_ref[0, :, :ffn].astype(f32)
+    up = gate_up_ref[0, :, ffn:].astype(f32)
+    total = parts_ref[0].astype(f32)
+    for n in range(1, ns):
+        gate = gate + gate_up_ref[n, :, :ffn].astype(f32)
+        up = up + gate_up_ref[n, :, ffn:].astype(f32)
+        total = total + parts_ref[n].astype(f32)
+    hidden_ref[...] = (gate / (1.0 + jnp.exp(-gate)) * up).astype(bf16)
+    shape = (block_ref.shape[0], rows)
+    zs = shape[0] // 8
+    to, at = iota(shape, 0), iota(shape, 1)
+    row = lax.rem(to, 8)
+    z = (to - row) // 8
+    take = ((row < toks) & (at == z * toks + row)) | ((row == toks) & (at == zs * toks + z))
+    take = jnp.where(take, 1.0, 0.0).astype(bf16)
+    block_ref[...] = jnp.dot(take, total.astype(bf16), preferred_element_type=f32).astype(bf16)
+
+
+def last_kernel(toks, per_z, parts_ref, source_ref, down_ref, mixed_ref, weights_ref, sem):
+    ns, rows, cols = parts_ref.shape
+    mine = mixed_ref.shape[0]
+    zs = rows - mine
+    copy = pltpu.make_async_copy(source_ref, weights_ref, sem)
+    copy.start()
+    head = cols // per_z
+    shape = (ns * mine, ns * zs)
+    start = iota(shape, 1) * toks
+    at = iota(shape, 0)
+    expand = jnp.where((at >= start) & (at < start + toks), 1.0, 0.0).astype(bf16)
+    shape = (ns * mine, 128)
+    at = iota(shape, 1)
+    own = (lax.rem(at, 8) == lax.rem(iota(shape, 0), toks)) & (at < 48)
+    at = iota((128, 128), 0)
+    pick_top = jnp.where(at < 24, 1.0, 0.0).astype(bf16)
+    pick_total = jnp.where((at >= 24) & (at < 48), 1.0, 0.0).astype(bf16)
+    mixed = down_ref[...].astype(f32)
+    for k in range(per_z):
+        marks = jnp.concatenate([parts_ref[n, mine:, k * head : k * head + 128] for n in range(ns)], axis=0)
+        marks = jnp.dot(expand, marks, preferred_element_type=f32)
+        marks = jnp.where(own, marks, 0.0).astype(bf16)
+        tops = jnp.dot(marks, pick_top, preferred_element_type=f32)
+        totals = jnp.dot(marks, pick_total, preferred_element_type=f32)
+        tops = [tops[n * mine : (n + 1) * mine] for n in range(ns)]
+        top = tops[0]
+        for n in range(1, ns):
+            top = jnp.maximum(top, tops[n])
+        total = jnp.zeros((mine, 128), f32)
+        weighted = jnp.zeros((mine, head), f32)
+        for n in range(ns):
+            scale = jnp.exp(tops[n] - top)
+            total = total + totals[n * mine : (n + 1) * mine] * scale
+            scale = jnp.concatenate([scale] * (head // 128), axis=1)
+            weighted = weighted + parts_ref[n, :mine, k * head : (k + 1) * head].astype(f32) * scale
+        total = jnp.concatenate([total] * (head // 128), axis=1)
+        attended = (weighted / total).astype(bf16)
+        if k == 0:
+            copy.wait()
+        mixed = mixed + jnp.dot(
+            attended, weights_ref[k * head : (k + 1) * head], preferred_element_type=f32
+        )
+    mixed_ref[...] = mixed.astype(bf16)
 
 
 def local(
@@ -56,44 +164,45 @@
     spread = sums[toks : 2 * toks, None] / D - centre * centre
     normed = ((values - centre) * lax.rsqrt(spread + eps_norm) * norm_gain).astype(bf16)
 
-    w_first = lax.all_gather(jnp.concatenate([w_query, w_keyval], axis=1), "y", axis=0, tiled=False)
+    chunks = width // lanes
+    pair_lanes = w_keyval.T.reshape(kv_cols, chunks, lanes).transpose(1, 0, 2).reshape(chunks * kv_cols, lanes)
+    w_first = lax.all_gather(jnp.concatenate([w_query, pair_lanes], axis=0), "y", axis=0, tiled=False)
     w_last = lax.all_gather(w_out, "y", axis=0, tiled=True)
+    w_hidden = lax.optimization_barrier(jnp.concatenate([w_gate, w_up], axis=1))
 
     packed = normed.reshape(toks * width // 128, 128)
     copies = jnp.broadcast_to(packed[None], (zs,) + packed.shape)
     column = lax.all_to_all(copies, "z", 0, 0, tiled=True).reshape(mine, width)
 
     flat = lax.all_gather(column, "y", axis=0, tiled=True)
-    gate_up = jnp.dot(flat, jnp.concatenate([w_gate, w_up], axis=1), preferred_element_type=f32)
+    gate_up = jnp.dot(flat, w_hidden, preferred_element_type=f32).astype(bf16)
     column, gate_up = lax.optimization_barrier((column, gate_up))
-    gate_up = lax.psum_scatter(gate_up, NARROW, scatter_dimension=0, tiled=True)
-
-    query_part = jnp.concatenate(
-        [jnp.dot(column, w_first[k, :, :lanes], preferred_element_type=f32) for k in range(ys)], axis=1
-    ).astype(bf16)
-    lane = np.arange(cols)
-    spreader = jnp.asarray(
-        (lane[None, :] % pair_cols == np.arange(pair_cols)[:, None]) & (lane[None, :] < toks * pair_cols), bf16
-    )
-    w_pair = jnp.concatenate([w_first[k, :, lanes:] for k in range(ys)], axis=1)
-    w_pair = jnp.dot(w_pair, spreader, preferred_element_type=f32).astype(bf16)
-    pair_part = jnp.dot(column, w_pair, preferred_element_type=f32).astype(bf16)
-    keep = (lane[None, :] // pair_cols) == (np.arange(mine)[:, None] % toks)
-    pair_part = jnp.where(keep, pair_part, jnp.zeros_like(pair_part))
-    collect = jnp.asarray(np.arange(zs)[:, None] == (np.arange(mine)[None, :] // toks), bf16)
-    pair_rows = jnp.dot(collect, pair_part, preferred_element_type=f32).astype(bf16)
-    parts = jnp.concatenate([query_part, pair_rows], axis=0)
+    gate_up = lax.all_to_all(gate_up.reshape(ns, -1, 2 * ffn), NARROW, 0, 0, tiled=True)
+
+    parts = pl.pallas_call(
+        functools.partial(first_kernel, toks),
+        out_shape=jax.ShapeDtypeStruct((mine + zs, cols), bf16),
+        in_specs=[vmem, anywhere],
+        out_specs=vmem,
+        scratch_shapes=[pltpu.VMEM(w_first.shape, bf16), pltpu.SemaphoreType.DMA((ys,))],
+        compiler_params=pltpu.CompilerParams(vmem_limit_bytes=24 * 2**20),
+        cost_estimate=pl.CostEstimate(flops=2 * mine * width * cols, bytes_accessed=2 * 2**20, transcendentals=0),
+        name="first",
+    )(column, w_first)
     parts = lax.all_gather(parts, NARROW, axis=0, tiled=False)
-    summed = parts.astype(f32).sum(0).astype(bf16)
-    block = jnp.concatenate(
-        [
-            summed[:mine].reshape(zs, toks, cols),
-            summed[mine:][:, None, :],
-            jnp.zeros((zs, 8 - toks - 1, cols), bf16),
-        ],
-        axis=1,
-    )
-    block = lax.all_to_all(block, "z", 0, 0, tiled=True)
+    hidden, block = pl.pallas_call(
+        functools.partial(second_kernel, toks),
+        out_shape=(
+            jax.ShapeDtypeStruct((gate_up.shape[1], ffn), bf16),
+            jax.ShapeDtypeStruct((zs * 8, cols), bf16),
+        ),
+        in_specs=[vmem, vmem],
+        out_specs=(vmem, vmem),
+        compiler_params=pltpu.CompilerParams(vmem_limit_bytes=24 * 2**20),
+        cost_estimate=pl.CostEstimate(flops=2**24, bytes_accessed=2 * 2**20, transcendentals=0),
+        name="second",
+    )(gate_up, parts)
+    block = lax.all_to_all(block.reshape(zs, 8, cols), "z", 0, 0, tiled=True)
 
     queries = (
         block[:, :toks]
@@ -141,23 +250,23 @@
     block = lax.all_to_all(block, "z", 0, 0, tiled=True)
     parts = jnp.concatenate([block[:, :toks].reshape(mine, cols), block[:, toks]], axis=0)
     parts = lax.all_gather(parts, NARROW, axis=0, tiled=False)
-    weighted = parts[:, :mine].astype(f32).reshape(ns, zs, toks, per_z, head_dim)
-    marks = parts[:, mine:].astype(f32).reshape(ns, zs, per_z, head_dim)[..., :48]
-    marks = marks.reshape(ns, zs, per_z, 6, 8)[..., :toks].transpose(3, 0, 1, 4, 2)
-    top = marks[0] + marks[1] + marks[2]
-    total = marks[3] + marks[4] + marks[5]
-    scale = jnp.exp(top - top.max(0))
-    scale = scale / (total * scale).sum(0)
-    attended = (weighted * scale[..., None]).sum(0).reshape(mine, cols).astype(bf16)
-    mixed = jnp.dot(attended, w_last, preferred_element_type=f32)
-
-    hidden = (jax.nn.silu(gate_up[:, :ffn]) * gate_up[:, ffn:]).astype(bf16)
     hidden = lax.all_gather(hidden, NARROW, axis=0, tiled=True)
     down = jnp.dot(hidden, w_down, preferred_element_type=f32).astype(bf16)
-    down = lax.all_to_all(down.reshape(ys, mine, width), "y", 0, 0, tiled=True)
-    mixed = mixed + down.astype(f32).sum(0)
-
-    mixed = mixed.astype(bf16).reshape(zs, toks * width // 128, 128)
+    down = lax.psum_scatter(down, "y", scatter_dimension=0, tiled=True)
+
+    mixed = pl.pallas_call(
+        functools.partial(last_kernel, toks, per_z),
+        out_shape=jax.ShapeDtypeStruct((mine, width), bf16),
+        in_specs=[vmem, anywhere, vmem],
+        out_specs=vmem,
+        scratch_shapes=[pltpu.VMEM(w_last.shape, bf16), pltpu.SemaphoreType.DMA],
+        compiler_params=pltpu.CompilerParams(vmem_limit_bytes=24 * 2**20),
+        cost_estimate=pl.CostEstimate(
+            flops=2 * mine * width * cols, bytes_accessed=3 * 2**20, transcendentals=0
+        ),
+        name="last",
+    )(parts, w_last, down)
+    mixed = mixed.reshape(zs, toks * width // 128, 128)
     mixed = lax.all_to_all(mixed, "z", 0, 0, tiled=True)
     mixed = mixed.astype(f32).sum(0).reshape(toks, width)
     return (values + mixed).astype(bf16).reshape(activations.shape)

time: 226 us -> 193 us (0.85)
  waiting for transfers between devices: 52.3 us -> 14.6 us
  blocking collectives: 85.4 us -> 118 us
  matrix products: 21.8 us -> 4.31 us
  starting transfers between devices: 30.5 us -> 24.6 us
  Pallas kernels: 0 us -> 3.86 us
  local copies, waits for them, and re-layouts: 10.6 us -> 6.84 us
  other arithmetic: 8.86 us -> 6.52 us
    all_to_all x3 -> x2, waiting for transfers between devices: 34.8 us -> 0.01 us  [the longest x1 0.01 us: local(): lax.all_to_all(gate_up.reshape(ns, -1, 2 * ffn), NARROW, 0, 0, tiled=True)]
    all_to_all x0 -> x1, blocking collectives: none -> 26.2 us  [local(): block = lax.all_to_all(block, 'z', 0, 0, tiled=True)]
    dot_general x11 -> x1, matrix products: 19.4 us -> 1.88 us  [local(): gate_up = jnp.dot(flat, w_hidden, preferred_element_type=f32).astype(bf16)]
    all_to_all x3 -> x2, starting transfers between devices: 15.2 us -> 9.33 us  [the longest x1 5.78 us: local(): block = lax.all_to_all(block.reshape(zs, 8, cols), 'z', 0, 0, tiled=True)]
    all_gather x2, blocking collectives: 27.2 us -> 32.7 us  [local(): parts = lax.all_gather(parts, NARROW, axis=0, tiled=False)]
    mul x2 -> x0, local copies, waits for them, and re-layouts: 4.4 us -> none  [local(): weighted * scale[..., None]]
    pallas_call x0 -> x3, Pallas kernels: none -> 3.86 us  [the longest x1 1.41 us: local(): pl.pallas_call(functools.partial(last_kernel, toks, per_z), out_shape=jax...]
    all_to_all x1, waiting for transfers between devices: 16.3 us -> 13.8 us  [local(): column = lax.all_to_all(copies, 'z', 0, 0, tiled=True).reshape(mine, width)]
  transfers between devices with their start and end apart: 7 -> 6, of which waited for: 4 -> 1; matrix products, arithmetic and copies ran while one was open for 9% -> 6% of each run, Pallas kernels for 0% -> 1%
where the time goes in v3:
time: 193 us; the launch traced here: 192 us
  blocking collectives  118 us (61%)
  starting transfers between devices  24.6 us (13%)
  waiting for transfers between devices  14.6 us (8%)
  between operations  13.4 us (7%)
  local copies, waits for them, and re-layouts  6.84 us (4%)
  other arithmetic  6.52 us (3%)
  matrix products  4.31 us (2%)
  Pallas kernels  3.86 us (2%)
    all_gather x2, blocking collectives, local(): parts = lax.all_gather(parts, NARROW, axis=0, tiled=False)  32.7 us
    all_to_all x1, blocking collectives, local(): block = lax.all_to_all(block, 'z', 0, 0, tiled=True)  26.2 us
    all_to_all x1, blocking collectives, local(): mixed = lax.all_to_all(mixed, 'z', 0, 0, tiled=True)  20.9 us
    all_to_all x1, starting transfers between devices, local(): column = lax.all_to_all(copies, 'z', 0, 0, tiled=True).reshape(mine, width)  15.2 us
    all_gather x1, blocking collectives, local(): flat = lax.all_gather(column, 'y', axis=0, tiled=True)  14.3 us
    all_to_all x1, waiting for transfers between devices, local(): column = lax.all_to_all(copies, 'z', 0, 0, tiled=True).reshape(mine, width)  13.8 us
    all_gather x1, blocking collectives, local(): hidden = lax.all_gather(hidden, NARROW, axis=0, tiled=True)  13.1 us
    all_gather x1, blocking collectives, local(): sums = lax.all_gather(sums, NARROW, axis=0, tiled=True).sum(0)  10.5 us
  transfers between devices with their start and end apart: 6, of which 1 were waited for; matrix products, arithmetic and copies ran while one was open for 6% of the time, Pallas kernels for 1%

profile of v3, /device:TPU:32, one launch (start us, length us, event | category | flops | bytes accessed | tf_op | source)
XLA Modules:
  0.0 191.8 jit_solution(7259602847761309298)
XLA Ops:
  6.5 1.8 pad_maximum_fusion.1
  8.4 0.7 reshape.262
  9.1 0.8 convert_reduce_fusion.1
  10.1 10.5 %all-gather.4 = f32[8,1,128]{2,1,0:T(1,128)S(1)} all-gather(f32[1,1,128]{2,1,0:T(1,128)S(1)} %fusion.18), channel_id=2, replica_groups=mesh['z'=16,'y'=4,'x'=4,'core'=2] {'x','core'}, dimensions={0}, use_global_device_ids=true | all-gather | bytes 4608 | tf_op jit(solution)/shard_map/all_gather | solution.py:162
  21.0 0.8 fusion.9
  22.5 15.2 %all-to-all-start = ((bf16[16,48,128]{2,1,0:T(8,128)(2,1)}), bf16[16,48,128]{2,1,0:T(8,128)(2,1)S(1)}, u32[]{:S(2)}, u32[]{:S(2)}) async-start(bf16[16,48,128]{2,1,0:T(8,128)(2,1)} %broadcast_in_dim.59), calls=%async_computation | async-start | bytes 393216 | tf_op jit(solution)/shard_map/all_to_all | solution.py:175
  38.5 1.8 pad_maximum_fusion
  40.3 13.8 %all-to-all-done = bf16[16,48,128]{2,1,0:T(8,128)(2,1)S(1)} async-done(((bf16[16,48,128]{2,1,0:T(8,128)(2,1)}), bf16[16,48,128]{2,1,0:T(8,128)(2,1)S(1)}, u32[]{:S(2)}, u32[]{:S(2)}) %all-to-all-start) | async-done | bytes 196640 | tf_op jit(solution)/shard_map/all_to_all | solution.py:175
  54.2 14.3 %all_gather.31 = bf16[384,1024]{1,0:T(8,128)(2,1)S(1)} all-gather(bf16[96,1024]{1,0:T(8,128)(2,1)S(1)} %reshape.247.column_ref), channel_id=1, replica_groups=mesh['z'=16,'y'=4,'x'=4,'core'=2] {'y'}, dimensions={0}, use_global_device_ids=true | all-gather | bytes 983040 | tf_op jit(solution)/shard_map/all_gather | solution.py:177
  68.5 1.9 convolution_convert_fusion.1
  70.4 3.5 %all-to-all-start.1 = ((bf16[8,48,1024]{2,1,0:T(8,128)(2,1)}), bf16[8,48,1024]{2,1,0:T(8,128)(2,1)S(1)}, u32[]{:S(2)}, u32[]{:S(2)}) async-start(bf16[8,48,1024]{2,1,0:T(8,128)(2,1)} %bitcast.49), calls=%async_computation.1 | async-start | bytes 1572864 | tf_op jit(solution)/shard_map/all_to_all | solution.py:180
  74.0 1.3 copy-done.1
  75.3 1.4 first.1
  76.7 19.1 %all-gather.2 = bf16[896,512]{1,0:T(8,128)(2,1)S(1)} all-gather(bf16[112,512]{1,0:T(8,128)(2,1)S(1)} %first.1), channel_id=4, replica_groups=mesh['z'=16,'y'=4,'x'=4,'core'=2] {'x','core'}, dimensions={0}, use_global_device_ids=true | all-gather | bytes 1032192 | tf_op jit(solution)/shard_map/all_gather | solution.py:192
  95.8 1.1 second.1
  96.8 5.8 %all-to-all-start.2 = ((bf16[16,8,512]{2,1,0:T(8,128)(2,1)}), bf16[16,8,512]{2,1,0:T(8,128)(2,1)S(1)}, u32[]{:S(2)}, u32[]{:S(2)}) async-start(bf16[16,8,512]{2,1,0:T(8,128)(2,1)} %bitcast.10), calls=%async_computation.2 | async-start | bytes 262144 | tf_op jit(solution)/shard_map/all_to_all | solution.py:205
  102.8 13.1 %all_gather.39 = bf16[384,512]{1,0:T(8,128)(2,1)S(1)} all-gather(bf16[48,512]{1,0:T(8,128)(2,1)S(1)} %get-tuple-element.12), channel_id=1, replica_groups=mesh['z'=16,'y'=4,'x'=4,'core'=2] {'x','core'}, dimensions={0}, use_global_device_ids=true | all-gather | bytes 442368 | tf_op jit(solution)/shard_map/all_gather | solution.py:253
  115.9 1.5 convolution_convert_fusion
  120.0 26.2 %all_to_all.25 = bf16[16,8,512]{2,1,0:T(8,128)(2,1)S(1)} all-to-all(bf16[16,8,512]{2,1,0:T(8,128)(2,1)S(1)} %copy.53), channel_id=1, replica_groups=mesh['z'=16,'y'=4,'x'=4,'core'=2] {'z'}, dimensions={0} | all-to-all | bytes 262144 | tf_op jit(solution)/shard_map/all_to_all | solution.py:250
  146.4 13.6 %all-gather.3 = bf16[896,512]{1,0:T(8,128)(2,1)S(1)} all-gather(bf16[112,512]{1,0:T(8,128)(2,1)S(1)} %pad_maximum_fusion.2), channel_id=5, replica_groups=mesh['z'=16,'y'=4,'x'=4,'core'=2] {'x','core'}, dimensions={0}, use_global_device_ids=true | all-gather | bytes 1032192 | tf_op jit(solution)/shard_map/all_gather | solution.py:252
  160.0 1.2 copy-done.2
  161.2 0.9 copy-done.3
  162.1 1.4 last.1
  163.7 20.9 %all_to_all.26 = bf16[16,48,128]{2,1,0:T(8,128)(2,1)S(1)} all-to-all(bf16[16,48,128]{2,1,0:T(8,128)(2,1)S(1)} %reshape.260), channel_id=1, replica_groups=mesh['z'=16,'y'=4,'x'=4,'core'=2] {'z'}, dimensions={0} | all-to-all | bytes 393216 | tf_op jit(solution)/shard_map/all_to_all | solution.py:270
  (82 shorter events, 5.8 us)
Async XLA Ops:
  6.5 109.3 %copy-start = (bf16[512,1024]{1,0:T(8,128)(2,1)S(1)}, bf16[512,1024]{1,0:T(8,128)(2,1)}, u32[]{:S(2)}) copy-start(bf16[512,1024]{1,0:T(8,128)(2,1)} %param.19) | copy-start | bytes 3145732
  6.5 67.5 %all-gather.10.cloned.1.call-start = ((), (), s32[]{:S(2)}) async-start(), calls=%async_computation.8 | async-start | bytes 1392640 | tf_op jit(solution)/shard_map/all_gather | solution.py:169
  22.5 31.6 %all-to-all-start = ((bf16[16,48,128]{2,1,0:T(8,128)(2,1)}), bf16[16,48,128]{2,1,0:T(8,128)(2,1)S(1)}, u32[]{:S(2)}, u32[]{:S(2)}) async-start(bf16[16,48,128]{2,1,0:T(8,128)(2,1)} %broadcast_in_dim.59), calls=%async_computation | async-start | bytes 393216 | tf_op jit(solution)/shard_map/all_to_all | solution.py:175
  37.7 122.3 %all-gather.8.cloned.1.call-start = ((), (), s32[]{:S(2)}) async-start(), calls=%async_computation.6 | async-start | bytes 1310720 | tf_op jit(solution)/shard_map/all_gather | solution.py:170
  68.5 5.5 %copy-start.7 = (s32[3]{0:T(128)S(1)}, s32[3]{0:T(128)}, u32[]{:S(2)}) copy-start(s32[3]{0:T(128)} %param.22) | copy-start | bytes 40
  70.4 25.4 %all-to-all-start.1 = ((bf16[8,48,1024]{2,1,0:T(8,128)(2,1)}), bf16[8,48,1024]{2,1,0:T(8,128)(2,1)S(1)}, u32[]{:S(2)}, u32[]{:S(2)}) async-start(bf16[8,48,1024]{2,1,0:T(8,128)(2,1)} %bitcast.49), calls=%async_computation.1 | async-start | bytes 1572864 | tf_op jit(solution)/shard_map/all_to_all | solution.py:180
  74.0 1.3 copy-start.1
  75.3 27.4 %copy-start.8 = (pred[1,64,2]{1,2,0:T(4,128)(4,1)S(1)}, pred[1,64,2]{1,2,0:T(4,128)(4,1)}, u32[]{:S(2)}) copy-start(pred[1,64,2]{1,2,0:T(4,128)(4,1)} %constant.35.clone) | copy-start | bytes 388
  96.8 20.5 %all-to-all-start.2 = ((bf16[16,8,512]{2,1,0:T(8,128)(2,1)}), bf16[16,8,512]{2,1,0:T(8,128)(2,1)S(1)}, u32[]{:S(2)}, u32[]{:S(2)}) async-start(bf16[16,8,512]{2,1,0:T(8,128)(2,1)} %bitcast.10), calls=%async_computation.2 | async-start | bytes 262144 | tf_op jit(solution)/shard_map/all_to_all | solution.py:205
  102.6 57.4 %reduce-scatter.2.cloned.1.call-start = ((), (), s32[]{:S(2)}) async-start(), calls=%async_computation.7 | async-start | bytes 983040 | tf_op jit(solution)/shard_map/reduce_scatter | solution.py:255
  102.8 15.2 %copy-start.5 = (bf16[3,256,256]{2,1,0:T(8,128)(2,1)S(1)}, bf16[3,256,256]{2,1,0:T(8,128)(2,1)}, u32[]{:S(2)}) copy-start(bf16[3,256,256]{2,1,0:T(8,128)(2,1)} %param.20) | copy-start | bytes 1179652
  115.9 3.0 %copy-start.4 = (bf16[3,256,256]{2,1,0:T(8,128)(2,1)S(1)}, bf16[3,256,256]{2,1,0:T(8,128)(2,1)}, u32[]{:S(2)}) copy-start(bf16[3,256,256]{2,1,0:T(8,128)(2,1)} %param.21) | copy-start | bytes 1179652
  146.3 38.3 %copy-start.6 = (bf16[3,2,1024]{2,1,0:T(2,128)(2,1)S(1)}, bf16[3,2,1024]{2,1,0:T(2,128)(2,1)}, u32[]{:S(2)}) copy-start(bf16[3,2,1024]{2,1,0:T(2,128)(2,1)} %param.12) | copy-start | bytes 36868
  160.0 1.2 copy-start.2
  161.2 0.9 copy-start.3
Sparse Core Ops, SparseCore 0:
  9.5 35.9 all-gather.9
  47.6 32.3 all-gather.7
  117.5 28.8 reduce-scatter.1

commit v4 on v3

--- a/solution.py
+++ b/solution.py
@@ -15,7 +15,8 @@
 bf16 = jnp.bfloat16
 f32 = jnp.float32
 vmem = pl.BlockSpec(memory_space=pltpu.VMEM)
-anywhere = pl.BlockSpec(memory_space=pl.ANY)
+hbm = pl.BlockSpec(memory_space=pltpu.HBM)
+smem = pl.BlockSpec(memory_space=pltpu.SMEM)
 WIDE = ("z", "y")
 NARROW = ("x", "core")
 
@@ -31,65 +32,208 @@
     return lax.broadcasted_iota(jnp.int32, shape, axis)
 
 
-def first_kernel(toks, column_ref, source_ref, parts_ref, weights_ref, sems):
+def parts_of(value, count):
+    found = []
+    for _ in range(count):
+        found.append(value.astype(bf16).astype(f32))
+        value = value - found[-1]
+    return found
+
+
+def gain_rows(gain_ref):
+    shape = (8, gain_ref.shape[1])
+    rows = jnp.zeros(shape, f32)
+    for k, part in enumerate(parts_of(gain_ref[...], 3)):
+        rows = jnp.where(iota(shape, 0) == k, part, rows)
+    return rows.astype(bf16)
+
+
+def centred(tokens_ref, gain_ref):
+    width = tokens_ref.shape[1]
+    tokens = tokens_ref[...]
+    mean = tokens.astype(f32).sum(1, keepdims=True) * (1.0 / width)
+    return ((tokens.astype(f32) - mean) * gain_ref[...]).astype(bf16)
+
+
+def across(left, right):
+    return lax.dot_general(left, right, (((1,), (1,)), ((), ())), preferred_element_type=f32)
+
+
+def hidden_kernel(tokens_ref, gain_ref, gate_ref, up_ref, sums_ref, notes_ref):
+    ffn = gate_ref.shape[1]
+    count, width = tokens_ref.shape
+    ready = centred(tokens_ref, gain_ref)
+    gains = gain_rows(gain_ref)
+    sums_ref[:, :ffn] = jnp.dot(ready, gate_ref[...], preferred_element_type=f32).astype(bf16)
+    sums_ref[:, ffn:] = jnp.dot(ready, up_ref[...], preferred_element_type=f32).astype(bf16)
+    tokens = tokens_ref[...].astype(f32)
+    notes_ref[...] = jnp.zeros_like(notes_ref)
+    for k, values in enumerate((tokens, tokens * tokens)):
+        total = jnp.broadcast_to(values.sum(1, keepdims=True), (count, 128))
+        for j in range(0, count, 128):
+            notes_ref[k : k + 1, j : j + 128] = total[j : j + 128].T[0:1]
+    for k, ref in enumerate((gate_ref, up_ref)):
+        product = jnp.dot(gains, ref[...], preferred_element_type=f32)
+        notes_ref[2:3, k * ffn : (k + 1) * ffn] = product.sum(0, keepdims=True)
+
+
+def first_kernel(toks, column_ref, gain_ref, notes_ref, source_ref, parts_ref, weights_ref, sems):
     mine, width = column_ref.shape
     ys, _, lanes = weights_ref.shape
     cols = ys * lanes
+    half = cols // 2
+    zs = mine // toks
     chunks = width // lanes
     copies = [pltpu.make_async_copy(source_ref.at[k], weights_ref.at[k], sems.at[k]) for k in range(ys)]
     for copy in copies:
         copy.start()
-    column = column_ref[...]
-    pairs = []
+    column = centred(column_ref, gain_ref)
+    gains = gain_rows(gain_ref)
+    pairs, products = [], []
     for k in range(ys):
         copies[k].wait()
         query = jnp.dot(column, weights_ref[k, :width], preferred_element_type=f32)
         parts_ref[:mine, k * lanes : (k + 1) * lanes] = query.astype(bf16)
+        products.append(jnp.dot(gains, weights_ref[k, :width], preferred_element_type=f32))
         rows = weights_ref[k, width:].astype(f32)
         count = rows.shape[0] // chunks
         pairs.append(jnp.concatenate([rows[j * count : (j + 1) * count] for j in range(chunks)], axis=1))
-    pairs = jnp.concatenate(pairs, axis=0).astype(bf16)
+    pairs = jnp.concatenate(pairs, axis=0)
     count = pairs.shape[0]
-    pairs = lax.dot_general(column, pairs, (((1,), (1,)), ((), ())), preferred_element_type=f32).astype(bf16)
-    at = iota((count, cols), 1)
-    spread = jnp.where((lax.rem(at, count) == iota((count, cols), 0)) & (at < toks * count), 1.0, 0.0)
+    pairs = jnp.concatenate([pairs, jnp.zeros((128 - count, width), f32)], axis=0).astype(bf16)
+    pair_products = across(gains, pairs).sum(0, keepdims=True)
+    pairs = across(column, pairs).astype(bf16)
+    at = iota((128, half), 1)
+    spread = jnp.where((lax.rem(at, count) == iota((128, half), 0)) & (at < toks * count), 1.0, 0.0)
     pairs = jnp.dot(pairs, spread.astype(bf16), preferred_element_type=f32)
-    start = lax.rem(iota((mine, cols), 0), toks) * count
-    at = iota((mine, cols), 1)
+    start = lax.rem(iota((mine, half), 0), toks) * count
+    at = iota((mine, half), 1)
     pairs = jnp.where((at >= start) & (at < start + count), pairs, 0.0).astype(bf16)
-    start = iota((mine // toks, mine), 0) * toks
-    at = iota((mine // toks, mine), 1)
+    start = iota((zs, mine), 0) * toks
+    at = iota((zs, mine), 1)
     collect = jnp.where((at >= start) & (at < start + toks), 1.0, 0.0).astype(bf16)
-    parts_ref[mine:] = jnp.dot(collect, pairs, preferred_element_type=f32).astype(bf16)
-
-
-def second_kernel(toks, gate_up_ref, parts_ref, hidden_ref, block_ref):
+    pairs = jnp.dot(collect, pairs, preferred_element_type=f32)
+
+    row = iota((zs, half), 0)
+    beside = jnp.zeros((zs, half), f32)
+    for j in range(4):
+        high, low = parts_of(notes_ref[2:3, j * half : (j + 1) * half], 2)
+        beside = jnp.where(row == j, high, jnp.where(row == 4 + j, low, beside))
+    parts_ref[mine : mine + zs] = jnp.concatenate([pairs, beside], axis=1).astype(bf16)
+
+    row = iota((8, cols), 0)
+    tail = jnp.zeros((8, cols), f32)
+    for k, part in enumerate(parts_of(notes_ref[0:1, :cols], 3) + parts_of(notes_ref[1:2, :cols], 3)):
+        tail = jnp.where(row == k, part, tail)
+    products = jnp.concatenate(products, axis=1).sum(0, keepdims=True)
+    for k, part in enumerate(parts_of(products, 2)):
+        tail = jnp.where(row == 6 + k, part, tail)
+    pair_products = jnp.concatenate([jnp.zeros((1, cols - 128), f32), pair_products], axis=1)
+    for k, part in enumerate(parts_of(pair_products, 2)):
+        tail = jnp.where((row == k) & (iota((8, cols), 1) >= cols - 128), part, tail)
+    parts_ref[mine + zs :] = tail.astype(bf16)
+
+
+def second_kernel(toks, where_ref, sums_ref, parts_ref, hidden_ref, block_ref):
     ns, rows, cols = parts_ref.shape
     ffn = hidden_ref.shape[1]
-    gate = gate_up_ref[0, :, :ffn].astype(f32)
-    up = gate_up_ref[0, :, ffn:].astype(f32)
-    total = parts_ref[0].astype(f32)
+    half = cols // 2
+    zs = block_ref.shape[0] // 8
+    mine = zs * toks
+    width = 2 * ffn
+    tails = jnp.concatenate([parts_ref[n, mine + zs :].astype(f32) for n in range(ns)], axis=0).astype(bf16)
+    besides = jnp.concatenate([parts_ref[n, mine : mine + zs, half:] for n in range(ns)], axis=0)
+    every = cols - 128
+
+    def pick(shape, group, mask):
+        frm, to = iota(shape, 0), iota(shape, 1)
+        kind = frm & 7
+        same = lax.shift_right_logical(frm, 3) == lax.shift_right_logical(to, group)
+        return jnp.where(same & (kind < 3) & mask(to), 1.0, 0.0).astype(bf16)
+
+    def norm(first, count):
+        shape = (count, every)
+        select = jnp.where(iota(shape, 1) == iota(shape, 0) + first, 1.0, 0.0).astype(bf16)
+        own = across(select, tails[:, :every]).astype(bf16)
+        kind = iota((ns * 8, 128), 0) & 7
+        total = jnp.dot(own, jnp.where(kind < 3, 1.0, 0.0).astype(bf16), preferred_element_type=f32)
+        centre = total * (1.0 / D)
+        total = jnp.dot(
+            own, jnp.where((kind >= 3) & (kind < 6), 1.0, 0.0).astype(bf16), preferred_element_type=f32
+        )
+        spread = total * (1.0 / D) - centre * centre
+        return own, centre, lax.rsqrt(spread + eps_norm)
+
+    def shift(own, centre, group, mask, table):
+        shape = (ns * 8, table.shape[0])
+        means = jnp.dot(own, pick(shape, group, mask), preferred_element_type=f32) * (1.0 / width)
+        shape = (own.shape[0], table.shape[0])
+        means = jnp.where(mask(iota(shape, 1)), means - centre[:, : shape[1]], 0.0)
+        high, low = parts_of(means, 2)
+        return jnp.dot(high.astype(bf16), table, preferred_element_type=f32) + jnp.dot(
+            low.astype(bf16), table, preferred_element_type=f32
+        )
+
+    count = hidden_ref.shape[0]
+    own, centre, scale = norm(where_ref[1] * count, count)
+    scale = jnp.concatenate([scale] * (half // 128), axis=1)
+    for j in range(2):
+        both = []
+        for k in (j, j + 2):
+            at = slice(k * half, (k + 1) * half)
+            total = sums_ref[0, :, at].astype(f32)
+            for n in range(1, ns):
+                total = total + sums_ref[n, :, at].astype(f32)
+            total = total + shift(
+                own, centre, 4, lambda to, k=k: ((to & 15) == k) | ((to & 15) == k + 4), besides
+            )
+            both.append(total * scale)
+        gate, up = both
+        hidden_ref[:, j * half : (j + 1) * half] = (gate / (1.0 + jnp.exp(-gate)) * up).astype(bf16)
+
+    total = parts_ref[0, : mine + zs].astype(f32)
     for n in range(1, ns):
-        gate = gate + gate_up_ref[n, :, :ffn].astype(f32)
-        up = up + gate_up_ref[n, :, ffn:].astype(f32)
-        total = total + parts_ref[n].astype(f32)
-    hidden_ref[...] = (gate / (1.0 + jnp.exp(-gate)) * up).astype(bf16)
-    shape = (block_ref.shape[0], rows)
-    zs = shape[0] // 8
+        total = total + parts_ref[n, : mine + zs].astype(f32)
+    own, centre, scale = norm(where_ref[0] * mine, mine)
+    query = total[:mine] + shift(own, centre, 3, lambda to: (to & 7) >= 6, tails)
+    query = (query * jnp.concatenate([scale] * (cols // 128), axis=1)).astype(bf16)
+    start = iota((mine, zs), 1) * toks
+    at = iota((mine, zs), 0)
+    expand = jnp.where((at >= start) & (at < start + toks), 1.0, 0.0).astype(bf16)
+    pairs = jnp.zeros((mine, half), f32)
+    for part in parts_of(total[mine:, :half], 3):
+        pairs = pairs + jnp.dot(expand, part.astype(bf16), preferred_element_type=f32)
+    pair_cols = 2 * cols // zs // 2
+    at = iota((128, half), 1)
+    spread = jnp.where((lax.rem(at, pair_cols) == iota((128, half), 0)) & (at < toks * pair_cols), 1.0, 0.0)
+    shifted = shift(own, centre, 3, lambda to: (to & 7) < 2, tails[:, every:])
+    for part in parts_of(shifted, 3):
+        pairs = pairs + jnp.dot(part.astype(bf16), spread.astype(bf16), preferred_element_type=f32)
+    pairs = pairs * jnp.concatenate([scale] * (half // 128), axis=1)
+    start = lax.rem(iota((mine, half), 0), toks) * pair_cols
+    at = iota((mine, half), 1)
+    pairs = jnp.where((at >= start) & (at < start + pair_cols), pairs, 0.0).astype(bf16)
+    shape = (zs * 8, mine)
     to, at = iota(shape, 0), iota(shape, 1)
-    row = lax.rem(to, 8)
-    z = (to - row) // 8
-    take = ((row < toks) & (at == z * toks + row)) | ((row == toks) & (at == zs * toks + z))
-    take = jnp.where(take, 1.0, 0.0).astype(bf16)
-    block_ref[...] = jnp.dot(take, total.astype(bf16), preferred_element_type=f32).astype(bf16)
-
-
-def last_kernel(toks, per_z, parts_ref, source_ref, down_ref, mixed_ref, weights_ref, sem):
+    row = to & 7
+    start = lax.shift_right_logical(to, 3) * toks
+    take = jnp.where((row < toks) & (at == start + row), 1.0, 0.0).astype(bf16)
+    block_ref[...] = jnp.dot(take, query, preferred_element_type=f32).astype(bf16)
+    take = jnp.where((row == toks) & (at >= start) & (at < start + toks), 1.0, 0.0).astype(bf16)
+    pairs = jnp.dot(take, pairs, preferred_element_type=f32)
+    block_ref[:, :half] = (block_ref[:, :half].astype(f32) + pairs).astype(bf16)
+
+
+def last_kernel(toks, per_z, parts_ref, source_ref, down_source_ref, mixed_ref, weights_ref, down_ref, sems):
     ns, rows, cols = parts_ref.shape
     mine = mixed_ref.shape[0]
     zs = rows - mine
-    copy = pltpu.make_async_copy(source_ref, weights_ref, sem)
-    copy.start()
+    copies = [
+        pltpu.make_async_copy(source_ref, weights_ref, sems.at[0]),
+        pltpu.make_async_copy(down_source_ref, down_ref, sems.at[1]),
+    ]
+    for copy in copies:
+        copy.start()
     head = cols // per_z
     shape = (ns * mine, ns * zs)
     start = iota(shape, 1) * toks
@@ -101,7 +245,7 @@
     at = iota((128, 128), 0)
     pick_top = jnp.where(at < 24, 1.0, 0.0).astype(bf16)
     pick_total = jnp.where((at >= 24) & (at < 48), 1.0, 0.0).astype(bf16)
-    mixed = down_ref[...].astype(f32)
+    mixed = None
     for k in range(per_z):
         marks = jnp.concatenate([parts_ref[n, mine:, k * head : k * head + 128] for n in range(ns)], axis=0)
         marks = jnp.dot(expand, marks, preferred_element_type=f32)
@@ -121,8 +265,10 @@
             weighted = weighted + parts_ref[n, :mine, k * head : (k + 1) * head].astype(f32) * scale
         total = jnp.concatenate([total] * (head // 128), axis=1)
         attended = (weighted / total).astype(bf16)
-        if k == 0:
-            copy.wait()
+        if mixed is None:
+            for copy in copies:
+                copy.wait()
+            mixed = down_ref[...].astype(f32)
         mixed = mixed + jnp.dot(
             attended, weights_ref[k * head : (k + 1) * head], preferred_element_type=f32
         )
@@ -157,51 +303,55 @@
     ffn = w_gate.shape[1]
 
     values = activations.reshape(toks, width).astype(f32)
-    sums = jnp.concatenate([values.sum(-1), (values * values).sum(-1)])
-    sums = jnp.pad(sums, (0, 128 - 2 * toks))[None]
-    sums = lax.all_gather(sums, NARROW, axis=0, tiled=True).sum(0)
-    centre = sums[:toks, None] / D
-    spread = sums[toks : 2 * toks, None] / D - centre * centre
-    normed = ((values - centre) * lax.rsqrt(spread + eps_norm) * norm_gain).astype(bf16)
+    gain = norm_gain.reshape(1, width)
 
     chunks = width // lanes
     pair_lanes = w_keyval.T.reshape(kv_cols, chunks, lanes).transpose(1, 0, 2).reshape(chunks * kv_cols, lanes)
     w_first = lax.all_gather(jnp.concatenate([w_query, pair_lanes], axis=0), "y", axis=0, tiled=False)
     w_last = lax.all_gather(w_out, "y", axis=0, tiled=True)
-    w_hidden = lax.optimization_barrier(jnp.concatenate([w_gate, w_up], axis=1))
-
-    packed = normed.reshape(toks * width // 128, 128)
+
+    packed = activations.reshape(toks * width // 128, 128)
     copies = jnp.broadcast_to(packed[None], (zs,) + packed.shape)
     column = lax.all_to_all(copies, "z", 0, 0, tiled=True).reshape(mine, width)
 
     flat = lax.all_gather(column, "y", axis=0, tiled=True)
-    gate_up = jnp.dot(flat, w_hidden, preferred_element_type=f32).astype(bf16)
-    column, gate_up = lax.optimization_barrier((column, gate_up))
-    gate_up = lax.all_to_all(gate_up.reshape(ns, -1, 2 * ffn), NARROW, 0, 0, tiled=True)
+    sums, notes = pl.pallas_call(
+        hidden_kernel,
+        out_shape=(
+            jax.ShapeDtypeStruct((ys * mine, 2 * ffn), bf16),
+            jax.ShapeDtypeStruct((8, 2 * ffn), f32),
+        ),
+        in_specs=[vmem] * 4,
+        out_specs=(vmem, vmem),
+        compiler_params=pltpu.CompilerParams(vmem_limit_bytes=40 * 2**20),
+        cost_estimate=pl.CostEstimate(flops=2**30, bytes_accessed=4 * 2**20, transcendentals=0),
+        name="hidden",
+    )(flat, gain, w_gate, w_up)
+    sums = lax.all_to_all(sums.reshape(ns, -1, 2 * ffn), NARROW, 0, 0, tiled=True)
 
     parts = pl.pallas_call(
         functools.partial(first_kernel, toks),
-        out_shape=jax.ShapeDtypeStruct((mine + zs, cols), bf16),
-        in_specs=[vmem, anywhere],
+        out_shape=jax.ShapeDtypeStruct((mine + zs + 8, cols), bf16),
+        in_specs=[vmem, vmem, vmem, hbm],
         out_specs=vmem,
         scratch_shapes=[pltpu.VMEM(w_first.shape, bf16), pltpu.SemaphoreType.DMA((ys,))],
         compiler_params=pltpu.CompilerParams(vmem_limit_bytes=24 * 2**20),
         cost_estimate=pl.CostEstimate(flops=2 * mine * width * cols, bytes_accessed=2 * 2**20, transcendentals=0),
         name="first",
-    )(column, w_first)
+    )(column, gain, notes, w_first)
     parts = lax.all_gather(parts, NARROW, axis=0, tiled=False)
     hidden, block = pl.pallas_call(
         functools.partial(second_kernel, toks),
         out_shape=(
-            jax.ShapeDtypeStruct((gate_up.shape[1], ffn), bf16),
+            jax.ShapeDtypeStruct((sums.shape[1], ffn), bf16),
             jax.ShapeDtypeStruct((zs * 8, cols), bf16),
         ),
-        in_specs=[vmem, vmem],
+        in_specs=[smem, vmem, vmem],
         out_specs=(vmem, vmem),
         compiler_params=pltpu.CompilerParams(vmem_limit_bytes=24 * 2**20),
         cost_estimate=pl.CostEstimate(flops=2**24, bytes_accessed=2 * 2**20, transcendentals=0),
         name="second",
-    )(gate_up, parts)
+    )(jnp.stack([lax.axis_index("y"), lax.axis_index(NARROW)]).astype(jnp.int32), sums, parts)
     block = lax.all_to_all(block.reshape(zs, 8, cols), "z", 0, 0, tiled=True)
 
     queries = (
@@ -257,9 +407,13 @@
     mixed = pl.pallas_call(
         functools.partial(last_kernel, toks, per_z),
         out_shape=jax.ShapeDtypeStruct((mine, width), bf16),
-        in_specs=[vmem, anywhere, vmem],
+        in_specs=[vmem, hbm, hbm],
         out_specs=vmem,
-        scratch_shapes=[pltpu.VMEM(w_last.shape, bf16), pltpu.SemaphoreType.DMA],
+        scratch_shapes=[
+            pltpu.VMEM(w_last.shape, bf16),
+            pltpu.VMEM((mine, width), bf16),
+            pltpu.SemaphoreType.DMA((2,)),
+        ],
         compiler_params=pltpu.CompilerParams(vmem_limit_bytes=24 * 2**20),
         cost_estimate=pl.CostEstimate(
             flops=2 * mine * width * cols, bytes_accessed=3 * 2**20, transcendentals=0

time: 193 us -> 187 us (0.969)
  blocking collectives: 118 us -> 106 us
  starting transfers between devices: 24.6 us -> 29.2 us
  Pallas kernels: 3.86 us -> 8.03 us
  other arithmetic: 6.52 us -> 3.02 us
    all_gather x1 -> x0, blocking collectives: 10.5 us -> none  [local(): sums = lax.all_gather(sums, NARROW, axis=0, tiled=True).sum(0)]
    all_to_all x1, starting transfers between devices: 5.78 us -> 9.49 us  [local(): block = lax.all_to_all(block.reshape(zs, 8, cols), 'z', 0, 0, tiled=True)]
    pallas_call x0 -> x1, Pallas kernels: none -> 2.13 us  [local(): pl.pallas_call(hidden_kernel, out_shape=(jax.ShapeDtypeStruct((ys * mine,...]
  transfers between devices with their start and end apart: 6 -> 6, of which waited for: 1 -> 1; matrix products, arithmetic and copies ran while one was open for 6% -> 4% of each run, Pallas kernels for 1% -> 3%
where the time goes in v4:
time: 187 us; the launch traced here: 186 us
  blocking collectives  106 us (57%)
  starting transfers between devices  29.2 us (16%)
  waiting for transfers between devices  15.9 us (9%)
  between operations  13.4 us (7%)
  Pallas kernels  8.03 us (4%)
  local copies, waits for them, and re-layouts  7.66 us (4%)
  other arithmetic  3.02 us (2%)
  matrix products  2.43 us (1%)
    all_gather x2, blocking collectives, local(): parts = lax.all_gather(parts, NARROW, axis=0, tiled=False)  32.3 us
    all_to_all x1, blocking collectives, local(): block = lax.all_to_all(block, 'z', 0, 0, tiled=True)  26.2 us
    all_to_all x1, blocking collectives, local(): mixed = lax.all_to_all(mixed, 'z', 0, 0, tiled=True)  20.9 us
    all_to_all x1, starting transfers between devices, local(): column = lax.all_to_all(copies, 'z', 0, 0, tiled=True).reshape(mine, width)  15.2 us
    all_to_all x1, waiting for transfers between devices, local(): column = lax.all_to_all(copies, 'z', 0, 0, tiled=True).reshape(mine, width)  15.2 us
    all_gather x1, blocking collectives, local(): flat = lax.all_gather(column, 'y', axis=0, tiled=True)  14 us
    all_gather x1, blocking collectives, local(): hidden = lax.all_gather(hidden, NARROW, axis=0, tiled=True)  13 us
    all_to_all x1, starting transfers between devices, local(): block = lax.all_to_all(block.reshape(zs, 8, cols), 'z', 0, 0, tiled=True)  9.49 us
  transfers between devices with their start and end apart: 6, of which 1 were waited for; matrix products, arithmetic and copies ran while one was open for 4% of the time, Pallas kernels for 3%

profile of v4, /device:TPU:32, one launch (start us, length us, event | category | flops | bytes accessed | tf_op | source)
XLA Modules:
  0.0 186.0 jit_solution(2532920444181335333)
XLA Ops:
  6.5 1.8 pad_maximum_fusion
  8.4 0.7 broadcast_in_dim.54
  9.1 0.7 broadcast_in_dim.55
  9.9 15.2 %all-to-all-start = ((bf16[16,48,128]{2,1,0:T(8,128)(2,1)}), bf16[16,48,128]{2,1,0:T(8,128)(2,1)}, u32[]{:S(2)}, u32[]{:S(2)}) async-start(bf16[16,48,128]{2,1,0:T(8,128)(2,1)} %broadcast_in_dim.55), calls=%async_computation | async-start | bytes 393216 | tf_op jit(solution)/shard_map/all_to_all | solution.py:315
  25.1 0.7 all-gather.6.cloned.1.call-update
  25.8 15.2 %all-to-all-done = bf16[16,48,128]{2,1,0:T(8,128)(2,1)} async-done(((bf16[16,48,128]{2,1,0:T(8,128)(2,1)}), bf16[16,48,128]{2,1,0:T(8,128)(2,1)}, u32[]{:S(2)}, u32[]{:S(2)}) %all-to-all-start) | async-done | bytes 196640 | tf_op jit(solution)/shard_map/all_to_all | solution.py:315
  41.0 1.0 reshape.197.column_ref
  42.0 14.0 %all_gather.27.tokens_ref = bf16[384,1024]{1,0:T(8,128)(2,1)S(1)} all-gather(bf16[96,1024]{1,0:T(8,128)(2,1)S(1)} %reshape.197.column_ref), channel_id=1, replica_groups=mesh['z'=16,'y'=4,'x'=4,'core'=2] {'y'}, dimensions={0}, use_global_device_ids=true | all-gather | bytes 983040 | tf_op jit(solution)/shard_map/all_gather | solution.py:317
  56.0 2.1 %hidden.1 = (bf16[384,1024]{1,0:T(8,128)(2,1)}, f32[8,1024]{1,0:T(8,128)S(1)}) custom-call(bf16[384,1024]{1,0:T(8,128)(2,1)S(1)} %all_gather.27.tokens_ref, f32[1,1024]{1,0:T(1,128)S(1)} %bitcast.43, bf16[1024,512]{1,0:T(8,128)(2,1)S(1)} %copy-done.5, bf16[1024,512]{1,0:T(8,128)(2,1)S(1)} %copy-done.6), custom_call_target="tpu_custom_call" | custom-call | flops 1073741824 | bytes 4194304 | tf_op jit(solution)/shard_map/hidden/pallas_call | solution.py:318
  58.1 4.4 %all-to-all-start.1 = ((bf16[8,48,1024]{2,1,0:T(8,128)(2,1)}), bf16[8,48,1024]{2,1,0:T(8,128)(2,1)S(1)}, u32[]{:S(2)}, u32[]{:S(2)}) async-start(bf16[8,48,1024]{2,1,0:T(8,128)(2,1)} %bitcast.3), calls=%async_computation.1 | async-start | bytes 1572864 | tf_op jit(solution)/shard_map/all_to_all | solution.py:330
  62.7 1.2 copy-done.1
  63.9 1.6 first.1
  65.5 18.7 %all-gather.1 = bf16[960,512]{1,0:T(8,128)(2,1)S(1)} all-gather(bf16[120,512]{1,0:T(8,128)(2,1)S(1)} %first.1), channel_id=3, replica_groups=mesh['z'=16,'y'=4,'x'=4,'core'=2] {'x','core'}, dimensions={0}, use_global_device_ids=true | all-gather | bytes 1105920 | tf_op jit(solution)/shard_map/all_gather | solution.py:342
  84.2 2.7 %second.1 = (bf16[48,512]{1,0:T(8,128)(2,1)S(1)}, bf16[128,512]{1,0:T(8,128)(2,1)}) custom-call(s32[2]{0:T(128)S(1)} %pad_add_fusion.where_ref, bf16[8,48,1024]{2,1,0:T(8,128)(2,1)S(1)} %all-to-all-done.1.sums_ref, bf16[8,120,512]{2,1,0:T(8,128)(2,1)S(1)} %bitcast.40), custom_call_target="tpu_custom_call" | custom-call | flops 16777216 | bytes 2097152 | tf_op jit(solution)/shard_map/second/pallas_call | solution.py:343
  86.9 9.5 %all-to-all-start.2 = ((bf16[16,8,512]{2,1,0:T(8,128)(2,1)}), bf16[16,8,512]{2,1,0:T(8,128)(2,1)S(1)}, u32[]{:S(2)}, u32[]{:S(2)}) async-start(bf16[16,8,512]{2,1,0:T(8,128)(2,1)} %bitcast.10), calls=%async_computation.2 | async-start | bytes 262144 | tf_op jit(solution)/shard_map/all_to_all | solution.py:355
  96.5 13.0 %all_gather.35 = bf16[384,512]{1,0:T(8,128)(2,1)S(1)} all-gather(bf16[48,512]{1,0:T(8,128)(2,1)S(1)} %get-tuple-element.12), channel_id=1, replica_groups=mesh['z'=16,'y'=4,'x'=4,'core'=2] {'x','core'}, dimensions={0}, use_global_device_ids=true | all-gather | bytes 442368 | tf_op jit(solution)/shard_map/all_gather | solution.py:403
  109.5 1.5 convolution_convert_fusion
  114.0 26.2 %all_to_all.25 = bf16[16,8,512]{2,1,0:T(8,128)(2,1)S(1)} all-to-all(bf16[16,8,512]{2,1,0:T(8,128)(2,1)S(1)} %copy.53), channel_id=1, replica_groups=mesh['z'=16,'y'=4,'x'=4,'core'=2] {'z'}, dimensions={0} | all-to-all | bytes 262144 | tf_op jit(solution)/shard_map/all_to_all | solution.py:400
  140.3 13.6 %all-gather.2 = bf16[896,512]{1,0:T(8,128)(2,1)S(1)} all-gather(bf16[112,512]{1,0:T(8,128)(2,1)S(1)} %pad_maximum_fusion.1), channel_id=4, replica_groups=mesh['z'=16,'y'=4,'x'=4,'core'=2] {'x','core'}, dimensions={0}, use_global_device_ids=true | all-gather | bytes 1032192 | tf_op jit(solution)/shard_map/all_gather | solution.py:402
  153.9 1.2 copy-done.2
  155.2 0.9 copy-done.3
  156.1 1.7 last.1
  157.8 20.9 %all_to_all.26 = bf16[16,48,128]{2,1,0:T(8,128)(2,1)S(1)} all-to-all(bf16[16,48,128]{2,1,0:T(8,128)(2,1)S(1)} %reshape.211), channel_id=1, replica_groups=mesh['z'=16,'y'=4,'x'=4,'core'=2] {'z'}, dimensions={0} | all-to-all | bytes 393216 | tf_op jit(solution)/shard_map/all_to_all | solution.py:424
  178.8 0.6 add_convert_fusion
  (76 shorter events, 3.5 us)
Async XLA Ops:
  6.5 102.9 %copy-start = (bf16[512,1024]{1,0:T(8,128)(2,1)S(1)}, bf16[512,1024]{1,0:T(8,128)(2,1)}, u32[]{:S(2)}) copy-start(bf16[512,1024]{1,0:T(8,128)(2,1)} %param.19) | copy-start | bytes 3145732
  6.5 56.1 %all-gather.8.cloned.1.call-start = ((), (), s32[]{:S(2)}) async-start(), calls=%async_computation.8 | async-start | bytes 1392640 | tf_op jit(solution)/shard_map/all_gather | solution.py:310
  9.1 46.9 %copy-start.4 = (f32[1024]{0:T(1024)S(1)}, f32[1024]{0:T(1024)}, u32[]{:S(2)}) copy-start(f32[1024]{0:T(1024)} %param.13) | copy-start | bytes 12292
  9.1 46.8 %copy-start.5 = (bf16[1024,512]{1,0:T(8,128)(2,1)S(1)}, bf16[1024,512]{1,0:T(8,128)(2,1)}, u32[]{:S(2)}) copy-start(bf16[1024,512]{1,0:T(8,128)(2,1)} %gate_ref.1) | copy-start | bytes 3145732
  9.1 46.8 %copy-start.6 = (bf16[1024,512]{1,0:T(8,128)(2,1)S(1)}, bf16[1024,512]{1,0:T(8,128)(2,1)}, u32[]{:S(2)}) copy-start(bf16[1024,512]{1,0:T(8,128)(2,1)} %up_ref.1) | copy-start | bytes 3145732
  9.9 31.1 %all-to-all-start = ((bf16[16,48,128]{2,1,0:T(8,128)(2,1)}), bf16[16,48,128]{2,1,0:T(8,128)(2,1)}, u32[]{:S(2)}, u32[]{:S(2)}) async-start(bf16[16,48,128]{2,1,0:T(8,128)(2,1)} %broadcast_in_dim.55), calls=%async_computation | async-start | bytes 393216 | tf_op jit(solution)/shard_map/all_to_all | solution.py:315
  25.1 128.9 %all-gather.6.cloned.1.call-start = ((), (), s32[]{:S(2)}) async-start(), calls=%async_computation.6 | async-start | bytes 1310720 | tf_op jit(solution)/shard_map/all_gather | solution.py:311
  58.1 4.5 %copy-start.10 = (s32[3]{0:T(128)S(1)}, s32[3]{0:T(128)}, u32[]{:S(2)}) copy-start(s32[3]{0:T(128)} %param.22) | copy-start | bytes 40
  58.1 26.1 %all-to-all-start.1 = ((bf16[8,48,1024]{2,1,0:T(8,128)(2,1)}), bf16[8,48,1024]{2,1,0:T(8,128)(2,1)S(1)}, u32[]{:S(2)}, u32[]{:S(2)}) async-start(bf16[8,48,1024]{2,1,0:T(8,128)(2,1)} %bitcast.3), calls=%async_computation.1 | async-start | bytes 1572864 | tf_op jit(solution)/shard_map/all_to_all | solution.py:330
  62.7 1.2 copy-start.1
  84.2 12.2 %copy-start.11 = (pred[1,64,2]{1,2,0:T(4,128)(4,1)S(1)}, pred[1,64,2]{1,2,0:T(4,128)(4,1)}, u32[]{:S(2)}) copy-start(pred[1,64,2]{1,2,0:T(4,128)(4,1)} %constant.31.clone) | copy-start | bytes 388
  86.9 24.1 %all-to-all-start.2 = ((bf16[16,8,512]{2,1,0:T(8,128)(2,1)}), bf16[16,8,512]{2,1,0:T(8,128)(2,1)S(1)}, u32[]{:S(2)}, u32[]{:S(2)}) async-start(bf16[16,8,512]{2,1,0:T(8,128)(2,1)} %bitcast.10), calls=%async_computation.2 | async-start | bytes 262144 | tf_op jit(solution)/shard_map/all_to_all | solution.py:355
  96.4 57.6 %reduce-scatter.2.cloned.1.call-start = ((), (), s32[]{:S(2)}) async-start(), calls=%async_computation.7 | async-start | bytes 983040 | tf_op jit(solution)/shard_map/reduce_scatter | solution.py:405
  110.9 1.0 copy-start.8
  111.0 1.9 %copy-start.7 = (bf16[3,256,256]{2,1,0:T(8,128)(2,1)S(1)}, bf16[3,256,256]{2,1,0:T(8,128)(2,1)}, u32[]{:S(2)}) copy-start(bf16[3,256,256]{2,1,0:T(8,128)(2,1)} %param.21) | copy-start | bytes 1179652
  153.9 1.2 copy-start.2
  155.2 0.9 copy-start.3
  156.1 22.7 %copy-start.9 = (bf16[3,2,1024]{2,1,0:T(2,128)(2,1)S(1)}, bf16[3,2,1024]{2,1,0:T(2,128)(2,1)}, u32[]{:S(2)}) copy-start(bf16[3,2,1024]{2,1,0:T(2,128)(2,1)} %param.12) | copy-start | bytes 36868
Sparse Core Ops, SparseCore 0:
  9.5 35.9 all-gather.7
  47.6 35.5 all-gather.5
  111.1 28.2 reduce-scatter.1

commit v5 on v4

v5 whole, which is shorter than its diff:
```python
import functools

import jax
import jax.numpy as jnp
import numpy as np
from jax import lax
from jax.experimental import pallas as pl
from jax.experimental.pallas import tpu as pltpu
from jax.sharding import Mesh
from jax.sharding import PartitionSpec as P

D = 8192
eps_norm = 1e-05
masked_score = -1e30
bf16 = jnp.bfloat16
f32 = jnp.float32
vmem = pl.BlockSpec(memory_space=pltpu.VMEM)
WIDE = ("z", "y")
NARROW = ("x", "core")


def three_parts(value):
    first = lax.reduce_precision(value, 8, 7)
    rest = value - first
    second = lax.reduce_precision(rest, 8, 7)
    return first, second, lax.reduce_precision(rest - second, 8, 7)


def iota(shape, axis):
    return lax.broadcasted_iota(jnp.int32, shape, axis)


def spread_kernel(packed_ref, pairs_ref, copies_ref, rows_ref):
    del pairs_ref
    ys, mine, width = copies_ref.shape
    chunks = width // 128
    rows_ref[...] = packed_ref[...].astype(f32)
    for j in range(chunks):
        chunk = rows_ref[pl.ds(j, mine, stride=chunks), :].astype(bf16)
        for y in range(ys):
            copies_ref[y, :, j * 128 : (j + 1) * 128] = chunk


def parts_of(value, count):
    found = []
    for _ in range(count):
        found.append(value.astype(bf16).astype(f32))
        value = value - found[-1]
    return found


def gain_rows(gain_ref):
    shape = (8, gain_ref.shape[1])
    rows = jnp.zeros(shape, f32)
    for k, part in enumerate(parts_of(gain_ref[...], 3)):
        rows = jnp.where(iota(shape, 0) == k, part, rows)
    return rows.astype(bf16)


def centred(tokens, gain_ref):
    tokens = tokens.astype(f32)
    total = tokens.sum(1, keepdims=True)
    mean = total * (1.0 / tokens.shape[1])
    squares = (tokens * tokens).sum(1, keepdims=True)
    return ((tokens - mean) * gain_ref[...]).astype(bf16), mean, total, squares


def across(left, right):
    return lax.dot_general(left, right, (((1,), (1,)), ((), ())), preferred_element_type=f32)


def gains_kernel(gain_ref, gate_ref, up_ref, products_ref):
    ffn = gate_ref.shape[1]
    gains = gain_rows(gain_ref)
    for k, ref in enumerate((gate_ref, up_ref)):
        product = jnp.dot(gains, ref[...], preferred_element_type=f32).sum(0, keepdims=True)
        products_ref[:, k * ffn : (k + 1) * ffn] = jnp.broadcast_to(product, (8, ffn))


def hidden_kernel(tokens_ref, gain_ref, products_ref, gate_ref, up_ref, parts_ref, sums_ref):
    ffn = gate_ref.shape[1]
    del parts_ref
    ready, mean, total, squares = centred(tokens_ref[...], gain_ref)
    for k, ref in enumerate((gate_ref, up_ref)):
        at = slice(k * ffn, (k + 1) * ffn)
        sums_ref[:, at] = jnp.dot(ready, ref[...], preferred_element_type=f32) + mean * products_ref[0:1, at]
    lane = iota((ready.shape[0], 128), 1)
    sums_ref[:, 2 * ffn :] = jnp.where(lane == 0, total, jnp.where(lane == 1, squares, 0.0))


def first_kernel(toks, column_ref, gain_ref, notes_ref, weights_ref, pairs_ref, parts_ref):
    ys, mine, width = column_ref.shape
    lanes = weights_ref.shape[2]
    cols = ys * lanes
    half = cols // 2
    zs = mine // toks
    chunks = width // lanes
    column, _, total, squares = centred(column_ref[0], gain_ref)
    gains = gain_rows(gain_ref)
    pairs, products = [], []
    for k in range(ys):
        query = jnp.dot(column, weights_ref[k], preferred_element_type=f32)
        parts_ref[:mine, k * lanes : (k + 1) * lanes] = query.astype(bf16)
        products.append(jnp.dot(gains, weights_ref[k], preferred_element_type=f32))
        rows = pairs_ref[k].astype(f32)
        count = rows.shape[0] // chunks
        pairs.append(jnp.concatenate([rows[j * count : (j + 1) * count] for j in range(chunks)], axis=1))
    pairs = jnp.concatenate(pairs, axis=0)
    count = pairs.shape[0]
    pairs = jnp.concatenate([pairs, jnp.zeros((128 - count, width), f32)], axis=0).astype(bf16)
    pair_products = across(gains, pairs).sum(0, keepdims=True)
    pairs = across(column, pairs).astype(bf16)
    at = iota((128, half), 1)
    spread = jnp.where((lax.rem(at, count) == iota((128, half), 0)) & (at < toks * count), 1.0, 0.0)
    pairs = jnp.dot(pairs, spread.astype(bf16), preferred_element_type=f32)
    start = lax.rem(iota((mine, half), 0), toks) * count
    at = iota((mine, half), 1)
    pairs = jnp.where((at >= start) & (at < start + count), pairs, 0.0).astype(bf16)
    start = iota((zs, mine), 0) * toks
    at = iota((zs, mine), 1)
    collect = jnp.where((at >= start) & (at < start + toks), 1.0, 0.0).astype(bf16)
    pairs = jnp.dot(collect, pairs, preferred_element_type=f32)

    row = iota((zs, half), 0)
    beside = jnp.zeros((zs, half), f32)
    for j in range(4):
        high, low = parts_of(notes_ref[0:1, j * half : (j + 1) * half], 2)
        beside = jnp.where(row == j, high, jnp.where(row == 4 + j, low, beside))
    parts_ref[mine : mine + zs] = jnp.concatenate([pairs, beside], axis=1).astype(bf16)

    row = iota((8, cols), 0)
    tail = jnp.zeros((8, cols), f32)
    for k, value in enumerate((total, squares)):
        value = jnp.concatenate([jnp.broadcast_to(value, (mine, 128)), jnp.zeros((128 - mine, 128), f32)], axis=0)
        value = jnp.concatenate([value.T[0:1], jnp.zeros((1, cols - 128), f32)], axis=1)
        for j, part in enumerate(parts_of(value, 3)):
            tail = jnp.where(row == 3 * k + j, part, tail)
    products = jnp.concatenate(products, axis=1).sum(0, keepdims=True)
    for k, part in enumerate(parts_of(products, 2)):
        tail = jnp.where(row == 6 + k, part, tail)
    pair_products = jnp.concatenate([jnp.zeros((1, cols - 128), f32), pair_products], axis=1)
    for k, part in enumerate(parts_of(pair_products, 2)):
        tail = jnp.where((row == k) & (iota((8, cols), 1) >= cols - 128), part, tail)
    parts_ref[mine + zs :] = tail.astype(bf16)


def pick(shape, group, mask):
    frm, to = iota(shape, 0), iota(shape, 1)
    kind = frm & 7
    same = lax.shift_right_logical(frm, 3) == lax.shift_right_logical(to, group)
    return jnp.where(same & (kind < 3) & mask(to), 1.0, 0.0).astype(bf16)


def norm(tails, first, count):
    every = tails.shape[1] - 128
    shape = (count, every)
    select = jnp.where(iota(shape, 1) == iota(shape, 0) + first, 1.0, 0.0).astype(bf16)
    own = across(select, tails[:, :every]).astype(bf16)
    kind = iota((tails.shape[0], 128), 0) & 7
    total = jnp.dot(own, jnp.where(kind < 3, 1.0, 0.0).astype(bf16), preferred_element_type=f32)
    centre = total * (1.0 / D)
    total = jnp.dot(
        own, jnp.where((kind >= 3) & (kind < 6), 1.0, 0.0).astype(bf16), preferred_element_type=f32
    )
    spread = total * (1.0 / D) - centre * centre
    return own, centre, lax.rsqrt(spread + eps_norm)


def shift(own, centre, group, mask, table, width):
    shape = (own.shape[1], table.shape[0])
    means = jnp.dot(own, pick(shape, group, mask), preferred_element_type=f32) * (1.0 / width)
    shape = (own.shape[0], table.shape[0])
    means = jnp.where(mask(iota(shape, 1)), means - centre[:, : shape[1]], 0.0)
    high, low = parts_of(means, 2)
    return jnp.dot(high.astype(bf16), table, preferred_element_type=f32) + jnp.dot(
        low.astype(bf16), table, preferred_element_type=f32
    )


def tails_of(parts_ref, first):
    ns = parts_ref.shape[0]
    return jnp.concatenate([parts_ref[n, first:].astype(f32) for n in range(ns)], axis=0).astype(bf16)


def third_kernel(toks, sums_ref, parts_ref, hidden_ref):
    ns, rows, cols = parts_ref.shape
    ffn = hidden_ref.shape[1]
    half = cols // 2
    zs = (rows - 8) // (toks + 1)
    mine = zs * toks
    besides = jnp.concatenate([parts_ref[n, mine : mine + zs, half:] for n in range(ns)], axis=0)
    at = iota((8, ns * zs), 1) & (zs - 1)
    centre = sums_ref[:, 2 * ffn : 2 * ffn + 1] * (1.0 / D)
    spread = sums_ref[:, 2 * ffn + 1 : 2 * ffn + 2] * (1.0 / D) - centre * centre
    scale = lax.rsqrt(spread + eps_norm)
    for j in range(2):
        both = []
        for k in (j, j + 2):
            take = jnp.where((at == k) | (at == k + 4), 1.0, 0.0).astype(bf16)
            product = jnp.dot(take, besides, preferred_element_type=f32)[0:1]
            both.append((sums_ref[:, k * half : (k + 1) * half] - centre * product) * scale)
        gate, up = both
        hidden_ref[:, j * half : (j + 1) * half] = (gate / (1.0 + jnp.exp(-gate)) * up).astype(bf16)


def second_kernel(toks, width, parts_ref, block_ref):
    ns, rows, cols = parts_ref.shape
    half = cols // 2
    zs = block_ref.shape[0] // 8
    mine = zs * toks
    every = cols - 128
    tails = tails_of(parts_ref, mine + zs)
    total = parts_ref[0, : mine + zs].astype(f32)
    for n in range(1, ns):
        total = total + parts_ref[n, : mine + zs].astype(f32)
    own, centre, scale = norm(tails, 0, mine)
    query = total[:mine] + shift(own, centre, 3, lambda to: (to & 7) >= 6, tails, width)
    query = (query * jnp.concatenate([scale] * (cols // 128), axis=1)).astype(bf16)
    start = iota((mine, zs), 1) * toks
    at = iota((mine, zs), 0)
    expand = jnp.where((at >= start) & (at < start + toks), 1.0, 0.0).astype(bf16)
    pairs = jnp.zeros((mine, half), f32)
    for part in parts_of(total[mine:, :half], 3):
        pairs = pairs + jnp.dot(expand, part.astype(bf16), preferred_element_type=f32)
    pair_cols = 2 * cols // zs // 2
    at = iota((128, half), 1)
    spread = jnp.where((lax.rem(at, pair_cols) == iota((128, half), 0)) & (at < toks * pair_cols), 1.0, 0.0)
    shifted = shift(own, centre, 3, lambda to: (to & 7) < 2, tails[:, every:], width)
    for part in parts_of(shifted, 3):
        pairs = pairs + jnp.dot(part.astype(bf16), spread.astype(bf16), preferred_element_type=f32)
    pairs = pairs * jnp.concatenate([scale] * (half // 128), axis=1)
    start = lax.rem(iota((mine, half), 0), toks) * pair_cols
    at = iota((mine, half), 1)
    pairs = jnp.where((at >= start) & (at < start + pair_cols), pairs, 0.0).astype(bf16)
    shape = (zs * 8, mine)
    to, at = iota(shape, 0), iota(shape, 1)
    row = to & 7
    start = lax.shift_right_logical(to, 3) * toks
    take = jnp.where((row < toks) & (at == start + row), 1.0, 0.0).astype(bf16)
    block_ref[...] = jnp.dot(take, query, preferred_element_type=f32).astype(bf16)
    take = jnp.where((row == toks) & (at >= start) & (at < start + toks), 1.0, 0.0).astype(bf16)
    pairs = jnp.dot(take, pairs, preferred_element_type=f32)
    block_ref[:, :half] = (block_ref[:, :half].astype(f32) + pairs).astype(bf16)


def last_kernel(toks, per_z, parts_ref, weights_ref, down_ref, mixed_ref):
    ns, rows, cols = parts_ref.shape
    mine = mixed_ref.shape[0]
    zs = rows - mine
    head = cols // per_z
    shape = (ns * mine, ns * zs)
    start = iota(shape, 1) * toks
    at = iota(shape, 0)
    expand = jnp.where((at >= start) & (at < start + toks), 1.0, 0.0).astype(bf16)
    shape = (ns * mine, 128)
    at = iota(shape, 1)
    own = (lax.rem(at, 8) == lax.rem(iota(shape, 0), toks)) & (at < 48)
    at = iota((128, 128), 0)
    pick_top = jnp.where(at < 24, 1.0, 0.0).astype(bf16)
    pick_total = jnp.where((at >= 24) & (at < 48), 1.0, 0.0).astype(bf16)
    mixed = down_ref[0].astype(f32)
    for k in range(1, down_ref.shape[0]):
        mixed = mixed + down_ref[k].astype(f32)
    for k in range(per_z):
        marks = jnp.concatenate([parts_ref[n, mine:, k * head : k * head + 128] for n in range(ns)], axis=0)
        marks = jnp.dot(expand, marks, preferred_element_type=f32)
        marks = jnp.where(own, marks, 0.0).astype(bf16)
        tops = jnp.dot(marks, pick_top, preferred_element_type=f32)
        totals = jnp.dot(marks, pick_total, preferred_element_type=f32)
        tops = [tops[n * mine : (n + 1) * mine] for n in range(ns)]
        top = tops[0]
        for n in range(1, ns):
            top = jnp.maximum(top, tops[n])
        total = jnp.zeros((mine, 128), f32)
        weighted = jnp.zeros((mine, head), f32)
        for n in range(ns):
            scale = jnp.exp(tops[n] - top)
            total = total + totals[n * mine : (n + 1) * mine] * scale
            scale = jnp.concatenate([scale] * (head // 128), axis=1)
            weighted = weighted + parts_ref[n, :mine, k * head : (k + 1) * head].astype(f32) * scale
        total = jnp.concatenate([total] * (head // 128), axis=1)
        attended = (weighted / total).astype(bf16)
        mixed = mixed + jnp.dot(
            attended, weights_ref[k * head : (k + 1) * head], preferred_element_type=f32
        )
    mixed_ref[...] = mixed.astype(bf16)


def local(
    activations,
    norm_gain,
    w_query,
    w_keyval,
    w_out,
    w_gate,
    w_up,
    w_down,
    key_cache,
    value_cache,
    lengths,
):
    zs, ys, ns = lax.axis_size("z"), lax.axis_size("y"), lax.axis_size(NARROW)
    ws = zs * ys
    rows, new, width = activations.shape
    toks = rows * new
    mine = zs * toks
    head_dim = key_cache.shape[2]
    kv_cols = w_keyval.shape[1]
    lanes = w_query.shape[1]
    heads = ws * lanes // head_dim
    cols = ys * lanes
    pair_cols = ys * kv_cols
    per_z = cols // head_dim
    ffn = w_gate.shape[1]

    values = activations.reshape(toks, width).astype(f32)
    gain = norm_gain.reshape(1, width)

    chunks = width // lanes
    pair_lanes = w_keyval.T.reshape(kv_cols, chunks, lanes).transpose(1, 0, 2).reshape(chunks * kv_cols, lanes)
    w_first = lax.all_gather(w_query, "y", axis=0, tiled=False)
    w_pair = lax.all_gather(pair_lanes, "y", axis=0, tiled=False)
    w_last = lax.all_gather(w_out, "y", axis=0, tiled=True)

    packed = activations.reshape(toks * width // 128, 128)
    copies = jnp.broadcast_to(packed[None], (zs,) + packed.shape)
    column = lax.all_to_all(copies, "z", 0, 0, tiled=True)
    column = pl.pallas_call(
        spread_kernel,
        out_shape=jax.ShapeDtypeStruct((ys, mine, width), bf16),
        in_specs=[vmem, vmem],
        out_specs=vmem,
        scratch_shapes=[pltpu.VMEM((mine * width // 128, 128), f32)],
        compiler_params=pltpu.CompilerParams(vmem_limit_bytes=8 * 2**20),
        cost_estimate=pl.CostEstimate(flops=0, bytes_accessed=2**20, transcendentals=0),
        name="spread",
    )(column.reshape(mine * width // 128, 128), w_pair)

    products = pl.pallas_call(
        gains_kernel,
        out_shape=jax.ShapeDtypeStruct((8, 2 * ffn), f32),
        in_specs=[vmem] * 3,
        out_specs=vmem,
        compiler_params=pltpu.CompilerParams(vmem_limit_bytes=8 * 2**20),
        cost_estimate=pl.CostEstimate(flops=2**25, bytes_accessed=2 * 2**20, transcendentals=0),
        name="gains",
    )(gain, w_gate, w_up)
    flat = lax.all_to_all(column, "y", 0, 0, tiled=True).reshape(ys * mine, width)
    parts = pl.pallas_call(
        functools.partial(first_kernel, toks),
        out_shape=jax.ShapeDtypeStruct((mine + zs + 8, cols), bf16),
        in_specs=[vmem] * 5,
        out_specs=vmem,
        compiler_params=pltpu.CompilerParams(vmem_limit_bytes=12 * 2**20),
        cost_estimate=pl.CostEstimate(flops=2 * mine * width * cols, bytes_accessed=2 * 2**20, transcendentals=0),
        name="first",
    )(column, gain, products, w_first, w_pair)

    sums = pl.pallas_call(
        hidden_kernel,
        out_shape=jax.ShapeDtypeStruct((ys * mine, 2 * ffn + 128), f32),
        in_specs=[vmem] * 6,
        out_specs=vmem,
        compiler_params=pltpu.CompilerParams(vmem_limit_bytes=16 * 2**20),
        cost_estimate=pl.CostEstimate(flops=2**30, bytes_accessed=4 * 2**20, transcendentals=0),
        name="hidden",
    )(flat, gain, products, w_gate, w_up, parts)
    sums = lax.psum_scatter(sums, NARROW, scatter_dimension=0, tiled=True)

    parts = lax.all_gather(parts, NARROW, axis=0, tiled=False)
    notes = parts
    block = pl.pallas_call(
        functools.partial(second_kernel, toks, width),
        out_shape=jax.ShapeDtypeStruct((zs * 8, cols), bf16),
        in_specs=[vmem],
        out_specs=vmem,
        compiler_params=pltpu.CompilerParams(vmem_limit_bytes=12 * 2**20),
        cost_estimate=pl.CostEstimate(flops=2**24, bytes_accessed=2 * 2**20, transcendentals=0),
        name="second",
    )(parts)
    block = lax.all_to_all(block.reshape(zs, 8, cols), "z", 0, 0, tiled=True)

    queries = (
        block[:, :toks]
        .reshape(zs, rows, new, per_z, head_dim)
        .transpose(1, 2, 0, 3, 4)
        .reshape(rows, new * heads, head_dim)
    )
    pairs = (
        block[:, toks, : toks * pair_cols]
        .reshape(zs, toks, pair_cols)
        .transpose(1, 0, 2)
        .reshape(rows, new, 2 * head_dim)
    )
    new_keys, new_values = pairs[..., :head_dim], pairs[..., head_dim:]
    narrow_index = lax.axis_index(NARROW)
    cache_part = key_cache.shape[1]
    factor = head_dim ** (-0.5)
    positions = narrow_index * cache_part + jnp.arange(cache_part, dtype=jnp.int32)
    usable = (positions[None, :] < lengths[:, None])[:, None, :]
    scores = jnp.einsum("rqd,rpd->rqp", queries, key_cache, preferred_element_type=f32) * factor
    scores = jnp.where(usable, scores, masked_score)
    own = jnp.einsum("rqd,rud->rqu", queries, new_keys, preferred_element_type=f32) * factor
    token_of = np.arange(new * heads) // heads
    causal = (token_of[:, None] >= np.arange(new)[None, :])[None]
    causal = jnp.logical_and(causal, narrow_index == 0)
    own = jnp.where(causal, own, masked_score)
    top = jnp.maximum(scores.max(-1), own.max(-1))
    weights = jnp.where(usable, jnp.exp(scores - top[..., None]), 0.0)
    own_weights = jnp.where(causal, jnp.exp(own - top[..., None]), 0.0)
    total = weights.sum(-1) + own_weights.sum(-1)
    weighted = jnp.einsum("rqp,rpd->rqd", weights.astype(bf16), value_cache, preferred_element_type=f32)
    weighted = weighted + jnp.einsum("rqu,rud->rqd", own_weights, new_values.astype(f32))

    sent = (
        weighted.astype(bf16)
        .reshape(rows, new, zs, per_z, head_dim)
        .transpose(2, 0, 1, 3, 4)
        .reshape(zs, toks, cols)
    )
    marks = jnp.stack(three_parts(top) + three_parts(total)).astype(bf16)
    marks = marks.reshape(6, toks, zs, per_z).transpose(2, 3, 0, 1)
    marks = jnp.pad(marks, ((0, 0), (0, 0), (0, 0), (0, 8 - toks))).reshape(zs, per_z, 48)
    marks = jnp.pad(marks, ((0, 0), (0, 0), (0, head_dim - 48))).reshape(zs, 1, cols)
    block = jnp.concatenate([sent, marks, jnp.zeros((zs, 8 - toks - 1, cols), bf16)], axis=1)
    block = lax.all_to_all(block, "z", 0, 0, tiled=True)
    parts = jnp.concatenate([block[:, :toks].reshape(mine, cols), block[:, toks]], axis=0)
    parts = lax.all_gather(parts, NARROW, axis=0, tiled=False)
    hidden = pl.pallas_call(
        functools.partial(third_kernel, toks),
        out_shape=jax.ShapeDtypeStruct((sums.shape[0], ffn), bf16),
        in_specs=[vmem, vmem],
        out_specs=vmem,
        compiler_params=pltpu.CompilerParams(vmem_limit_bytes=8 * 2**20),
        cost_estimate=pl.CostEstimate(flops=2**24, bytes_accessed=2 * 2**20, transcendentals=0),
        name="third",
    )(sums, notes)
    hidden = lax.all_gather(hidden, NARROW, axis=0, tiled=True)
    down = jnp.dot(hidden, w_down, preferred_element_type=f32).astype(bf16)
    down = lax.all_to_all(down.reshape(ys, mine, width), "y", 0, 0, tiled=True)

    mixed = pl.pallas_call(
        functools.partial(last_kernel, toks, per_z),
        out_shape=jax.ShapeDtypeStruct((mine, width), bf16),
        in_specs=[vmem, vmem, vmem],
        out_specs=vmem,
        compiler_params=pltpu.CompilerParams(vmem_limit_bytes=12 * 2**20),
        cost_estimate=pl.CostEstimate(
            flops=2 * mine * width * cols, bytes_accessed=3 * 2**20, transcendentals=0
        ),
        name="last",
    )(parts, w_last, down)
    mixed = mixed.reshape(zs, toks * width // 128, 128)
    mixed = lax.all_to_all(mixed, "z", 0, 0, tiled=True)
    mixed = mixed.astype(f32).sum(0).reshape(toks, width)
    return (values + mixed).astype(bf16).reshape(activations.shape)


def solution(mesh):
    names = ("z", "y", "x", "core")
    split = Mesh(mesh.devices.reshape(16, 4, 4, 2), names)
    return jax.shard_map(
        local,
        mesh=split,
        in_specs=(
            P(WIDE, None, NARROW),
            P(NARROW),
            P(NARROW, WIDE),
            P(NARROW, WIDE),
            P(WIDE, NARROW),
            P(NARROW, WIDE),
            P(NARROW, WIDE),
            P(WIDE, NARROW),
            P(WIDE, NARROW, None),
            P(WIDE, NARROW, None),
            P(WIDE),
        ),
        out_specs=P(WIDE, None, NARROW),
        check_vma=False,
    )
```

time: 187 us -> 180 us (0.963)
  the two profiles are of different devices: /device:TPU:32 before, /device:TPU:40 now
where the time goes in v5:
time: 180 us; the launch traced here: 179 us
  blocking collectives  81.1 us (45%)
  starting transfers between devices  37.7 us (21%)
  waiting for transfers between devices  25.9 us (14%)
  between operations  13.4 us (7%)
  Pallas kernels  10.1 us (6%)
  local copies, waits for them, and re-layouts  6.92 us (4%)
  matrix products  2.45 us (1%)
    all_to_all x1, blocking collectives, local(): mixed = lax.all_to_all(mixed, 'z', 0, 0, tiled=True)  28.3 us
    all_gather x2, blocking collectives, local(): parts = lax.all_gather(parts, NARROW, axis=0, tiled=False)  27.6 us
    all_to_all x1, starting transfers between devices, local(): column = lax.all_to_all(copies, 'z', 0, 0, tiled=True)  15.2 us
    all_to_all x1, waiting for transfers between devices, local(): block = lax.all_to_all(block.reshape(zs, 8, cols), 'z', 0, 0, tiled=True)  14.2 us
    all_gather x1, blocking collectives, local(): hidden = lax.all_gather(hidden, NARROW, axis=0, tiled=True)  13 us
    all_gather x1, blocking collectives, local(): w_pair = lax.all_gather(pair_lanes, 'y', axis=0, tiled=False)  12.3 us
    all_to_all x1, starting transfers between devices, local(): block = lax.all_to_all(block.reshape(zs, 8, cols), 'z', 0, 0, tiled=True)  8.88 us
    all_to_all x1, waiting for transfers between devices, local(): lax.all_to_all(column, 'y', 0, 0, tiled=True).reshape(ys * mine, width)  6.81 us
  transfers between devices with their start and end apart: 8, of which 3 were waited for; matrix products, arithmetic and copies ran while one was open for 4% of the time, Pallas kernels for 3%

profile of v5, /device:TPU:40, one launch (start us, length us, event | category | flops | bytes accessed | tf_op | source)
XLA Modules:
  0.0 178.8 jit_solution(14265603157793549412)
XLA Ops:
  7.3 0.7 broadcast_in_dim.54
  8.7 15.2 %all-to-all-start = ((bf16[16,48,128]{2,1,0:T(8,128)(2,1)}), bf16[16,48,128]{2,1,0:T(8,128)(2,1)S(1)}, u32[]{:S(2)}, u32[]{:S(2)}) async-start(bf16[16,48,128]{2,1,0:T(8,128)(2,1)} %broadcast_in_dim.55), calls=%async_computation | async-start | bytes 393216 | tf_op jit(solution)/shard_map/all_to_all | solution.py:327
  23.9 12.3 %all_gather.27.pairs_ref = bf16[4,64,128]{2,1,0:T(8,128)(2,1)S(1)} all-gather(bf16[1,64,128]{2,1,0:T(8,128)(2,1)} %bitcast.56), channel_id=1, replica_groups=mesh['z'=16,'y'=4,'x'=4,'core'=2] {'y'}, dimensions={0}, use_global_device_ids=true | all-gather | bytes 81920 | tf_op jit(solution)/shard_map/all_gather | solution.py:322
  36.2 3.5 %all-to-all-done = bf16[16,48,128]{2,1,0:T(8,128)(2,1)S(1)} async-done(((bf16[16,48,128]{2,1,0:T(8,128)(2,1)}), bf16[16,48,128]{2,1,0:T(8,128)(2,1)S(1)}, u32[]{:S(2)}, u32[]{:S(2)}) %all-to-all-start) | async-done | bytes 196640 | tf_op jit(solution)/shard_map/all_to_all | solution.py:327
  39.7 1.2 spread.1.column_ref
  40.9 4.9 %all-to-all-start.3 = ((bf16[4,96,1024]{2,1,0:T(8,128)(2,1)}), bf16[4,96,1024]{2,1,0:T(8,128)(2,1)}, u32[]{:S(2)}, u32[]{:S(2)}) async-start(bf16[4,96,1024]{2,1,0:T(8,128)(2,1)} %spread.1.column_ref), calls=%async_computation.3 | async-start | bytes 1572864 | tf_op jit(solution)/shard_map/all_to_all | solution.py:348
  46.2 1.2 copy-done.4
  47.4 2.0 %first.1.parts_ref = bf16[120,512]{1,0:T(8,128)(2,1)S(1)} custom-call(bf16[4,96,1024]{2,1,0:T(8,128)(2,1)} %spread.1.column_ref, f32[1,1024]{1,0:T(1,128)S(1)} %bitcast.46, f32[8,1024]{1,0:T(8,128)S(1)} %gains.1.notes_ref.products_ref, bf16[4,1024,128]{2,1,0:T(8,128)(2,1)S(1)} %bitcast.43, bf16[4,64,128]{2,1,0:T(8,128)(2,1)S(1)} %all_gather.27.pairs_ref), custom_call_target="tpu_custom_call" | custom-call | flops 100663296 | bytes 2097152 | tf_op jit(solution)/shard_map/first/pallas_call | solution.py:349
  49.5 6.8 %all-to-all-done.3 = bf16[4,96,1024]{2,1,0:T(8,128)(2,1)} async-done(((bf16[4,96,1024]{2,1,0:T(8,128)(2,1)}), bf16[4,96,1024]{2,1,0:T(8,128)(2,1)}, u32[]{:S(2)}, u32[]{:S(2)}) %all-to-all-start.3) | async-done | bytes 786464 | tf_op jit(solution)/shard_map/all_to_all | solution.py:348
  56.3 3.5 %hidden.1 = f32[384,1152]{1,0:T(8,128)} custom-call(bf16[384,1024]{1,0:T(8,128)(2,1)} %bitcast.18.tokens_ref, f32[1,1024]{1,0:T(1,128)S(1)} %bitcast.47, f32[8,1024]{1,0:T(8,128)S(1)} %gains.1.notes_ref.products_ref, bf16[1024,512]{1,0:T(8,128)(2,1)S(1)} %copy-done.1, bf16[1024,512]{1,0:T(8,128)(2,1)S(1)} %copy-done.2, bf16[120,512]{1,0:T(8,128)(2,1)S(1)} %first.1.parts_ref), custom_call_target="tpu_custom_call" | custom-call | flops 1073741824 | bytes 4194304 | tf_op jit(solution)/shard_map/hidden/pallas_call | solution.py:359
  60.5 14.1 %all-gather.1 = bf16[960,512]{1,0:T(8,128)(2,1)S(1)} all-gather(bf16[120,512]{1,0:T(8,128)(2,1)S(1)} %first.1.parts_ref), channel_id=3, replica_groups=mesh['z'=16,'y'=4,'x'=4,'core'=2] {'x','core'}, dimensions={0}, use_global_device_ids=true | all-gather | bytes 1105920 | tf_op jit(solution)/shard_map/all_gather | solution.py:370
  74.6 1.6 second.1
  76.3 8.9 %all-to-all-start.1 = ((bf16[16,8,512]{2,1,0:T(8,128)(2,1)}), bf16[16,8,512]{2,1,0:T(8,128)(2,1)S(1)}, u32[]{:S(2)}, u32[]{:S(2)}) async-start(bf16[16,8,512]{2,1,0:T(8,128)(2,1)} %bitcast.8), calls=%async_computation.1 | async-start | bytes 262144 | tf_op jit(solution)/shard_map/all_to_all | solution.py:381
  85.3 14.2 %all-to-all-done.1 = bf16[16,8,512]{2,1,0:T(8,128)(2,1)S(1)} async-done(((bf16[16,8,512]{2,1,0:T(8,128)(2,1)}), bf16[16,8,512]{2,1,0:T(8,128)(2,1)S(1)}, u32[]{:S(2)}, u32[]{:S(2)}) %all-to-all-start.1) | async-done | bytes 131104 | tf_op jit(solution)/shard_map/all_to_all | solution.py:381
  102.1 0.7 copy.53
  102.8 4.7 %all-to-all-start.2 = ((bf16[16,8,512]{2,1,0:T(8,128)(2,1)}), bf16[16,8,512]{2,1,0:T(8,128)(2,1)S(1)}, u32[]{:S(2)}, u32[]{:S(2)}) async-start(bf16[16,8,512]{2,1,0:T(8,128)(2,1)} %copy.53), calls=%async_computation.2 | async-start | bytes 262144 | tf_op jit(solution)/shard_map/all_to_all | solution.py:426
  107.6 0.9 copy-done.5
  108.7 13.0 %all_gather.35 = bf16[384,512]{1,0:T(8,128)(2,1)S(1)} all-gather(bf16[48,512]{1,0:T(8,128)(2,1)S(1)} %third.1), channel_id=1, replica_groups=mesh['z'=16,'y'=4,'x'=4,'core'=2] {'x','core'}, dimensions={0}, use_global_device_ids=true | all-gather | bytes 442368 | tf_op jit(solution)/shard_map/all_gather | solution.py:438
  121.7 1.5 convolution_convert_fusion
  123.1 3.9 %all-to-all-start.4 = ((bf16[4,96,1024]{2,1,0:T(8,128)(2,1)}), bf16[4,96,1024]{2,1,0:T(8,128)(2,1)S(1)}, u32[]{:S(2)}, u32[]{:S(2)}) async-start(bf16[4,96,1024]{2,1,0:T(8,128)(2,1)} %bitcast.19), calls=%async_computation.5 | async-start | bytes 1572864 | tf_op jit(solution)/shard_map/all_to_all | solution.py:440
  127.2 13.5 %all-gather.2 = bf16[896,512]{1,0:T(8,128)(2,1)S(1)} all-gather(bf16[112,512]{1,0:T(8,128)(2,1)S(1)} %pad_maximum_fusion), channel_id=4, replica_groups=mesh['z'=16,'y'=4,'x'=4,'core'=2] {'x','core'}, dimensions={0}, use_global_device_ids=true | all-gather | bytes 1032192 | tf_op jit(solution)/shard_map/all_gather | solution.py:428
  140.7 1.2 copy-done.3
  141.9 1.3 last.1
  143.3 28.3 %all_to_all.30 = bf16[16,48,128]{2,1,0:T(8,128)(2,1)S(1)} all-to-all(bf16[16,48,128]{2,1,0:T(8,128)(2,1)S(1)} %reshape.211), channel_id=1, replica_groups=mesh['z'=16,'y'=4,'x'=4,'core'=2] {'z'}, dimensions={0} | all-to-all | bytes 393216 | tf_op jit(solution)/shard_map/all_to_all | solution.py:454
  (79 shorter events, 6.3 us)
Async XLA Ops:
  6.5 115.1 %copy-start = (bf16[512,1024]{1,0:T(8,128)(2,1)S(1)}, bf16[512,1024]{1,0:T(8,128)(2,1)}, u32[]{:S(2)}) copy-start(bf16[512,1024]{1,0:T(8,128)(2,1)} %param.19) | copy-start | bytes 3145732
  6.5 39.3 %copy-start.1 = (bf16[1024,512]{1,0:T(8,128)(2,1)S(1)}, bf16[1024,512]{1,0:T(8,128)(2,1)}, u32[]{:S(2)}) copy-start(bf16[1024,512]{1,0:T(8,128)(2,1)} %gate_ref.3) | copy-start | bytes 3145732
  6.5 39.3 %copy-start.2 = (bf16[1024,512]{1,0:T(8,128)(2,1)S(1)}, bf16[1024,512]{1,0:T(8,128)(2,1)}, u32[]{:S(2)}) copy-start(bf16[1024,512]{1,0:T(8,128)(2,1)} %up_ref.3) | copy-start | bytes 3145732
  6.5 39.3 %copy-start.6 = (f32[1024]{0:T(1024)S(1)}, f32[1024]{0:T(1024)}, u32[]{:S(2)}) copy-start(f32[1024]{0:T(1024)} %param.13) | copy-start | bytes 12292
  6.5 39.7 %all-gather.8.cloned.1.call-start = ((), (), s32[]{:S(2)}) async-start(), calls=%async_computation.9 | async-start | bytes 1310720 | tf_op jit(solution)/shard_map/all_gather | solution.py:321
  8.7 31.0 %all-to-all-start = ((bf16[16,48,128]{2,1,0:T(8,128)(2,1)}), bf16[16,48,128]{2,1,0:T(8,128)(2,1)S(1)}, u32[]{:S(2)}, u32[]{:S(2)}) async-start(bf16[16,48,128]{2,1,0:T(8,128)(2,1)} %broadcast_in_dim.55), calls=%async_computation | async-start | bytes 393216 | tf_op jit(solution)/shard_map/all_to_all | solution.py:327
  40.9 15.4 %all-to-all-start.3 = ((bf16[4,96,1024]{2,1,0:T(8,128)(2,1)}), bf16[4,96,1024]{2,1,0:T(8,128)(2,1)}, u32[]{:S(2)}, u32[]{:S(2)}) async-start(bf16[4,96,1024]{2,1,0:T(8,128)(2,1)} %spread.1.column_ref), calls=%async_computation.3 | async-start | bytes 1572864 | tf_op jit(solution)/shard_map/all_to_all | solution.py:348
  45.8 61.7 %reduce-scatter.2.cloned.1.call-start = ((), (), s32[]{:S(2)}) async-start(), calls=%async_computation.8 | async-start | bytes 1990656 | tf_op jit(solution)/shard_map/reduce_scatter | solution.py:368
  46.2 1.2 copy-start.4
  59.8 25.5 %copy-start.11 = (pred[1,64,2]{1,2,0:T(4,128)(4,1)S(1)}, pred[1,64,2]{1,2,0:T(4,128)(4,1)}, u32[]{:S(2)}) copy-start(pred[1,64,2]{1,2,0:T(4,128)(4,1)} %constant.28.clone) | copy-start | bytes 388
  59.8 25.5 %copy-start.10 = (s32[3]{0:T(128)S(1)}, s32[3]{0:T(128)}, u32[]{:S(2)}) copy-start(s32[3]{0:T(128)} %param.22) | copy-start | bytes 40
  59.8 40.3 %copy-start.8 = (bf16[3,256,256]{2,1,0:T(8,128)(2,1)S(1)}, bf16[3,256,256]{2,1,0:T(8,128)(2,1)}, u32[]{:S(2)}) copy-start(bf16[3,256,256]{2,1,0:T(8,128)(2,1)} %param.20) | copy-start | bytes 1179652
  59.8 80.9 %all-gather.6.cloned.1.call-start = ((), (), s32[]{:S(2)}) async-start(), calls=%async_computation.7 | async-start | bytes 1310720 | tf_op jit(solution)/shard_map/all_gather | solution.py:323
  74.6 27.0 %copy-start.7 = (bf16[3,256,256]{2,1,0:T(8,128)(2,1)S(1)}, bf16[3,256,256]{2,1,0:T(8,128)(2,1)}, u32[]{:S(2)}) copy-start(bf16[3,256,256]{2,1,0:T(8,128)(2,1)} %param.21) | copy-start | bytes 1179652
  76.3 23.3 %all-to-all-start.1 = ((bf16[16,8,512]{2,1,0:T(8,128)(2,1)}), bf16[16,8,512]{2,1,0:T(8,128)(2,1)S(1)}, u32[]{:S(2)}, u32[]{:S(2)}) async-start(bf16[16,8,512]{2,1,0:T(8,128)(2,1)} %bitcast.8), calls=%async_computation.1 | async-start | bytes 262144 | tf_op jit(solution)/shard_map/all_to_all | solution.py:381
  102.8 20.3 %all-to-all-start.2 = ((bf16[16,8,512]{2,1,0:T(8,128)(2,1)}), bf16[16,8,512]{2,1,0:T(8,128)(2,1)S(1)}, u32[]{:S(2)}, u32[]{:S(2)}) async-start(bf16[16,8,512]{2,1,0:T(8,128)(2,1)} %copy.53), calls=%async_computation.2 | async-start | bytes 262144 | tf_op jit(solution)/shard_map/all_to_all | solution.py:426
  107.5 0.9 copy-start.5
  123.1 17.6 %all-to-all-start.4 = ((bf16[4,96,1024]{2,1,0:T(8,128)(2,1)}), bf16[4,96,1024]{2,1,0:T(8,128)(2,1)S(1)}, u32[]{:S(2)}, u32[]{:S(2)}) async-start(bf16[4,96,1024]{2,1,0:T(8,128)(2,1)} %bitcast.19), calls=%async_computation.5 | async-start | bytes 1572864 | tf_op jit(solution)/shard_map/all_to_all | solution.py:440
  140.7 1.2 copy-start.3
  141.9 29.7 %copy-start.9 = (bf16[3,2,1024]{2,1,0:T(2,128)(2,1)S(1)}, bf16[3,2,1024]{2,1,0:T(2,128)(2,1)}, u32[]{:S(2)}) copy-start(bf16[3,2,1024]{2,1,0:T(2,128)(2,1)} %param.12) | copy-start | bytes 36868
Sparse Core Ops, SparseCore 0:
  9.5 34.4 all-gather.7
  59.9 37.5 reduce-scatter.1
  99.6 30.0 all-gather.5

commit v6 on v5

--- a/solution.py
+++ b/solution.py
@@ -15,6 +15,7 @@
 bf16 = jnp.bfloat16
 f32 = jnp.float32
 vmem = pl.BlockSpec(memory_space=pltpu.VMEM)
+anywhere = pl.BlockSpec(memory_space=pl.ANY)
 WIDE = ("z", "y")
 NARROW = ("x", "core")
 
@@ -77,15 +78,29 @@
         products_ref[:, k * ffn : (k + 1) * ffn] = jnp.broadcast_to(product, (8, ffn))
 
 
-def hidden_kernel(tokens_ref, gain_ref, products_ref, gate_ref, up_ref, parts_ref, sums_ref):
+def hidden_kernel(
+    source_ref, gain_ref, products_ref, gate_ref, up_ref, parts_ref, out_ref, tokens_ref, sums_ref, arrived, sent
+):
+    del parts_ref
     ffn = gate_ref.shape[1]
-    del parts_ref
-    ready, mean, total, squares = centred(tokens_ref[...], gain_ref)
-    for k, ref in enumerate((gate_ref, up_ref)):
-        at = slice(k * ffn, (k + 1) * ffn)
-        sums_ref[:, at] = jnp.dot(ready, ref[...], preferred_element_type=f32) + mean * products_ref[0:1, at]
-    lane = iota((ready.shape[0], 128), 1)
-    sums_ref[:, 2 * ffn :] = jnp.where(lane == 0, total, jnp.where(lane == 1, squares, 0.0))
+    pieces = arrived.shape[0]
+    count = source_ref.shape[0] // pieces
+    lane = iota((count, 128), 1)
+    rows = [slice(j * count, (j + 1) * count) for j in range(pieces)]
+    reads = [pltpu.make_async_copy(source_ref.at[at], tokens_ref.at[at], arrived.at[j]) for j, at in enumerate(rows)]
+    writes = [pltpu.make_async_copy(sums_ref.at[at], out_ref.at[at], sent.at[j]) for j, at in enumerate(rows)]
+    for read in reads:
+        read.start()
+    for j, at in enumerate(rows):
+        reads[j].wait()
+        ready, mean, total, squares = centred(tokens_ref[at], gain_ref)
+        for k, ref in enumerate((gate_ref, up_ref)):
+            product = jnp.dot(ready, ref[...], preferred_element_type=f32)
+            sums_ref[at, k * ffn : (k + 1) * ffn] = product + mean * products_ref[0:1, k * ffn : (k + 1) * ffn]
+        sums_ref[at, 2 * ffn :] = jnp.where(lane == 0, total, jnp.where(lane == 1, squares, 0.0))
+        writes[j].start()
+    for write in writes:
+        write.wait()
 
 
 def first_kernel(toks, column_ref, gain_ref, notes_ref, weights_ref, pairs_ref, parts_ref):
@@ -241,6 +256,104 @@
     take = jnp.where((row == toks) & (at >= start) & (at < start + toks), 1.0, 0.0).astype(bf16)
     pairs = jnp.dot(take, pairs, preferred_element_type=f32)
     block_ref[:, :half] = (block_ref[:, :half].astype(f32) + pairs).astype(bf16)
+
+
+def attend_kernel(new, lengths_ref, block_ref, keys_ref, values_ref, sent_ref):
+    rows, part, head = keys_ref.shape
+    size, cols = block_ref.shape
+    zs = size // 8
+    toks = rows * new
+    groups = cols // head
+    pair_cols = 2 * head // zs
+    half = cols // 2
+    count = zs * new
+    narrow = lax.axis_index("x") * lax.axis_size("core") + lax.axis_index("core")
+    block = block_ref[...]
+
+    def place(shape, axis, target):
+        at = iota(shape, axis)
+        row = lax.div(at, count)
+        at = at - row * count
+        z = lax.div(at, new)
+        to = z * 8 + (toks if target is None else row * new + at - z * new)
+        return jnp.where(iota(shape, 1 - axis) == to, 1.0, 0.0).astype(bf16)
+
+    def by_group(values):
+        return [
+            jnp.concatenate([values[(r * groups + k) * count : (r * groups + k + 1) * count] for r in range(rows)], axis=0)
+            for k in range(groups)
+        ]
+
+    chosen = jnp.dot(place((rows * count, size), 0, 0), block, preferred_element_type=f32).astype(bf16)
+    queries = [
+        jnp.concatenate([chosen[r * count : (r + 1) * count, k * head : (k + 1) * head] for k in range(groups)], axis=0)
+        for r in range(rows)
+    ]
+    scores = jnp.concatenate([across(queries[r], keys_ref[r]) for r in range(rows)], axis=0)
+
+    shape = (8 * zs, size)
+    note = lax.rem(iota(shape, 0), zs) * 8 + toks
+    pairs = jnp.dot(
+        jnp.where(iota(shape, 1) == note, 1.0, 0.0).astype(bf16), block[:, :half], preferred_element_type=f32
+    )
+    shape = (8 * zs, half)
+    start = lax.div(iota(shape, 0), zs) * pair_cols
+    at = iota(shape, 1)
+    pairs = jnp.where((at >= start) & (at < start + pair_cols), pairs, 0.0).astype(bf16)
+    shape = (half, 2 * head)
+    spread = jnp.where(lax.rem(iota(shape, 0), pair_cols) == lax.rem(iota(shape, 1), pair_cols), 1.0, 0.0)
+    pairs = jnp.dot(pairs, spread.astype(bf16), preferred_element_type=f32)
+    shape = (8 * zs, 2 * head)
+    start = lax.rem(iota(shape, 0), zs) * pair_cols
+    at = iota(shape, 1)
+    pairs = jnp.where((at >= start) & (at < start + pair_cols), pairs, 0.0).astype(bf16)
+    shape = (128, 8 * zs)
+    start = iota(shape, 0) * zs
+    at = iota(shape, 1)
+    fresh = jnp.where((at >= start) & (at < start + zs) & (at < toks * zs), 1.0, 0.0).astype(bf16)
+    fresh = jnp.dot(fresh, pairs, preferred_element_type=f32).astype(bf16)
+
+    own = across(jnp.concatenate(queries, axis=0), fresh[:, :head])
+    scores = jnp.concatenate([scores, own], axis=1) * head**-0.5
+    shape = scores.shape
+    at = iota(shape, 1)
+    row = lax.div(iota(shape, 0), groups * count)
+    token = row * new + lax.rem(iota(shape, 0), new)
+    length = jnp.zeros(shape, jnp.int32)
+    for r in range(rows):
+        length = jnp.where(row == r, lengths_ref[r], length)
+    cached = (at < part) & (at + narrow * part < length)
+    usable = cached | ((at >= part + row * new) & (at <= part + token) & (narrow == 0))
+    scores = jnp.where(usable, scores, masked_score)
+    top = scores.max(1, keepdims=True)
+    weights = jnp.where(usable, jnp.exp(scores - top), 0.0)
+    total = weights.sum(1, keepdims=True)
+    weights = weights.astype(bf16)
+    size_r = groups * count
+    weighted = jnp.concatenate(
+        [
+            jnp.dot(weights[r * size_r : (r + 1) * size_r, :part], values_ref[r], preferred_element_type=f32)
+            for r in range(rows)
+        ],
+        axis=0,
+    )
+    weighted = weighted + jnp.dot(weights[:, part:], fresh[:, head:], preferred_element_type=f32)
+    weighted = by_group(weighted.astype(bf16))
+
+    shape = (rows * size_r, 128)
+    row = lax.div(iota(shape, 0), groups * count)
+    at = iota(shape, 1) - row * new - lax.rem(iota(shape, 0), new)
+    marks = jnp.zeros(shape, f32)
+    for k, value in enumerate(parts_of(top, 3) + parts_of(total, 3)):
+        marks = jnp.where(at == k * 8, value, marks)
+    marks = by_group(marks.astype(bf16))
+    shape = (size, rows * count)
+    there, note = place(shape, 1, 0), place(shape, 1, None)
+    for k in range(groups):
+        piece = jnp.dot(there, weighted[k], preferred_element_type=f32)
+        mark = jnp.dot(note, marks[k], preferred_element_type=f32)
+        sent_ref[:, k * head : k * head + 128] = (piece[:, :128] + mark).astype(bf16)
+        sent_ref[:, k * head + 128 : (k + 1) * head] = piece[:, 128:].astype(bf16)
 
 
 def last_kernel(toks, per_z, parts_ref, weights_ref, down_ref, mixed_ref):
@@ -359,8 +472,14 @@
     sums = pl.pallas_call(
         hidden_kernel,
         out_shape=jax.ShapeDtypeStruct((ys * mine, 2 * ffn + 128), f32),
-        in_specs=[vmem] * 6,
-        out_specs=vmem,
+        in_specs=[anywhere] + [vmem] * 5,
+        out_specs=anywhere,
+        scratch_shapes=[
+            pltpu.VMEM((ys * mine, width), bf16),
+            pltpu.VMEM((ys * mine, 2 * ffn + 128), f32),
+            pltpu.SemaphoreType.DMA((2,)),
+            pltpu.SemaphoreType.DMA((2,)),
+        ],
         compiler_params=pltpu.CompilerParams(vmem_limit_bytes=16 * 2**20),
         cost_estimate=pl.CostEstimate(flops=2**30, bytes_accessed=4 * 2**20, transcendentals=0),
         name="hidden",
@@ -380,49 +499,16 @@
     )(parts)
     block = lax.all_to_all(block.reshape(zs, 8, cols), "z", 0, 0, tiled=True)
 
-    queries = (
-        block[:, :toks]
-        .reshape(zs, rows, new, per_z, head_dim)
-        .transpose(1, 2, 0, 3, 4)
-        .reshape(rows, new * heads, head_dim)
-    )
-    pairs = (
-        block[:, toks, : toks * pair_cols]
-        .reshape(zs, toks, pair_cols)
-        .transpose(1, 0, 2)
-        .reshape(rows, new, 2 * head_dim)
-    )
-    new_keys, new_values = pairs[..., :head_dim], pairs[..., head_dim:]
-    narrow_index = lax.axis_index(NARROW)
-    cache_part = key_cache.shape[1]
-    factor = head_dim ** (-0.5)
-    positions = narrow_index * cache_part + jnp.arange(cache_part, dtype=jnp.int32)
-    usable = (positions[None, :] < lengths[:, None])[:, None, :]
-    scores = jnp.einsum("rqd,rpd->rqp", queries, key_cache, preferred_element_type=f32) * factor
-    scores = jnp.where(usable, scores, masked_score)
-    own = jnp.einsum("rqd,rud->rqu", queries, new_keys, preferred_element_type=f32) * factor
-    token_of = np.arange(new * heads) // heads
-    causal = (token_of[:, None] >= np.arange(new)[None, :])[None]
-    causal = jnp.logical_and(causal, narrow_index == 0)
-    own = jnp.where(causal, own, masked_score)
-    top = jnp.maximum(scores.max(-1), own.max(-1))
-    weights = jnp.where(usable, jnp.exp(scores - top[..., None]), 0.0)
-    own_weights = jnp.where(causal, jnp.exp(own - top[..., None]), 0.0)
-    total = weights.sum(-1) + own_weights.sum(-1)
-    weighted = jnp.einsum("rqp,rpd->rqd", weights.astype(bf16), value_cache, preferred_element_type=f32)
-    weighted = weighted + jnp.einsum("rqu,rud->rqd", own_weights, new_values.astype(f32))
-
-    sent = (
-        weighted.astype(bf16)
-        .reshape(rows, new, zs, per_z, head_dim)
-        .transpose(2, 0, 1, 3, 4)
-        .reshape(zs, toks, cols)
-    )
-    marks = jnp.stack(three_parts(top) + three_parts(total)).astype(bf16)
-    marks = marks.reshape(6, toks, zs, per_z).transpose(2, 3, 0, 1)
-    marks = jnp.pad(marks, ((0, 0), (0, 0), (0, 0), (0, 8 - toks))).reshape(zs, per_z, 48)
-    marks = jnp.pad(marks, ((0, 0), (0, 0), (0, head_dim - 48))).reshape(zs, 1, cols)
-    block = jnp.concatenate([sent, marks, jnp.zeros((zs, 8 - toks - 1, cols), bf16)], axis=1)
+    block = pl.pallas_call(
+        functools.partial(attend_kernel, new),
+        out_shape=jax.ShapeDtypeStruct((zs * 8, cols), bf16),
+        in_specs=[pl.BlockSpec(memory_space=pltpu.SMEM), vmem, vmem, vmem],
+        out_specs=vmem,
+        compiler_params=pltpu.CompilerParams(vmem_limit_bytes=12 * 2**20),
+        cost_estimate=pl.CostEstimate(flops=2**28, bytes_accessed=2**20, transcendentals=2**16),
+        name="attend",
+    )(lengths, block.reshape(zs * 8, cols), key_cache, value_cache)
+    block = block.reshape(zs, 8, cols)
     block = lax.all_to_all(block, "z", 0, 0, tiled=True)
     parts = jnp.concatenate([block[:, :toks].reshape(mine, cols), block[:, toks]], axis=0)
     parts = lax.all_gather(parts, NARROW, axis=0, tiled=False)

time: 180 us -> 178 us (0.989)
  Pallas kernels: 10.1 us -> 12.4 us
  local copies, waits for them, and re-layouts: 6.92 us -> 5.03 us
    pallas_call x0 -> x1, Pallas kernels: none -> 2.5 us  [local(): pl.pallas_call(functools.partial(attend_kernel, new), out_shape=jax.Shape...]
  transfers between devices with their start and end apart: 8 -> 8, of which waited for: 3 -> 3; matrix products, arithmetic and copies ran while one was open for 4% -> 2% of each run, Pallas kernels for 3% -> 4%
where the time goes in v6:
time: 178 us; the launch traced here: 177 us
  blocking collectives  81.3 us (46%)
  starting transfers between devices  37.7 us (21%)
  waiting for transfers between devices  25.4 us (14%)
  between operations  13.3 us (7%)
  Pallas kernels  12.4 us (7%)
  local copies, waits for them, and re-layouts  5.03 us (3%)
    all_to_all x1, blocking collectives, local(): mixed = lax.all_to_all(mixed, 'z', 0, 0, tiled=True)  28.3 us
    all_gather x2, blocking collectives, local(): parts = lax.all_gather(parts, NARROW, axis=0, tiled=False)  27.7 us
    all_to_all x1, starting transfers between devices, local(): column = lax.all_to_all(copies, 'z', 0, 0, tiled=True)  15.2 us
    all_to_all x1, waiting for transfers between devices, local(): block = lax.all_to_all(block.reshape(zs, 8, cols), 'z', 0, 0, tiled=True)  13.6 us
    all_gather x1, blocking collectives, local(): hidden = lax.all_gather(hidden, NARROW, axis=0, tiled=True)  13 us
    all_gather x1, blocking collectives, local(): w_pair = lax.all_gather(pair_lanes, 'y', axis=0, tiled=False)  12.3 us
    all_to_all x1, starting transfers between devices, local(): block = lax.all_to_all(block.reshape(zs, 8, cols), 'z', 0, 0, tiled=True)  8.9 us
    all_to_all x1, waiting for transfers between devices, local(): lax.all_to_all(column, 'y', 0, 0, tiled=True).reshape(ys * mine, width)  6.81 us
  transfers between devices with their start and end apart: 8, of which 3 were waited for; matrix products, arithmetic and copies ran while one was open for 2% of the time, Pallas kernels for 4%

profile of v6, /device:TPU:40, one launch (start us, length us, event | category | flops | bytes accessed | tf_op | source)
XLA Modules:
  0.0 177.2 jit_solution(16230294896342270046)
XLA Ops:
  7.3 0.7 broadcast_in_dim.7
  8.7 15.2 %all-to-all-start = ((bf16[16,48,128]{2,1,0:T(8,128)(2,1)}), bf16[16,48,128]{2,1,0:T(8,128)(2,1)S(1)}, u32[]{:S(2)}, u32[]{:S(2)}) async-start(bf16[16,48,128]{2,1,0:T(8,128)(2,1)} %broadcast_in_dim.8), calls=%async_computation | async-start | bytes 393216 | tf_op jit(solution)/shard_map/all_to_all | solution.py:440
  23.9 12.3 %all_gather.27.pairs_ref = bf16[4,64,128]{2,1,0:T(8,128)(2,1)S(1)} all-gather(bf16[1,64,128]{2,1,0:T(8,128)(2,1)} %bitcast.34), channel_id=1, replica_groups=mesh['z'=16,'y'=4,'x'=4,'core'=2] {'y'}, dimensions={0}, use_global_device_ids=true | all-gather | bytes 81920 | tf_op jit(solution)/shard_map/all_gather | solution.py:435
  36.2 3.5 %all-to-all-done = bf16[16,48,128]{2,1,0:T(8,128)(2,1)S(1)} async-done(((bf16[16,48,128]{2,1,0:T(8,128)(2,1)}), bf16[16,48,128]{2,1,0:T(8,128)(2,1)S(1)}, u32[]{:S(2)}, u32[]{:S(2)}) %all-to-all-start) | async-done | bytes 196640 | tf_op jit(solution)/shard_map/all_to_all | solution.py:440
  39.7 1.1 spread.1.column_ref
  40.9 4.9 %all-to-all-start.3 = ((bf16[4,96,1024]{2,1,0:T(8,128)(2,1)}), bf16[4,96,1024]{2,1,0:T(8,128)(2,1)}, u32[]{:S(2)}, u32[]{:S(2)}) async-start(bf16[4,96,1024]{2,1,0:T(8,128)(2,1)} %spread.1.column_ref), calls=%async_computation.3 | async-start | bytes 1572864 | tf_op jit(solution)/shard_map/all_to_all | solution.py:461
  46.2 1.2 copy-done.4
  47.4 2.0 %first.1.parts_ref = bf16[120,512]{1,0:T(8,128)(2,1)S(1)} custom-call(bf16[4,96,1024]{2,1,0:T(8,128)(2,1)} %spread.1.column_ref, f32[1,1024]{1,0:T(1,128)S(1)} %bitcast.30, f32[8,1024]{1,0:T(8,128)S(1)} %gains.1.notes_ref.products_ref, bf16[4,1024,128]{2,1,0:T(8,128)(2,1)S(1)} %bitcast.26, bf16[4,64,128]{2,1,0:T(8,128)(2,1)S(1)} %all_gather.27.pairs_ref), custom_call_target="tpu_custom_call" | custom-call | flops 100663296 | bytes 2097152 | tf_op jit(solution)/shard_map/first/pallas_call | solution.py:462
  49.4 6.8 %all-to-all-done.3 = bf16[4,96,1024]{2,1,0:T(8,128)(2,1)} async-done(((bf16[4,96,1024]{2,1,0:T(8,128)(2,1)}), bf16[4,96,1024]{2,1,0:T(8,128)(2,1)}, u32[]{:S(2)}, u32[]{:S(2)}) %all-to-all-start.3) | async-done | bytes 786464 | tf_op jit(solution)/shard_map/all_to_all | solution.py:461
  56.2 3.3 %hidden.1 = f32[384,1152]{1,0:T(8,128)} custom-call(bf16[384,1024]{1,0:T(8,128)(2,1)} %bitcast.13.source_ref, f32[1,1024]{1,0:T(1,128)S(1)} %bitcast.31, f32[8,1024]{1,0:T(8,128)S(1)} %gains.1.notes_ref.products_ref, bf16[1024,512]{1,0:T(8,128)(2,1)S(1)} %copy-done.1, bf16[1024,512]{1,0:T(8,128)(2,1)S(1)} %copy-done.2, bf16[120,512]{1,0:T(8,128)(2,1)S(1)} %first.1.parts_ref), custom_call_target="tpu_custom_call" | custom-call | flops 1073741824 | bytes 4194304 | tf_op jit(solution)/shard_map/hidden/pallas_call | solution.py:472
  59.6 14.2 %all-gather.1 = bf16[960,512]{1,0:T(8,128)(2,1)S(1)} all-gather(bf16[120,512]{1,0:T(8,128)(2,1)S(1)} %first.1.parts_ref), channel_id=3, replica_groups=mesh['z'=16,'y'=4,'x'=4,'core'=2] {'x','core'}, dimensions={0}, use_global_device_ids=true | all-gather | bytes 1105920 | tf_op jit(solution)/shard_map/all_gather | solution.py:489
  73.8 1.6 second.1
  75.5 8.9 %all-to-all-start.1 = ((bf16[16,8,512]{2,1,0:T(8,128)(2,1)}), bf16[16,8,512]{2,1,0:T(8,128)(2,1)S(1)}, u32[]{:S(2)}, u32[]{:S(2)}) async-start(bf16[16,8,512]{2,1,0:T(8,128)(2,1)} %bitcast.8), calls=%async_computation.1 | async-start | bytes 262144 | tf_op jit(solution)/shard_map/all_to_all | solution.py:500
  85.1 13.6 %all-to-all-done.1 = bf16[16,8,512]{2,1,0:T(8,128)(2,1)S(1)} async-done(((bf16[16,8,512]{2,1,0:T(8,128)(2,1)}), bf16[16,8,512]{2,1,0:T(8,128)(2,1)S(1)}, u32[]{:S(2)}, u32[]{:S(2)}) %all-to-all-start.1) | async-done | bytes 131104 | tf_op jit(solution)/shard_map/all_to_all | solution.py:500
  98.8 2.5 %attend.1 = bf16[128,512]{1,0:T(8,128)(2,1)} custom-call(s32[3]{0:T(128)S(1)} %copy-done.9, bf16[128,512]{1,0:T(8,128)(2,1)S(1)} %bitcast.28, bf16[3,256,256]{2,1,0:T(8,128)(2,1)S(1)} %copy-done.5, bf16[3,256,256]{2,1,0:T(8,128)(2,1)S(1)} %copy-done.6), custom_call_target="tpu_custom_call" | custom-call | flops 268435456 | bytes 1048576 | tf_op jit(solution)/shard_map/attend/pallas_call | solution.py:502
  101.3 4.7 %all-to-all-start.2 = ((bf16[16,8,512]{2,1,0:T(8,128)(2,1)}), bf16[16,8,512]{2,1,0:T(8,128)(2,1)S(1)}, u32[]{:S(2)}, u32[]{:S(2)}) async-start(bf16[16,8,512]{2,1,0:T(8,128)(2,1)} %bitcast.10), calls=%async_computation.2 | async-start | bytes 262144 | tf_op jit(solution)/shard_map/all_to_all | solution.py:512
  106.0 0.9 copy-done.7
  107.1 13.0 %all_gather.35 = bf16[384,512]{1,0:T(8,128)(2,1)S(1)} all-gather(bf16[48,512]{1,0:T(8,128)(2,1)S(1)} %third.1), channel_id=1, replica_groups=mesh['z'=16,'y'=4,'x'=4,'core'=2] {'x','core'}, dimensions={0}, use_global_device_ids=true | all-gather | bytes 442368 | tf_op jit(solution)/shard_map/all_gather | solution.py:524
  120.1 1.5 convolution_convert_fusion
  121.5 3.9 %all-to-all-start.4 = ((bf16[4,96,1024]{2,1,0:T(8,128)(2,1)}), bf16[4,96,1024]{2,1,0:T(8,128)(2,1)S(1)}, u32[]{:S(2)}, u32[]{:S(2)}) async-start(bf16[4,96,1024]{2,1,0:T(8,128)(2,1)} %bitcast.14), calls=%async_computation.5 | async-start | bytes 1572864 | tf_op jit(solution)/shard_map/all_to_all | solution.py:526
  125.6 13.5 %all-gather.2 = bf16[896,512]{1,0:T(8,128)(2,1)S(1)} all-gather(bf16[112,512]{1,0:T(8,128)(2,1)S(1)} %pad_maximum_fusion), channel_id=4, replica_groups=mesh['z'=16,'y'=4,'x'=4,'core'=2] {'x','core'}, dimensions={0}, use_global_device_ids=true | all-gather | bytes 1032192 | tf_op jit(solution)/shard_map/all_gather | solution.py:514
  139.1 1.2 copy-done.3
  140.3 1.3 last.1
  141.7 28.3 %all_to_all.30 = bf16[16,48,128]{2,1,0:T(8,128)(2,1)S(1)} all-to-all(bf16[16,48,128]{2,1,0:T(8,128)(2,1)S(1)} %reshape.46), channel_id=1, replica_groups=mesh['z'=16,'y'=4,'x'=4,'core'=2] {'z'}, dimensions={0} | all-to-all | bytes 393216 | tf_op jit(solution)/shard_map/all_to_all | solution.py:540
  (41 shorter events, 3.7 us)
Async XLA Ops:
  6.5 113.5 %copy-start = (bf16[512,1024]{1,0:T(8,128)(2,1)S(1)}, bf16[512,1024]{1,0:T(8,128)(2,1)}, u32[]{:S(2)}) copy-start(bf16[512,1024]{1,0:T(8,128)(2,1)} %param.18) | copy-start | bytes 3145732
  6.5 39.2 %copy-start.1 = (bf16[1024,512]{1,0:T(8,128)(2,1)S(1)}, bf16[1024,512]{1,0:T(8,128)(2,1)}, u32[]{:S(2)}) copy-start(bf16[1024,512]{1,0:T(8,128)(2,1)} %gate_ref.3) | copy-start | bytes 3145732
  6.5 39.2 %copy-start.2 = (bf16[1024,512]{1,0:T(8,128)(2,1)S(1)}, bf16[1024,512]{1,0:T(8,128)(2,1)}, u32[]{:S(2)}) copy-start(bf16[1024,512]{1,0:T(8,128)(2,1)} %up_ref.3) | copy-start | bytes 3145732
  6.5 39.2 %copy-start.8 = (f32[1024]{0:T(1024)S(1)}, f32[1024]{0:T(1024)}, u32[]{:S(2)}) copy-start(f32[1024]{0:T(1024)} %param.12) | copy-start | bytes 12292
  6.5 39.7 %all-gather.8.cloned.1.call-start = ((), (), s32[]{:S(2)}) async-start(), calls=%async_computation.9 | async-start | bytes 1310720 | tf_op jit(solution)/shard_map/all_gather | solution.py:434
  8.7 31.0 %all-to-all-start = ((bf16[16,48,128]{2,1,0:T(8,128)(2,1)}), bf16[16,48,128]{2,1,0:T(8,128)(2,1)S(1)}, u32[]{:S(2)}, u32[]{:S(2)}) async-start(bf16[16,48,128]{2,1,0:T(8,128)(2,1)} %broadcast_in_dim.8), calls=%async_computation | async-start | bytes 393216 | tf_op jit(solution)/shard_map/all_to_all | solution.py:440
  40.9 15.4 %all-to-all-start.3 = ((bf16[4,96,1024]{2,1,0:T(8,128)(2,1)}), bf16[4,96,1024]{2,1,0:T(8,128)(2,1)}, u32[]{:S(2)}, u32[]{:S(2)}) async-start(bf16[4,96,1024]{2,1,0:T(8,128)(2,1)} %spread.1.column_ref), calls=%async_computation.3 | async-start | bytes 1572864 | tf_op jit(solution)/shard_map/all_to_all | solution.py:461
  45.8 60.2 %reduce-scatter.2.cloned.1.call-start = ((), (), s32[]{:S(2)}) async-start(), calls=%async_computation.8 | async-start | bytes 1990656 | tf_op jit(solution)/shard_map/reduce_scatter | solution.py:487
  46.2 1.2 copy-start.4
  59.6 39.2 %copy-start.5 = (bf16[3,256,256]{2,1,0:T(8,128)(2,1)S(1)}, bf16[3,256,256]{2,1,0:T(8,128)(2,1)}, u32[]{:S(2)}) copy-start(bf16[3,256,256]{2,1,0:T(8,128)(2,1)} %keys_ref.1) | copy-start | bytes 1179652
  59.6 39.2 %copy-start.6 = (bf16[3,256,256]{2,1,0:T(8,128)(2,1)S(1)}, bf16[3,256,256]{2,1,0:T(8,128)(2,1)}, u32[]{:S(2)}) copy-start(bf16[3,256,256]{2,1,0:T(8,128)(2,1)} %values_ref.1) | copy-start | bytes 1179652
  59.6 39.1 %copy-start.9 = (s32[3]{0:T(128)S(1)}, s32[3]{0:T(128)}, u32[]{:S(2)}) copy-start(s32[3]{0:T(128)} %lengths_ref.1) | copy-start | bytes 40
  75.5 23.3 %all-to-all-start.1 = ((bf16[16,8,512]{2,1,0:T(8,128)(2,1)}), bf16[16,8,512]{2,1,0:T(8,128)(2,1)S(1)}, u32[]{:S(2)}, u32[]{:S(2)}) async-start(bf16[16,8,512]{2,1,0:T(8,128)(2,1)} %bitcast.8), calls=%async_computation.1 | async-start | bytes 262144 | tf_op jit(solution)/shard_map/all_to_all | solution.py:500
  84.4 54.7 %all-gather.6.cloned.1.call-start = ((), (), s32[]{:S(2)}) async-start(), calls=%async_computation.7 | async-start | bytes 1310720 | tf_op jit(solution)/shard_map/all_gather | solution.py:436
  101.3 20.3 %all-to-all-start.2 = ((bf16[16,8,512]{2,1,0:T(8,128)(2,1)}), bf16[16,8,512]{2,1,0:T(8,128)(2,1)S(1)}, u32[]{:S(2)}, u32[]{:S(2)}) async-start(bf16[16,8,512]{2,1,0:T(8,128)(2,1)} %bitcast.10), calls=%async_computation.2 | async-start | bytes 262144 | tf_op jit(solution)/shard_map/all_to_all | solution.py:512
  106.0 0.9 copy-start.7
  121.5 17.6 %all-to-all-start.4 = ((bf16[4,96,1024]{2,1,0:T(8,128)(2,1)}), bf16[4,96,1024]{2,1,0:T(8,128)(2,1)S(1)}, u32[]{:S(2)}, u32[]{:S(2)}) async-start(bf16[4,96,1024]{2,1,0:T(8,128)(2,1)} %bitcast.14), calls=%async_computation.5 | async-start | bytes 1572864 | tf_op jit(solution)/shard_map/all_to_all | solution.py:526
  139.1 1.2 copy-start.3
  140.3 29.7 %copy-start.10 = (bf16[3,2,1024]{2,1,0:T(2,128)(2,1)S(1)}, bf16[3,2,1024]{2,1,0:T(2,128)(2,1)}, u32[]{:S(2)}) copy-start(bf16[3,2,1024]{2,1,0:T(2,128)(2,1)} %param.11) | copy-start | bytes 36868
Sparse Core Ops, SparseCore 0:
  9.5 34.4 all-gather.7
  59.7 37.5 reduce-scatter.1
  99.4 31.1 all-gather.5

commit v7 on v6

--- a/solution.py
+++ b/solution.py
@@ -166,18 +166,18 @@
     return jnp.where(same & (kind < 3) & mask(to), 1.0, 0.0).astype(bf16)
 
 
-def norm(tails, first, count):
+def norm(tails, count, depth):
     every = tails.shape[1] - 128
     shape = (count, every)
-    select = jnp.where(iota(shape, 1) == iota(shape, 0) + first, 1.0, 0.0).astype(bf16)
+    select = jnp.where(iota(shape, 1) == iota(shape, 0), 1.0, 0.0).astype(bf16)
     own = across(select, tails[:, :every]).astype(bf16)
     kind = iota((tails.shape[0], 128), 0) & 7
     total = jnp.dot(own, jnp.where(kind < 3, 1.0, 0.0).astype(bf16), preferred_element_type=f32)
-    centre = total * (1.0 / D)
+    centre = total * (1.0 / depth)
     total = jnp.dot(
         own, jnp.where((kind >= 3) & (kind < 6), 1.0, 0.0).astype(bf16), preferred_element_type=f32
     )
-    spread = total * (1.0 / D) - centre * centre
+    spread = total * (1.0 / depth) - centre * centre
     return own, centre, lax.rsqrt(spread + eps_norm)
 
 
@@ -195,6 +195,68 @@
 def tails_of(parts_ref, first):
     ns = parts_ref.shape[0]
     return jnp.concatenate([parts_ref[n, first:].astype(f32) for n in range(ns)], axis=0).astype(bf16)
+
+
+def combine_kernel(toks, width, parts_ref, copies_ref, mark_ref):
+    mark_ref[...] = jnp.zeros_like(mark_ref)
+    ns, rows, cols = parts_ref.shape
+    half = cols // 2
+    zs = (rows - 8) // (toks + 1)
+    mine = zs * toks
+    every = cols - 128
+    tails = tails_of(parts_ref, mine + zs)
+    total = parts_ref[0, : mine + zs].astype(f32)
+    for n in range(1, ns):
+        total = total + parts_ref[n, : mine + zs].astype(f32)
+    own, centre, _ = norm(tails, mine, ns * width)
+    query = total[:mine] + shift(own, centre, 3, lambda to: (to & 7) >= 6, tails, width)
+    query = query.astype(bf16)
+
+    pair_cols = cols // zs
+    at = iota((128, half), 1)
+    spread = jnp.where((lax.rem(at, pair_cols) == iota((128, half), 0)) & (at < toks * pair_cols), 1.0, 0.0)
+    shifted = shift(own, centre, 3, lambda to: (to & 7) < 2, tails[:, every:], width)
+    pairs = jnp.zeros((mine, half), f32)
+    for part in parts_of(shifted, 2):
+        pairs = pairs + jnp.dot(part.astype(bf16), spread.astype(bf16), preferred_element_type=f32)
+    start = lax.rem(iota((mine, half), 0), toks) * pair_cols
+    at = iota((mine, half), 1)
+    pairs = jnp.where((at >= start) & (at < start + pair_cols), pairs, 0.0)
+    start = iota((zs, mine), 0) * toks
+    at = iota((zs, mine), 1)
+    collect = jnp.where((at >= start) & (at < start + toks), 1.0, 0.0).astype(bf16)
+    rows_of_z = total[mine:, :half]
+    for part in parts_of(pairs, 2):
+        rows_of_z = rows_of_z + jnp.dot(collect, part.astype(bf16), preferred_element_type=f32)
+
+    row, at = iota((zs, zs), 0), iota((zs, zs), 1)
+    join = jnp.where((row < 8) & ((at & 3) == (row & 3)) & (at < 8), 1.0, 0.0).astype(bf16)
+    products = jnp.zeros((zs, half), f32)
+    for n in range(ns):
+        products = products + jnp.dot(join, parts_ref[n, mine : mine + zs, half:], preferred_element_type=f32)
+    high, low = parts_of(products, 2)
+    row = iota((zs, half), 0)
+    beside = jnp.where(row < 4, high, jnp.where(row < 8, low, 0.0))
+    rows_of_z = jnp.concatenate([rows_of_z, beside], axis=1).astype(bf16)
+
+    ends = tails.astype(f32)
+    ends = sum(ends[8 * n : 8 * n + 8] for n in range(ns))
+    row = iota((8, cols), 0)
+    at = iota((8, cols), 1)
+    tail = jnp.zeros((8, cols), f32)
+    for k in (0, 3):
+        value = ends[k : k + 1] + ends[k + 1 : k + 2] + ends[k + 2 : k + 3]
+        for j, part in enumerate(parts_of(value, 3)):
+            tail = jnp.where((row == k + j) & (at < every), part, tail)
+    for j, part in enumerate(parts_of(ends[6:7] + ends[7:8], 2)):
+        tail = jnp.where(row == 6 + j, part, tail)
+    for j, part in enumerate(parts_of(ends[0:1] + ends[1:2], 2)):
+        tail = jnp.where((row == j) & (at >= every), part, tail)
+    tail = tail.astype(bf16)
+    for x in range(copies_ref.shape[0]):
+        copies_ref[x, :mine] = query
+        copies_ref[x, mine : mine + zs] = rows_of_z
+        copies_ref[x, mine + zs :] = tail
 
 
 def third_kernel(toks, sums_ref, parts_ref, hidden_ref):
@@ -228,7 +290,7 @@
     total = parts_ref[0, : mine + zs].astype(f32)
     for n in range(1, ns):
         total = total + parts_ref[n, : mine + zs].astype(f32)
-    own, centre, scale = norm(tails, 0, mine)
+    own, centre, scale = norm(tails, mine, D)
     query = total[:mine] + shift(own, centre, 3, lambda to: (to & 7) >= 6, tails, width)
     query = (query * jnp.concatenate([scale] * (cols // 128), axis=1)).astype(bf16)
     start = iota((mine, zs), 1) * toks
@@ -454,7 +516,7 @@
         out_shape=jax.ShapeDtypeStruct((8, 2 * ffn), f32),
         in_specs=[vmem] * 3,
         out_specs=vmem,
-        compiler_params=pltpu.CompilerParams(vmem_limit_bytes=8 * 2**20),
+        compiler_params=pltpu.CompilerParams(vmem_limit_bytes=5 * 2**20),
         cost_estimate=pl.CostEstimate(flops=2**25, bytes_accessed=2 * 2**20, transcendentals=0),
         name="gains",
     )(gain, w_gate, w_up)
@@ -464,10 +526,24 @@
         out_shape=jax.ShapeDtypeStruct((mine + zs + 8, cols), bf16),
         in_specs=[vmem] * 5,
         out_specs=vmem,
-        compiler_params=pltpu.CompilerParams(vmem_limit_bytes=12 * 2**20),
+        compiler_params=pltpu.CompilerParams(vmem_limit_bytes=6 * 2**20),
         cost_estimate=pl.CostEstimate(flops=2 * mine * width * cols, bytes_accessed=2 * 2**20, transcendentals=0),
         name="first",
     )(column, gain, products, w_first, w_pair)
+
+    parts = lax.all_gather(parts, "core", axis=0, tiled=False)
+    copies, mark = pl.pallas_call(
+        functools.partial(combine_kernel, toks, width),
+        out_shape=(
+            jax.ShapeDtypeStruct((ns // 2,) + parts.shape[1:], bf16),
+            jax.ShapeDtypeStruct((8, 128), f32),
+        ),
+        in_specs=[vmem],
+        out_specs=(vmem, vmem),
+        compiler_params=pltpu.CompilerParams(vmem_limit_bytes=5 * 2**20),
+        cost_estimate=pl.CostEstimate(flops=2**24, bytes_accessed=2**20, transcendentals=0),
+        name="combine",
+    )(parts)
 
     sums = pl.pallas_call(
         hidden_kernel,
@@ -480,20 +556,20 @@
             pltpu.SemaphoreType.DMA((2,)),
             pltpu.SemaphoreType.DMA((2,)),
         ],
-        compiler_params=pltpu.CompilerParams(vmem_limit_bytes=16 * 2**20),
+        compiler_params=pltpu.CompilerParams(vmem_limit_bytes=10 * 2**20),
         cost_estimate=pl.CostEstimate(flops=2**30, bytes_accessed=4 * 2**20, transcendentals=0),
         name="hidden",
-    )(flat, gain, products, w_gate, w_up, parts)
+    )(flat, gain, products, w_gate, w_up, mark)
     sums = lax.psum_scatter(sums, NARROW, scatter_dimension=0, tiled=True)
 
-    parts = lax.all_gather(parts, NARROW, axis=0, tiled=False)
+    parts = lax.all_to_all(copies, "x", 0, 0, tiled=True)
     notes = parts
     block = pl.pallas_call(
-        functools.partial(second_kernel, toks, width),
+        functools.partial(second_kernel, toks, 2 * width),
         out_shape=jax.ShapeDtypeStruct((zs * 8, cols), bf16),
         in_specs=[vmem],
         out_specs=vmem,
-        compiler_params=pltpu.CompilerParams(vmem_limit_bytes=12 * 2**20),
+        compiler_params=pltpu.CompilerParams(vmem_limit_bytes=6 * 2**20),
         cost_estimate=pl.CostEstimate(flops=2**24, bytes_accessed=2 * 2**20, transcendentals=0),
         name="second",
     )(parts)
@@ -517,7 +593,7 @@
         out_shape=jax.ShapeDtypeStruct((sums.shape[0], ffn), bf16),
         in_specs=[vmem, vmem],
         out_specs=vmem,
-        compiler_params=pltpu.CompilerParams(vmem_limit_bytes=8 * 2**20),
+        compiler_params=pltpu.CompilerParams(vmem_limit_bytes=5 * 2**20),
         cost_estimate=pl.CostEstimate(flops=2**24, bytes_accessed=2 * 2**20, transcendentals=0),
         name="third",
     )(sums, notes)

time: 178 us -> 178 us (level)
  waiting for transfers between devices: 25.4 us -> 20.1 us
  starting transfers between devices: 37.7 us -> 40.4 us
    all_gather x2 -> x1, blocking collectives: 27.7 us -> 13.6 us  [local(): parts = lax.all_gather(parts, NARROW, axis=0, tiled=False)]
    all_to_all x0 -> x1, blocking collectives: none -> 12 us  [local(): parts = lax.all_to_all(copies, 'x', 0, 0, tiled=True)]
    all_to_all x1, waiting for transfers between devices: 6.81 us -> 3.13 us  [local(): lax.all_to_all(column, 'y', 0, 0, tiled=True).reshape(ys * mine, width)]
    all_to_all x1, starting transfers between devices: 8.9 us -> 11 us  [local(): block = lax.all_to_all(block.reshape(zs, 8, cols), 'z', 0, 0, tiled=True)]
    all_gather x0 -> x1, blocking collectives: none -> 1.98 us  [local(): parts = lax.all_gather(parts, 'core', axis=0, tiled=False)]
    unnamed x23 -> x27, local copies, waits for them, and re-layouts: 3.42 us -> 5.16 us
  transfers between devices with their start and end apart: 8 -> 8, of which waited for: 3 -> 3; matrix products, arithmetic and copies ran while one was open for 2% -> 2% of each run, Pallas kernels for 4% -> 5%
where the time goes in v7:
time: 178 us; the launch traced here: 177 us
  blocking collectives  81.1 us (46%)
  starting transfers between devices  40.4 us (23%)
  waiting for transfers between devices  20.1 us (11%)
  Pallas kernels  13.3 us (7%)
  between operations  13.3 us (7%)
  local copies, waits for them, and re-layouts  6.75 us (4%)
    all_to_all x1, blocking collectives, local(): mixed = lax.all_to_all(mixed, 'z', 0, 0, tiled=True)  28.3 us
    all_to_all x1, starting transfers between devices, local(): column = lax.all_to_all(copies, 'z', 0, 0, tiled=True)  15.2 us
    all_gather x1, blocking collectives, local(): parts = lax.all_gather(parts, NARROW, axis=0, tiled=False)  13.6 us
    all_gather x1, blocking collectives, local(): hidden = lax.all_gather(hidden, NARROW, axis=0, tiled=True)  13 us
    all_gather x1, blocking collectives, local(): w_pair = lax.all_gather(pair_lanes, 'y', axis=0, tiled=False)  12.3 us
    all_to_all x1, waiting for transfers between devices, local(): block = lax.all_to_all(block.reshape(zs, 8, cols), 'z', 0, 0, tiled=True)  12.1 us
    all_to_all x1, blocking collectives, local(): parts = lax.all_to_all(copies, 'x', 0, 0, tiled=True)  12 us
    all_to_all x1, starting transfers between devices, local(): block = lax.all_to_all(block.reshape(zs, 8, cols), 'z', 0, 0, tiled=True)  11 us
  transfers between devices with their start and end apart: 8, of which 3 were waited for; matrix products, arithmetic and copies ran while one was open for 2% of the time, Pallas kernels for 5%

profile of v7, /device:TPU:40, one launch (start us, length us, event | category | flops | bytes accessed | tf_op | source)
XLA Modules:
  0.0 177.1 jit_solution(6033715314521902864)
XLA Ops:
  8.7 15.2 %all-to-all-start = ((bf16[16,48,128]{2,1,0:T(8,128)(2,1)}), bf16[16,48,128]{2,1,0:T(8,128)(2,1)S(1)}, u32[]{:S(2)}, u32[]{:S(2)}) async-start(bf16[16,48,128]{2,1,0:T(8,128)(2,1)} %broadcast_in_dim.8), calls=%async_computation | async-start | bytes 393216 | tf_op jit(solution)/shard_map/all_to_all | solution.py:502
  23.9 12.3 %all_gather.27.pairs_ref = bf16[4,64,128]{2,1,0:T(8,128)(2,1)S(1)} all-gather(bf16[1,64,128]{2,1,0:T(8,128)(2,1)} %bitcast.33), channel_id=1, replica_groups=mesh['z'=16,'y'=4,'x'=4,'core'=2] {'y'}, dimensions={0}, use_global_device_ids=true | all-gather | bytes 81920 | tf_op jit(solution)/shard_map/all_gather | solution.py:497
  36.2 3.5 %all-to-all-done = bf16[16,48,128]{2,1,0:T(8,128)(2,1)S(1)} async-done(((bf16[16,48,128]{2,1,0:T(8,128)(2,1)}), bf16[16,48,128]{2,1,0:T(8,128)(2,1)S(1)}, u32[]{:S(2)}, u32[]{:S(2)}) %all-to-all-start) | async-done | bytes 196640 | tf_op jit(solution)/shard_map/all_to_all | solution.py:502
  39.7 1.1 spread.1.column_ref
  40.8 4.9 %all-to-all-start.4 = ((bf16[4,96,1024]{2,1,0:T(8,128)(2,1)}), bf16[4,96,1024]{2,1,0:T(8,128)(2,1)}, u32[]{:S(2)}, u32[]{:S(2)}) async-start(bf16[4,96,1024]{2,1,0:T(8,128)(2,1)} %spread.1.column_ref), calls=%async_computation.4 | async-start | bytes 1572864 | tf_op jit(solution)/shard_map/all_to_all | solution.py:523
  46.2 1.2 copy-done.4
  47.4 2.0 %first.1 = bf16[120,512]{1,0:T(8,128)(2,1)S(1)} custom-call(bf16[4,96,1024]{2,1,0:T(8,128)(2,1)} %spread.1.column_ref, f32[1,1024]{1,0:T(1,128)S(1)} %bitcast.29, f32[8,1024]{1,0:T(8,128)S(1)} %gains.1.notes_ref.products_ref, bf16[4,1024,128]{2,1,0:T(8,128)(2,1)S(1)} %bitcast.24, bf16[4,64,128]{2,1,0:T(8,128)(2,1)S(1)} %all_gather.27.pairs_ref), custom_call_target="tpu_custom_call" | custom-call | flops 100663296 | bytes 2097152 | tf_op jit(solution)/shard_map/first/pallas_call | solution.py:524
  49.4 2.0 %all-gather.1 = bf16[240,512]{1,0:T(8,128)(2,1)S(1)} all-gather(bf16[120,512]{1,0:T(8,128)(2,1)S(1)} %first.1), channel_id=3, replica_groups=mesh['z'=16,'y'=4,'x'=4,'core'=2] {'core'}, dimensions={0}, use_global_device_ids=true | all-gather | bytes 368640 | tf_op jit(solution)/shard_map/all_gather | solution.py:534
  53.1 3.1 %all-to-all-done.4 = bf16[4,96,1024]{2,1,0:T(8,128)(2,1)} async-done(((bf16[4,96,1024]{2,1,0:T(8,128)(2,1)}), bf16[4,96,1024]{2,1,0:T(8,128)(2,1)}, u32[]{:S(2)}, u32[]{:S(2)}) %all-to-all-start.4) | async-done | bytes 786464 | tf_op jit(solution)/shard_map/all_to_all | solution.py:523
  56.2 3.3 %hidden.1 = f32[384,1152]{1,0:T(8,128)} custom-call(bf16[384,1024]{1,0:T(8,128)(2,1)} %bitcast.13.source_ref, f32[1,1024]{1,0:T(1,128)S(1)} %bitcast.30, f32[8,1024]{1,0:T(8,128)S(1)} %gains.1.notes_ref.products_ref, bf16[1024,512]{1,0:T(8,128)(2,1)S(1)} %copy-done.1, bf16[1024,512]{1,0:T(8,128)(2,1)S(1)} %copy-done.2, f32[8,128]{1,0:T(8,128)S(1)} %get-tuple-element.8.parts_ref), custom_call_target="tpu_custom_call" | custom-call | flops 1073741824 | bytes 4194304 | tf_op jit(solution)/shard_map/hidden/pallas_call | solution.py:548
  59.6 1.0 copy-done.6
  60.6 12.0 %all_to_all.35.parts_ref = bf16[4,120,512]{2,1,0:T(8,128)(2,1)S(1)} all-to-all(bf16[4,120,512]{2,1,0:T(8,128)(2,1)S(1)} %copy-done.6), channel_id=1, replica_groups=mesh['z'=16,'y'=4,'x'=4,'core'=2] {'x'}, dimensions={0} | all-to-all | bytes 983040 | tf_op jit(solution)/shard_map/all_to_all | solution.py:565
  72.6 1.6 second.1
  74.2 11.0 %all-to-all-start.2 = ((bf16[16,8,512]{2,1,0:T(8,128)(2,1)}), bf16[16,8,512]{2,1,0:T(8,128)(2,1)S(1)}, u32[]{:S(2)}, u32[]{:S(2)}) async-start(bf16[16,8,512]{2,1,0:T(8,128)(2,1)} %bitcast.8), calls=%async_computation.2 | async-start | bytes 262144 | tf_op jit(solution)/shard_map/all_to_all | solution.py:576
  86.0 12.1 %all-to-all-done.2 = bf16[16,8,512]{2,1,0:T(8,128)(2,1)S(1)} async-done(((bf16[16,8,512]{2,1,0:T(8,128)(2,1)}), bf16[16,8,512]{2,1,0:T(8,128)(2,1)S(1)}, u32[]{:S(2)}, u32[]{:S(2)}) %all-to-all-start.2) | async-done | bytes 131104 | tf_op jit(solution)/shard_map/all_to_all | solution.py:576
  98.0 2.5 %attend.1 = bf16[128,512]{1,0:T(8,128)(2,1)} custom-call(s32[3]{0:T(128)S(1)} %copy-done.11, bf16[128,512]{1,0:T(8,128)(2,1)S(1)} %bitcast.27, bf16[3,256,256]{2,1,0:T(8,128)(2,1)S(1)} %copy-done.7, bf16[3,256,256]{2,1,0:T(8,128)(2,1)S(1)} %copy-done.8), custom_call_target="tpu_custom_call" | custom-call | flops 268435456 | bytes 1048576 | tf_op jit(solution)/shard_map/attend/pallas_call | solution.py:578
  100.5 4.7 %all-to-all-start.3 = ((bf16[16,8,512]{2,1,0:T(8,128)(2,1)}), bf16[16,8,512]{2,1,0:T(8,128)(2,1)S(1)}, u32[]{:S(2)}, u32[]{:S(2)}) async-start(bf16[16,8,512]{2,1,0:T(8,128)(2,1)} %bitcast.10), calls=%async_computation.3 | async-start | bytes 262144 | tf_op jit(solution)/shard_map/all_to_all | solution.py:588
  106.3 13.0 %all_gather.35 = bf16[384,512]{1,0:T(8,128)(2,1)S(1)} all-gather(bf16[48,512]{1,0:T(8,128)(2,1)S(1)} %third.1), channel_id=1, replica_groups=mesh['z'=16,'y'=4,'x'=4,'core'=2] {'x','core'}, dimensions={0}, use_global_device_ids=true | all-gather | bytes 442368 | tf_op jit(solution)/shard_map/all_gather | solution.py:600
  119.3 1.5 convolution_convert_fusion
  120.8 4.5 %all-to-all-start.5 = ((bf16[4,96,1024]{2,1,0:T(8,128)(2,1)}), bf16[4,96,1024]{2,1,0:T(8,128)(2,1)S(1)}, u32[]{:S(2)}, u32[]{:S(2)}) async-start(bf16[4,96,1024]{2,1,0:T(8,128)(2,1)} %bitcast.14), calls=%async_computation.6 | async-start | bytes 1572864 | tf_op jit(solution)/shard_map/all_to_all | solution.py:602
  125.4 13.6 %all-gather.2 = bf16[896,512]{1,0:T(8,128)(2,1)S(1)} all-gather(bf16[112,512]{1,0:T(8,128)(2,1)S(1)} %pad_maximum_fusion), channel_id=4, replica_groups=mesh['z'=16,'y'=4,'x'=4,'core'=2] {'x','core'}, dimensions={0}, use_global_device_ids=true | all-gather | bytes 1032192 | tf_op jit(solution)/shard_map/all_gather | solution.py:590
  139.0 1.2 copy-done.3
  140.3 1.3 last.1
  141.6 28.3 %all_to_all.36 = bf16[16,48,128]{2,1,0:T(8,128)(2,1)S(1)} all-to-all(bf16[16,48,128]{2,1,0:T(8,128)(2,1)S(1)} %reshape.46), channel_id=1, replica_groups=mesh['z'=16,'y'=4,'x'=4,'core'=2] {'z'}, dimensions={0} | all-to-all | bytes 393216 | tf_op jit(solution)/shard_map/all_to_all | solution.py:616
  (47 shorter events, 7.0 us)
Async XLA Ops:
  6.5 112.8 %copy-start = (bf16[512,1024]{1,0:T(8,128)(2,1)S(1)}, bf16[512,1024]{1,0:T(8,128)(2,1)}, u32[]{:S(2)}) copy-start(bf16[512,1024]{1,0:T(8,128)(2,1)} %param.18) | copy-start | bytes 3145732
  6.5 39.2 %copy-start.1 = (bf16[1024,512]{1,0:T(8,128)(2,1)S(1)}, bf16[1024,512]{1,0:T(8,128)(2,1)}, u32[]{:S(2)}) copy-start(bf16[1024,512]{1,0:T(8,128)(2,1)} %gate_ref.3) | copy-start | bytes 3145732
  6.5 39.2 %copy-start.2 = (bf16[1024,512]{1,0:T(8,128)(2,1)S(1)}, bf16[1024,512]{1,0:T(8,128)(2,1)}, u32[]{:S(2)}) copy-start(bf16[1024,512]{1,0:T(8,128)(2,1)} %up_ref.3) | copy-start | bytes 3145732
  6.5 39.2 %copy-start.10 = (f32[1024]{0:T(1024)S(1)}, f32[1024]{0:T(1024)}, u32[]{:S(2)}) copy-start(f32[1024]{0:T(1024)} %param.12) | copy-start | bytes 12292
  6.5 39.6 %all-gather.8.cloned.1.call-start = ((), (), s32[]{:S(2)}) async-start(), calls=%async_computation.10 | async-start | bytes 1310720 | tf_op jit(solution)/shard_map/all_gather | solution.py:496
  8.7 31.0 %all-to-all-start = ((bf16[16,48,128]{2,1,0:T(8,128)(2,1)}), bf16[16,48,128]{2,1,0:T(8,128)(2,1)S(1)}, u32[]{:S(2)}, u32[]{:S(2)}) async-start(bf16[16,48,128]{2,1,0:T(8,128)(2,1)} %broadcast_in_dim.8), calls=%async_computation | async-start | bytes 393216 | tf_op jit(solution)/shard_map/all_to_all | solution.py:502
  40.8 15.4 %all-to-all-start.4 = ((bf16[4,96,1024]{2,1,0:T(8,128)(2,1)}), bf16[4,96,1024]{2,1,0:T(8,128)(2,1)}, u32[]{:S(2)}, u32[]{:S(2)}) async-start(bf16[4,96,1024]{2,1,0:T(8,128)(2,1)} %spread.1.column_ref), calls=%async_computation.4 | async-start | bytes 1572864 | tf_op jit(solution)/shard_map/all_to_all | solution.py:523
  45.8 59.4 %reduce-scatter.2.cloned.1.call-start = ((), (), s32[]{:S(2)}) async-start(), calls=%async_computation.9 | async-start | bytes 1990656 | tf_op jit(solution)/shard_map/reduce_scatter | solution.py:563
  46.2 1.2 copy-start.4
  52.3 0.8 copy-start.5
  59.6 1.0 copy-start.6
  59.6 38.4 %copy-start.7 = (bf16[3,256,256]{2,1,0:T(8,128)(2,1)S(1)}, bf16[3,256,256]{2,1,0:T(8,128)(2,1)}, u32[]{:S(2)}) copy-start(bf16[3,256,256]{2,1,0:T(8,128)(2,1)} %keys_ref.1) | copy-start | bytes 1179652
  59.6 38.4 %copy-start.8 = (bf16[3,256,256]{2,1,0:T(8,128)(2,1)S(1)}, bf16[3,256,256]{2,1,0:T(8,128)(2,1)}, u32[]{:S(2)}) copy-start(bf16[3,256,256]{2,1,0:T(8,128)(2,1)} %values_ref.1) | copy-start | bytes 1179652
  59.6 38.4 %copy-start.11 = (s32[3]{0:T(128)S(1)}, s32[3]{0:T(128)}, u32[]{:S(2)}) copy-start(s32[3]{0:T(128)} %lengths_ref.1) | copy-start | bytes 40
  74.2 23.8 %all-to-all-start.2 = ((bf16[16,8,512]{2,1,0:T(8,128)(2,1)}), bf16[16,8,512]{2,1,0:T(8,128)(2,1)S(1)}, u32[]{:S(2)}, u32[]{:S(2)}) async-start(bf16[16,8,512]{2,1,0:T(8,128)(2,1)} %bitcast.8), calls=%async_computation.2 | async-start | bytes 262144 | tf_op jit(solution)/shard_map/all_to_all | solution.py:576
  85.2 53.8 %all-gather.6.cloned.1.call-start = ((), (), s32[]{:S(2)}) async-start(), calls=%async_computation.8 | async-start | bytes 1310720 | tf_op jit(solution)/shard_map/all_gather | solution.py:498
  100.5 20.3 %all-to-all-start.3 = ((bf16[16,8,512]{2,1,0:T(8,128)(2,1)}), bf16[16,8,512]{2,1,0:T(8,128)(2,1)S(1)}, u32[]{:S(2)}, u32[]{:S(2)}) async-start(bf16[16,8,512]{2,1,0:T(8,128)(2,1)} %bitcast.10), calls=%async_computation.3 | async-start | bytes 262144 | tf_op jit(solution)/shard_map/all_to_all | solution.py:588
  105.2 0.9 copy-start.9
  120.8 18.3 %all-to-all-start.5 = ((bf16[4,96,1024]{2,1,0:T(8,128)(2,1)}), bf16[4,96,1024]{2,1,0:T(8,128)(2,1)S(1)}, u32[]{:S(2)}, u32[]{:S(2)}) async-start(bf16[4,96,1024]{2,1,0:T(8,128)(2,1)} %bitcast.14), calls=%async_computation.6 | async-start | bytes 1572864 | tf_op jit(solution)/shard_map/all_to_all | solution.py:602
  139.0 1.2 copy-start.3
  140.2 29.7 %copy-start.12 = (bf16[3,2,1024]{2,1,0:T(2,128)(2,1)S(1)}, bf16[3,2,1024]{2,1,0:T(2,128)(2,1)}, u32[]{:S(2)}) copy-start(bf16[3,2,1024]{2,1,0:T(2,128)(2,1)} %param.11) | copy-start | bytes 36868
Sparse Core Ops, SparseCore 0:
  9.5 34.4 all-gather.7
  59.8 38.6 reduce-scatter.1
  100.6 32.0 all-gather.5

commit v8 on v7

--- a/solution.py
+++ b/solution.py
@@ -506,7 +506,7 @@
         in_specs=[vmem, vmem],
         out_specs=vmem,
         scratch_shapes=[pltpu.VMEM((mine * width // 128, 128), f32)],
-        compiler_params=pltpu.CompilerParams(vmem_limit_bytes=8 * 2**20),
+        compiler_params=pltpu.CompilerParams(vmem_limit_bytes=5 * 2**20),
         cost_estimate=pl.CostEstimate(flops=0, bytes_accessed=2**20, transcendentals=0),
         name="spread",
     )(column.reshape(mine * width // 128, 128), w_pair)
@@ -580,7 +580,7 @@
         out_shape=jax.ShapeDtypeStruct((zs * 8, cols), bf16),
         in_specs=[pl.BlockSpec(memory_space=pltpu.SMEM), vmem, vmem, vmem],
         out_specs=vmem,
-        compiler_params=pltpu.CompilerParams(vmem_limit_bytes=12 * 2**20),
+        compiler_params=pltpu.CompilerParams(vmem_limit_bytes=6 * 2**20),
         cost_estimate=pl.CostEstimate(flops=2**28, bytes_accessed=2**20, transcendentals=2**16),
         name="attend",
     )(lengths, block.reshape(zs * 8, cols), key_cache, value_cache)
@@ -606,7 +606,7 @@
         out_shape=jax.ShapeDtypeStruct((mine, width), bf16),
         in_specs=[vmem, vmem, vmem],
         out_specs=vmem,
-        compiler_params=pltpu.CompilerParams(vmem_limit_bytes=12 * 2**20),
+        compiler_params=pltpu.CompilerParams(vmem_limit_bytes=6 * 2**20),
         cost_estimate=pl.CostEstimate(
             flops=2 * mine * width * cols, bytes_accessed=3 * 2**20, transcendentals=0
         ),

time: 178 us -> 178 us (level)
  no operation moved by 1% of the time
where the time goes in v8:
time: 178 us; the launch traced here: 177 us
  blocking collectives  81.1 us (46%)
  starting transfers between devices  40.4 us (23%)
  waiting for transfers between devices  20.1 us (11%)
  Pallas kernels  13.3 us (7%)
  between operations  13.3 us (7%)
  local copies, waits for them, and re-layouts  6.75 us (4%)
    all_to_all x1, blocking collectives, local(): mixed = lax.all_to_all(mixed, 'z', 0, 0, tiled=True)  28.3 us
    all_to_all x1, starting transfers between devices, local(): column = lax.all_to_all(copies, 'z', 0, 0, tiled=True)  15.2 us
    all_gather x1, blocking collectives, local(): parts = lax.all_gather(parts, NARROW, axis=0, tiled=False)  13.6 us
    all_gather x1, blocking collectives, local(): hidden = lax.all_gather(hidden, NARROW, axis=0, tiled=True)  13 us
    all_gather x1, blocking collectives, local(): w_pair = lax.all_gather(pair_lanes, 'y', axis=0, tiled=False)  12.3 us
    all_to_all x1, waiting for transfers between devices, local(): block = lax.all_to_all(block.reshape(zs, 8, cols), 'z', 0, 0, tiled=True)  12.1 us
    all_to_all x1, blocking collectives, local(): parts = lax.all_to_all(copies, 'x', 0, 0, tiled=True)  12 us
    all_to_all x1, starting transfers between devices, local(): block = lax.all_to_all(block.reshape(zs, 8, cols), 'z', 0, 0, tiled=True)  11 us
  transfers between devices with their start and end apart: 8, of which 3 were waited for; matrix products, arithmetic and copies ran while one was open for 2% of the time, Pallas kernels for 5%

profile of v8, /device:TPU:40, one launch (start us, length us, event | category | flops | bytes accessed | tf_op | source)
XLA Modules:
  0.0 177.1 jit_solution(1880334324413248662)
XLA Ops:
  8.7 15.2 %all-to-all-start = ((bf16[16,48,128]{2,1,0:T(8,128)(2,1)}), bf16[16,48,128]{2,1,0:T(8,128)(2,1)S(1)}, u32[]{:S(2)}, u32[]{:S(2)}) async-start(bf16[16,48,128]{2,1,0:T(8,128)(2,1)} %broadcast_in_dim.8), calls=%async_computation | async-start | bytes 393216 | tf_op jit(solution)/shard_map/all_to_all | solution.py:502
  23.9 12.3 %all_gather.27.pairs_ref = bf16[4,64,128]{2,1,0:T(8,128)(2,1)S(1)} all-gather(bf16[1,64,128]{2,1,0:T(8,128)(2,1)} %bitcast.33), channel_id=1, replica_groups=mesh['z'=16,'y'=4,'x'=4,'core'=2] {'y'}, dimensions={0}, use_global_device_ids=true | all-gather | bytes 81920 | tf_op jit(solution)/shard_map/all_gather | solution.py:497
  36.2 3.5 %all-to-all-done = bf16[16,48,128]{2,1,0:T(8,128)(2,1)S(1)} async-done(((bf16[16,48,128]{2,1,0:T(8,128)(2,1)}), bf16[16,48,128]{2,1,0:T(8,128)(2,1)S(1)}, u32[]{:S(2)}, u32[]{:S(2)}) %all-to-all-start) | async-done | bytes 196640 | tf_op jit(solution)/shard_map/all_to_all | solution.py:502
  39.7 1.1 spread.1.column_ref
  40.8 4.9 %all-to-all-start.4 = ((bf16[4,96,1024]{2,1,0:T(8,128)(2,1)}), bf16[4,96,1024]{2,1,0:T(8,128)(2,1)}, u32[]{:S(2)}, u32[]{:S(2)}) async-start(bf16[4,96,1024]{2,1,0:T(8,128)(2,1)} %spread.1.column_ref), calls=%async_computation.4 | async-start | bytes 1572864 | tf_op jit(solution)/shard_map/all_to_all | solution.py:523
  46.2 1.2 copy-done.4
  47.4 2.0 %first.1 = bf16[120,512]{1,0:T(8,128)(2,1)S(1)} custom-call(bf16[4,96,1024]{2,1,0:T(8,128)(2,1)} %spread.1.column_ref, f32[1,1024]{1,0:T(1,128)S(1)} %bitcast.29, f32[8,1024]{1,0:T(8,128)S(1)} %gains.1.notes_ref.products_ref, bf16[4,1024,128]{2,1,0:T(8,128)(2,1)S(1)} %bitcast.24, bf16[4,64,128]{2,1,0:T(8,128)(2,1)S(1)} %all_gather.27.pairs_ref), custom_call_target="tpu_custom_call" | custom-call | flops 100663296 | bytes 2097152 | tf_op jit(solution)/shard_map/first/pallas_call | solution.py:524
  49.4 2.0 %all-gather.1 = bf16[240,512]{1,0:T(8,128)(2,1)S(1)} all-gather(bf16[120,512]{1,0:T(8,128)(2,1)S(1)} %first.1), channel_id=3, replica_groups=mesh['z'=16,'y'=4,'x'=4,'core'=2] {'core'}, dimensions={0}, use_global_device_ids=true | all-gather | bytes 368640 | tf_op jit(solution)/shard_map/all_gather | solution.py:534
  53.1 3.1 %all-to-all-done.4 = bf16[4,96,1024]{2,1,0:T(8,128)(2,1)} async-done(((bf16[4,96,1024]{2,1,0:T(8,128)(2,1)}), bf16[4,96,1024]{2,1,0:T(8,128)(2,1)}, u32[]{:S(2)}, u32[]{:S(2)}) %all-to-all-start.4) | async-done | bytes 786464 | tf_op jit(solution)/shard_map/all_to_all | solution.py:523
  56.2 3.3 %hidden.1 = f32[384,1152]{1,0:T(8,128)} custom-call(bf16[384,1024]{1,0:T(8,128)(2,1)} %bitcast.13.source_ref, f32[1,1024]{1,0:T(1,128)S(1)} %bitcast.30, f32[8,1024]{1,0:T(8,128)S(1)} %gains.1.notes_ref.products_ref, bf16[1024,512]{1,0:T(8,128)(2,1)S(1)} %copy-done.1, bf16[1024,512]{1,0:T(8,128)(2,1)S(1)} %copy-done.2, f32[8,128]{1,0:T(8,128)S(1)} %get-tuple-element.8.parts_ref), custom_call_target="tpu_custom_call" | custom-call | flops 1073741824 | bytes 4194304 | tf_op jit(solution)/shard_map/hidden/pallas_call | solution.py:548
  59.6 1.0 copy-done.6
  60.6 12.0 %all_to_all.35.parts_ref = bf16[4,120,512]{2,1,0:T(8,128)(2,1)S(1)} all-to-all(bf16[4,120,512]{2,1,0:T(8,128)(2,1)S(1)} %copy-done.6), channel_id=1, replica_groups=mesh['z'=16,'y'=4,'x'=4,'core'=2] {'x'}, dimensions={0} | all-to-all | bytes 983040 | tf_op jit(solution)/shard_map/all_to_all | solution.py:565
  72.6 1.6 second.1
  74.2 11.0 %all-to-all-start.2 = ((bf16[16,8,512]{2,1,0:T(8,128)(2,1)}), bf16[16,8,512]{2,1,0:T(8,128)(2,1)S(1)}, u32[]{:S(2)}, u32[]{:S(2)}) async-start(bf16[16,8,512]{2,1,0:T(8,128)(2,1)} %bitcast.8), calls=%async_computation.2 | async-start | bytes 262144 | tf_op jit(solution)/shard_map/all_to_all | solution.py:576
  86.0 12.1 %all-to-all-done.2 = bf16[16,8,512]{2,1,0:T(8,128)(2,1)S(1)} async-done(((bf16[16,8,512]{2,1,0:T(8,128)(2,1)}), bf16[16,8,512]{2,1,0:T(8,128)(2,1)S(1)}, u32[]{:S(2)}, u32[]{:S(2)}) %all-to-all-start.2) | async-done | bytes 131104 | tf_op jit(solution)/shard_map/all_to_all | solution.py:576
  98.0 2.5 %attend.1 = bf16[128,512]{1,0:T(8,128)(2,1)} custom-call(s32[3]{0:T(128)S(1)} %copy-done.11, bf16[128,512]{1,0:T(8,128)(2,1)S(1)} %bitcast.27, bf16[3,256,256]{2,1,0:T(8,128)(2,1)S(1)} %copy-done.7, bf16[3,256,256]{2,1,0:T(8,128)(2,1)S(1)} %copy-done.8), custom_call_target="tpu_custom_call" | custom-call | flops 268435456 | bytes 1048576 | tf_op jit(solution)/shard_map/attend/pallas_call | solution.py:578
  100.5 4.7 %all-to-all-start.3 = ((bf16[16,8,512]{2,1,0:T(8,128)(2,1)}), bf16[16,8,512]{2,1,0:T(8,128)(2,1)S(1)}, u32[]{:S(2)}, u32[]{:S(2)}) async-start(bf16[16,8,512]{2,1,0:T(8,128)(2,1)} %bitcast.10), calls=%async_computation.3 | async-start | bytes 262144 | tf_op jit(solution)/shard_map/all_to_all | solution.py:588
  106.3 13.0 %all_gather.35 = bf16[384,512]{1,0:T(8,128)(2,1)S(1)} all-gather(bf16[48,512]{1,0:T(8,128)(2,1)S(1)} %third.1), channel_id=1, replica_groups=mesh['z'=16,'y'=4,'x'=4,'core'=2] {'x','core'}, dimensions={0}, use_global_device_ids=true | all-gather | bytes 442368 | tf_op jit(solution)/shard_map/all_gather | solution.py:600
  119.3 1.5 convolution_convert_fusion
  120.8 4.5 %all-to-all-start.5 = ((bf16[4,96,1024]{2,1,0:T(8,128)(2,1)}), bf16[4,96,1024]{2,1,0:T(8,128)(2,1)S(1)}, u32[]{:S(2)}, u32[]{:S(2)}) async-start(bf16[4,96,1024]{2,1,0:T(8,128)(2,1)} %bitcast.14), calls=%async_computation.6 | async-start | bytes 1572864 | tf_op jit(solution)/shard_map/all_to_all | solution.py:602
  125.4 13.6 %all-gather.2 = bf16[896,512]{1,0:T(8,128)(2,1)S(1)} all-gather(bf16[112,512]{1,0:T(8,128)(2,1)S(1)} %pad_maximum_fusion), channel_id=4, replica_groups=mesh['z'=16,'y'=4,'x'=4,'core'=2] {'x','core'}, dimensions={0}, use_global_device_ids=true | all-gather | bytes 1032192 | tf_op jit(solution)/shard_map/all_gather | solution.py:590
  139.0 1.2 copy-done.3
  140.3 1.3 last.1
  141.6 28.3 %all_to_all.36 = bf16[16,48,128]{2,1,0:T(8,128)(2,1)S(1)} all-to-all(bf16[16,48,128]{2,1,0:T(8,128)(2,1)S(1)} %reshape.46), channel_id=1, replica_groups=mesh['z'=16,'y'=4,'x'=4,'core'=2] {'z'}, dimensions={0} | all-to-all | bytes 393216 | tf_op jit(solution)/shard_map/all_to_all | solution.py:616
  (47 shorter events, 7.0 us)
Async XLA Ops:
  6.5 112.8 %copy-start = (bf16[512,1024]{1,0:T(8,128)(2,1)S(1)}, bf16[512,1024]{1,0:T(8,128)(2,1)}, u32[]{:S(2)}) copy-start(bf16[512,1024]{1,0:T(8,128)(2,1)} %param.18) | copy-start | bytes 3145732
  6.5 39.2 %copy-start.1 = (bf16[1024,512]{1,0:T(8,128)(2,1)S(1)}, bf16[1024,512]{1,0:T(8,128)(2,1)}, u32[]{:S(2)}) copy-start(bf16[1024,512]{1,0:T(8,128)(2,1)} %gate_ref.3) | copy-start | bytes 3145732
  6.5 39.2 %copy-start.2 = (bf16[1024,512]{1,0:T(8,128)(2,1)S(1)}, bf16[1024,512]{1,0:T(8,128)(2,1)}, u32[]{:S(2)}) copy-start(bf16[1024,512]{1,0:T(8,128)(2,1)} %up_ref.3) | copy-start | bytes 3145732
  6.5 39.2 %copy-start.10 = (f32[1024]{0:T(1024)S(1)}, f32[1024]{0:T(1024)}, u32[]{:S(2)}) copy-start(f32[1024]{0:T(1024)} %param.12) | copy-start | bytes 12292
  6.5 39.6 %all-gather.8.cloned.1.call-start = ((), (), s32[]{:S(2)}) async-start(), calls=%async_computation.10 | async-start | bytes 1310720 | tf_op jit(solution)/shard_map/all_gather | solution.py:496
  8.7 31.0 %all-to-all-start = ((bf16[16,48,128]{2,1,0:T(8,128)(2,1)}), bf16[16,48,128]{2,1,0:T(8,128)(2,1)S(1)}, u32[]{:S(2)}, u32[]{:S(2)}) async-start(bf16[16,48,128]{2,1,0:T(8,128)(2,1)} %broadcast_in_dim.8), calls=%async_computation | async-start | bytes 393216 | tf_op jit(solution)/shard_map/all_to_all | solution.py:502
  40.8 15.4 %all-to-all-start.4 = ((bf16[4,96,1024]{2,1,0:T(8,128)(2,1)}), bf16[4,96,1024]{2,1,0:T(8,128)(2,1)}, u32[]{:S(2)}, u32[]{:S(2)}) async-start(bf16[4,96,1024]{2,1,0:T(8,128)(2,1)} %spread.1.column_ref), calls=%async_computation.4 | async-start | bytes 1572864 | tf_op jit(solution)/shard_map/all_to_all | solution.py:523
  45.8 59.4 %reduce-scatter.2.cloned.1.call-start = ((), (), s32[]{:S(2)}) async-start(), calls=%async_computation.9 | async-start | bytes 1990656 | tf_op jit(solution)/shard_map/reduce_scatter | solution.py:563
  46.2 1.2 copy-start.4
  52.3 0.8 copy-start.5
  59.6 1.0 copy-start.6
  59.6 38.4 %copy-start.7 = (bf16[3,256,256]{2,1,0:T(8,128)(2,1)S(1)}, bf16[3,256,256]{2,1,0:T(8,128)(2,1)}, u32[]{:S(2)}) copy-start(bf16[3,256,256]{2,1,0:T(8,128)(2,1)} %keys_ref.1) | copy-start | bytes 1179652
  59.6 38.4 %copy-start.8 = (bf16[3,256,256]{2,1,0:T(8,128)(2,1)S(1)}, bf16[3,256,256]{2,1,0:T(8,128)(2,1)}, u32[]{:S(2)}) copy-start(bf16[3,256,256]{2,1,0:T(8,128)(2,1)} %values_ref.1) | copy-start | bytes 1179652
  59.6 38.4 %copy-start.11 = (s32[3]{0:T(128)S(1)}, s32[3]{0:T(128)}, u32[]{:S(2)}) copy-start(s32[3]{0:T(128)} %lengths_ref.1) | copy-start | bytes 40
  74.2 23.8 %all-to-all-start.2 = ((bf16[16,8,512]{2,1,0:T(8,128)(2,1)}), bf16[16,8,512]{2,1,0:T(8,128)(2,1)S(1)}, u32[]{:S(2)}, u32[]{:S(2)}) async-start(bf16[16,8,512]{2,1,0:T(8,128)(2,1)} %bitcast.8), calls=%async_computation.2 | async-start | bytes 262144 | tf_op jit(solution)/shard_map/all_to_all | solution.py:576
  85.2 53.8 %all-gather.6.cloned.1.call-start = ((), (), s32[]{:S(2)}) async-start(), calls=%async_computation.8 | async-start | bytes 1310720 | tf_op jit(solution)/shard_map/all_gather | solution.py:498
  100.5 20.3 %all-to-all-start.3 = ((bf16[16,8,512]{2,1,0:T(8,128)(2,1)}), bf16[16,8,512]{2,1,0:T(8,128)(2,1)S(1)}, u32[]{:S(2)}, u32[]{:S(2)}) async-start(bf16[16,8,512]{2,1,0:T(8,128)(2,1)} %bitcast.10), calls=%async_computation.3 | async-start | bytes 262144 | tf_op jit(solution)/shard_map/all_to_all | solution.py:588
  105.2 0.9 copy-start.9
  120.8 18.3 %all-to-all-start.5 = ((bf16[4,96,1024]{2,1,0:T(8,128)(2,1)}), bf16[4,96,1024]{2,1,0:T(8,128)(2,1)S(1)}, u32[]{:S(2)}, u32[]{:S(2)}) async-start(bf16[4,96,1024]{2,1,0:T(8,128)(2,1)} %bitcast.14), calls=%async_computation.6 | async-start | bytes 1572864 | tf_op jit(solution)/shard_map/all_to_all | solution.py:602
  139.0 1.2 copy-start.3
  140.2 29.7 %copy-start.12 = (bf16[3,2,1024]{2,1,0:T(2,128)(2,1)S(1)}, bf16[3,2,1024]{2,1,0:T(2,128)(2,1)}, u32[]{:S(2)}) copy-start(bf16[3,2,1024]{2,1,0:T(2,128)(2,1)} %param.11) | copy-start | bytes 36868
Sparse Core Ops, SparseCore 0:
  9.5 34.4 all-gather.7
  59.8 38.6 reduce-scatter.1
  100.6 32.0 all-gather.5
